TPU v7x, 256 devices: a whole 4x4x8 slice. The times are simulated.
256 devices in a mesh: tile: 32 (over y, z), vir: 8 (over x, core).
Axes of the slice: x: 4, y: 4, z: 8, core: 2. Of those that a mesh axis runs over, the one named last changes fastest.
Arguments:
- amplitudes: bfloat16 [2048, 128, 512], P('vir', 'tile'), may hold values from -6 to 6
- source_block: bfloat16 [2048, 128, 512], P('vir', 'tile'), may hold values from -4 to 4
- ladder_integrals: bfloat16 [2048, 2048], P('vir'), may hold values from -0.110485435 to 0.110485435, as said below
- cholesky_vectors: bfloat16 [2048, 128, 1024], P('vir', 'tile'), may hold values from -0.0625 to 0.0625
- integral_tiles: int32 [32, 32], replicated, may hold values from 0 to 1, as said below
- amplitude_tiles: int32 [32, 128], replicated, may hold values 0 or 1
Outputs:
- residual: bfloat16 [2048, 128, 512], P('vir', 'tile')
Inputs may be any that keep to these rules, and one draw needn't show every extreme that they name: symmetric: ladder_integrals[a, c] equals ladder_integrals[c, a]. `integral_tiles`: symmetric 0/1 tile list.
All inputs are finite; a program needn't handle non-finite values.
Results may differ from a plain program's by a relative error of at most 0.0046.
Values may be sent and summed in bfloat16 or wider, within the bound.
No kernel may reach another device: no remote copies, remote signals or barrier semaphores. Data moves between devices by JAX's collectives and lax.ppermute only.
A program may use at most 128 MiB of HBM per device.

v0:
```python
import jax
import jax.numpy as jnp
from jax import lax
from jax.sharding import PartitionSpec as P

TILE = 64


def shards(
    amplitudes, source_block, ladder_integrals, cholesky_vectors, integral_tiles, amplitude_tiles
):
    local_rows = amplitudes.shape[0]
    occ_local = amplitudes.shape[1]
    columns = amplitudes.shape[2]
    virt_total = ladder_integrals.shape[1]
    tile_rows = local_rows // TILE
    vir_index = lax.axis_index("vir")
    tile_index = lax.axis_index("tile")
    row_tiles = lax.dynamic_slice(
        integral_tiles, (vir_index * tile_rows, 0), (tile_rows, virt_total // TILE)
    )
    w_mask = jnp.repeat(jnp.repeat(row_tiles, TILE, axis=0), TILE, axis=1).astype(jnp.bfloat16)
    w_eff = ladder_integrals * w_mask
    occ_tiles = lax.dynamic_slice(
        amplitude_tiles, (0, tile_index * occ_local), (virt_total // TILE, occ_local)
    )
    full_mask = jnp.repeat(occ_tiles, TILE, axis=0).astype(jnp.bfloat16)
    own_mask = lax.dynamic_slice_in_dim(full_mask, vir_index * local_rows, local_rows, 0)
    t_eff = amplitudes * own_mask[:, :, None]
    chol_flat = cholesky_vectors.reshape(local_rows * occ_local, -1)
    partial_value = lax.dot_general(
        chol_flat,
        t_eff.reshape(local_rows * occ_local, columns),
        (((0,), (0,)), ((), ())),
        preferred_element_type=jnp.float32,
    )
    flat_amps = t_eff.reshape(local_rows, -1)
    ladder = lax.psum_scatter(
        lax.dot_general(
            w_eff, flat_amps, (((0,), (0,)), ((), ())), preferred_element_type=jnp.float32
        ),
        "vir",
        scatter_dimension=0,
        tiled=True,
    )
    cycle_total = lax.psum(partial_value, ("tile", "vir")).astype(jnp.bfloat16)
    cycle = jnp.dot(chol_flat, cycle_total, preferred_element_type=jnp.float32)
    total = (
        source_block.astype(jnp.float32)
        + ladder.reshape(local_rows, occ_local, columns)
        + cycle.reshape(local_rows, occ_local, columns)
    )
    return total.astype(jnp.bfloat16)


def solution(mesh):
    return jax.shard_map(
        shards,
        mesh=mesh,
        in_specs=(
            P("vir", "tile", None),
            P("vir", "tile", None),
            P("vir", None),
            P("vir", "tile", None),
            P(),
            P(),
        ),
        out_specs=P("vir", "tile", None),
        check_vma=False,
    )
```

profile of v0, /device:TPU:1, one launch (start us, length us, event | category | flops | bytes accessed | tf_op | source)
XLA Modules:
  0.0 143.9 jit_solution(4027380882298740700)
XLA Ops:
  6.5 0.0 reduce-scatter.2.cloned.1.call-start
  6.5 0.8 dynamic-slice_convert_fusion
  7.3 0.1 broadcast_in_dim.12
  7.4 1.8 %broadcast_multiply_fusion = bf16[256,4,512]{2,1,0:T(4,128)(2,1)S(1)} fusion(bf16[256,4,512]{2,1,0:T(4,128)(2,1)} %param.6, bf16[256,4]{1,0:T(8,128)(2,1)S(1)} %constant_dynamic-slice_fusion), kind=kLoop, calls=%fused_computation.8 | loop fusion | flops 524288 | bytes 2099200 | tf_op jit(solution)/shard_map/mul | solution.py:29
  9.2 0.3 copy.13
  9.5 0.7 dynamic-slice_convert_fusion.1
  10.2 0.1 copy.8
  10.3 0.1 broadcast_in_dim.10
  10.4 0.1 convert_element_type.29
  10.5 1.5 %copy.9 = bf16[256,2048]{0,1:T(8,128)(2,1)S(1)} copy(bf16[256,2048]{1,0:T(8,128)(2,1)} %param.8) | data formatting | bytes 2097152 | tf_op args[2]
  12.0 0.1 bitcast_multiply_fusion
  12.1 8.1 %fusion.7 = f32[2048,2048]{1,0:T(8,128)} fusion(bf16[256,2048]{0,1:T(8,128)(2,1)S(1)} %bitcast_multiply_fusion, bf16[256,2048]{1,0:T(8,128)(2,1)S(1)} %bitcast.17), kind=kOutput, calls=%fused_computation.12 | convolution fusion | flops 2147483648 | bytes 18874368 | tf_op jit(solution)/shard_map/dot_general | solution.py:39
  20.2 0.0 copy-start
  20.2 0.0 reduce-scatter.2.cloned.1.call-update
  20.2 1.6 %copy-done = bf16[256,4,1024]{2,1,0:T(4,128)(2,1)S(1)} copy-done((bf16[256,4,1024]{2,1,0:T(4,128)(2,1)S(1)}, bf16[256,4,1024]{2,1,0:T(4,128)(2,1)}, u32[]{:S(2)}) %copy-start) | copy-done | bytes 2097176
  21.7 2.0 %reshape.22 = bf16[1024,1024]{1,0:T(8,128)(2,1)} reshape(bf16[256,4,1024]{2,1,0:T(4,128)(2,1)S(1)} %copy-done) | data formatting | bytes 4194304 | tf_op jit(solution)/shard_map/reshape | solution.py:30
  23.8 3.6 %fusion.2 = f32[1024,512]{0,1:T(8,128)S(1)} fusion(bf16[256,4,1024]{2,1,0:T(4,128)(2,1)} %param.9, bf16[256,4,512]{2,1,0:T(4,128)(2,1)S(1)} %broadcast_multiply_fusion), kind=kOutput, calls=%fused_computation.3 | convolution fusion | flops 1073741824 | bytes 5242880 | tf_op jit(solution)/shard_map/dot_general | solution.py:31
  27.4 95.8 %all-reduce.1 = bf16[1024,512]{0,1:T(8,128)(2,1)S(1)} all-reduce(f32[1024,512]{0,1:T(8,128)S(1)} %fusion.2), channel_id=1, replica_groups=mesh['tile'=32,'vir'=8] {'tile','vir'}, use_global_device_ids=true, to_apply=%region_1.0 | all-reduce | flops 524288 | bytes 3145728 | tf_op jit(solution)/shard_map/psum | solution.py:46
  123.3 2.9 %convolution_bitcast_fusion = f32[1024,512]{0,1:T(8,128)S(1)} fusion(bf16[1024,1024]{1,0:T(8,128)(2,1)} %reshape.22, bf16[1024,512]{0,1:T(8,128)(2,1)S(1)} %all-reduce.1), kind=kOutput, calls=%fused_computation.4 | convolution fusion | flops 1073741824 | bytes 5242880 | tf_op jit(solution)/shard_map/dot_general | solution.py:47
  126.1 1.8 %copy.10 = f32[1024,512]{1,0:T(8,128)} copy(f32[1024,512]{0,1:T(8,128)S(1)} %convolution_bitcast_fusion) | data formatting | bytes 4194304 | tf_op jit(solution)/shard_map/dot_general | solution.py:47
  128.0 1.9 %reshape.23 = f32[256,4,512]{2,1,0:T(4,128)S(1)} reshape(f32[1024,512]{1,0:T(8,128)} %copy.10) | data formatting | bytes 4194304 | tf_op jit(solution)/shard_map/reshape | solution.py:51
  129.9 0.0 copy-start.1
  129.9 0.0 reduce-scatter.2.cloned.1.call-done
  130.0 3.8 %reshape.21 = f32[256,4,512]{2,1,0:T(4,128)} reshape(f32[256,2048]{1,0:T(8,128)} %reduce-scatter.2.cloned.1.call-done) | data formatting | bytes 4194304 | tf_op jit(solution)/shard_map/reshape | solution.py:50
  133.7 0.0 copy-done.1
  133.7 3.3 %add_convert_fusion = bf16[256,4,512]{2,1,0:T(4,128)(2,1)} fusion(f32[256,4,512]{2,1,0:T(4,128)S(1)} %reshape.23, f32[256,4,512]{2,1,0:T(4,128)} %reshape.21, bf16[256,4,512]{2,1,0:T(4,128)(2,1)S(1)} %copy-done.1), kind=kLoop, calls=%fused_computation.2 | loop fusion | flops 2097152 | bytes 6291456 | tf_op jit(solution)/shard_map/convert_element_type | solution.py:53
  (1 shorter events, 0.0 us)
Async XLA Ops:
  6.5 123.4 %reduce-scatter.2.cloned.1.call-start = ((), (), s32[]{:S(2)}) async-start(), calls=%async_computation.1 | async-start | bytes 18874368 | tf_op jit(solution)/shard_map/reduce_scatter | solution.py:38
  20.2 1.6 %copy-start = (bf16[256,4,1024]{2,1,0:T(4,128)(2,1)S(1)}, bf16[256,4,1024]{2,1,0:T(4,128)(2,1)}, u32[]{:S(2)}) copy-start(bf16[256,4,1024]{2,1,0:T(4,128)(2,1)} %param.9) | copy-start | bytes 6291460
  129.9 3.8 %copy-start.1 = (bf16[256,4,512]{2,1,0:T(4,128)(2,1)S(1)}, bf16[256,4,512]{2,1,0:T(4,128)(2,1)}, u32[]{:S(2)}) copy-start(bf16[256,4,512]{2,1,0:T(4,128)(2,1)} %param.7) | copy-start | bytes 3145732
Sparse Core Ops, SparseCore 0:
  20.3 108.6 reduce-scatter.1
where the time goes:
time: 145 us; the launch traced here: 144 us
  blocking collectives  95.8 us (66%)
  matrix products  14.6 us (10%)
  between operations  13.5 us (9%)
  local copies, waits for them, and re-layouts  13.3 us (9%)
  other arithmetic  6.64 us (5%)
    psum x1, blocking collectives, shards(): cycle_total = lax.psum(partial_value, ('tile', 'vir')).astype(jnp.bfloat16)  95.8 us
    dot_general x1, matrix products, shards(): lax.dot_general(w_eff, flat_amps, (((0,), (0,)), ((), ())), preferred_ele...  8.07 us
    reshape x1, local copies, waits for them, and re-layouts, shards(): ladder.reshape(local_rows, occ_local, columns)  3.77 us
    dot_general x1, matrix products, shards(): lax.dot_general(chol_flat, t_eff.reshape(local_rows * occ_local, columns)...  3.64 us
    unnamed x6, local copies, waits for them, and re-layouts  3.32 us
    convert_element_type x1, other arithmetic, shards(): return total.astype(jnp.bfloat16)  3.28 us
  transfers between devices with their start and end apart: 1, of which 0 were waited for; matrix products, arithmetic and copies ran while one was open for 9% of the time, Pallas kernels for 0%

commit v1 on v0

v1 whole, which is shorter than its diff:
```python
import jax
import jax.numpy as jnp
from jax import lax
from jax.sharding import Mesh, PartitionSpec as P

TILE = 64
SWAP = [(0, 1), (1, 0)]


def shift(n, d):
    return [(i, (i + d) % n) for i in range(n)]


def pair_sum(partial):
    core = lax.axis_index("c")
    rows = partial.shape[0] // 2
    halves = partial.reshape((2, rows) + partial.shape[1:])
    sent = lax.dynamic_index_in_dim(halves, 1 - core, 0, keepdims=False)
    kept = lax.dynamic_index_in_dim(halves, core, 0, keepdims=False)
    got = lax.ppermute(sent.astype(jnp.bfloat16), "c", SWAP)
    return kept + got.astype(jnp.float32)


def pair_gather(half):
    core = lax.axis_index("c")
    got = lax.ppermute(half, "c", SWAP)
    return jnp.concatenate(
        [jnp.where(core == 0, half, got), jnp.where(core == 0, got, half)], 0
    )


def shards(
    amplitudes, source_block, ladder_integrals, cholesky_vectors, integral_tiles, amplitude_tiles
):
    rows, occ, columns = amplitudes.shape
    total = ladder_integrals.shape[1]
    vectors = cholesky_vectors.shape[2]
    tile_rows = rows // TILE
    ny, nz, nx = lax.axis_size("y"), lax.axis_size("z"), lax.axis_size("x")
    core = lax.axis_index("c")
    x = lax.axis_index("x")
    vir = x * 2 + core
    tile = lax.axis_index("y") * nz + lax.axis_index("z")

    occ_tiles = lax.dynamic_slice(
        amplitude_tiles, (vir * tile_rows, tile * occ), (tile_rows, occ)
    )
    own_mask = jnp.repeat(occ_tiles, TILE, axis=0).astype(jnp.bfloat16)
    t_eff = amplitudes * own_mask[:, :, None]

    t_flat = t_eff.reshape(rows, occ * columns)
    from_left = lax.ppermute(t_flat, "x", shift(nx, 1))
    from_right = lax.ppermute(t_flat, "x", shift(nx, -1))

    partial = lax.dot_general(
        cholesky_vectors.reshape(rows * occ, vectors),
        t_eff.reshape(rows * occ, columns),
        (((0,), (0,)), ((), ())),
        preferred_element_type=jnp.float32,
    )

    row_tiles = lax.dynamic_slice(
        integral_tiles, (vir * tile_rows, 0), (tile_rows, total // TILE)
    )
    w_mask = jnp.repeat(jnp.repeat(row_tiles, TILE, axis=0), TILE, axis=1).astype(jnp.bfloat16)
    w_parts = (ladder_integrals * w_mask).reshape(rows, nx, 2, rows)
    w_keep = lax.dynamic_index_in_dim(w_parts, core, 2, keepdims=False)
    w_send = lax.dynamic_index_in_dim(w_parts, 1 - core, 2, keepdims=False)
    w_other = lax.ppermute(w_send, "c", SWAP)

    s = pair_sum(partial)
    group = ny * nz
    chunk = s.shape[0] // group
    s = lax.all_to_all(
        s.astype(jnp.bfloat16).reshape(group, chunk, columns), ("y", "z"), 0, 0, tiled=True
    )
    s = s.astype(jnp.float32).sum(0)
    sent = s.astype(jnp.bfloat16)
    s = s + sum(
        lax.ppermute(sent, "x", shift(nx, d)).astype(jnp.float32) for d in range(1, nx)
    )
    s = s.astype(jnp.bfloat16)
    s = lax.all_to_all(
        jnp.broadcast_to(s[None], (group, chunk, columns)), ("y", "z"), 0, 0, tiled=True
    )
    cycle_total = pair_gather(s.reshape(group * chunk, columns))
    cycle = jnp.dot(
        cholesky_vectors.reshape(rows * occ, vectors),
        cycle_total,
        preferred_element_type=jnp.float32,
    )

    half = rows // 2
    far_a = lax.ppermute(from_left[:half], "x", shift(nx, 1))
    far_b = lax.ppermute(from_right[half:], "x", shift(nx, -1))

    def of(w, place):
        return lax.dynamic_index_in_dim(w, (place + nx) % nx, 1, keepdims=False)

    def product(w):
        terms = [
            (of(w, x), t_flat),
            (of(w, x - 1), from_left),
            (of(w, x + 1), from_right),
            (of(w, x + 2)[:, :half], far_a),
            (of(w, x + 2)[:, half:], far_b),
        ]
        return sum(jnp.dot(a, b, preferred_element_type=jnp.float32) for a, b in terms)

    got = lax.ppermute(product(w_other).astype(jnp.bfloat16), "c", SWAP)
    ladder = product(w_keep) + got.astype(jnp.float32)
    total = (
        source_block.astype(jnp.float32)
        + ladder.reshape(rows, occ, columns)
        + cycle.reshape(rows, occ, columns)
    )
    return total.astype(jnp.bfloat16)


def solution(mesh):
    split = Mesh(mesh.devices.reshape(4, 8, 4, 2), ("y", "z", "x", "c"))
    rows, cols = ("x", "c"), ("y", "z")
    return jax.shard_map(
        shards,
        mesh=split,
        in_specs=(
            P(rows, cols, None),
            P(rows, cols, None),
            P(rows, None),
            P(rows, cols, None),
            P(),
            P(),
        ),
        out_specs=P(rows, cols, None),
        check_vma=False,
    )
```

time: 145 us -> 121 us (0.83)
  blocking collectives: 95.8 us -> 0 us
  starting transfers between devices: 0.01 us -> 37.9 us
  local copies, waits for them, and re-layouts: 13.3 us -> 34 us
  matrix products: 14.6 us -> 30.1 us
  between operations: 13.5 us -> 0.3 us
  other arithmetic: 6.64 us -> 13 us
  waiting for transfers between devices: 0.04 us -> 4.23 us
    psum x1 -> x0, blocking collectives: 95.8 us -> none  [shards(): cycle_total = lax.psum(partial_value, ('tile', 'vir')).astype(jnp.bfloat16)]
    all_to_all x0 -> x2, starting transfers between devices: none -> 20.2 us  [the longest x1 10.6 us: shards(): lax.all_to_all(s.astype(jnp.bfloat16).reshape(group, chunk, columns), ('y...]
    ppermute x0 -> x11, starting transfers between devices: none -> 17.7 us  [the longest x1 4.18 us: pair_gather(): got = lax.ppermute(half, 'c', SWAP)]
    dot_general x3 -> x12, matrix products: 14.6 us -> 30.1 us  [the longest x10 24.1 us: product(): jnp.dot(a, b, preferred_element_type=jnp.float32)]
    dynamic_slice x1 -> x5, local copies, waits for them, and re-layouts: 0.02 us -> 5.08 us  [the longest x2 3.17 us: pair_sum(): kept = lax.dynamic_index_in_dim(halves, core, 0, keepdims=False)]
    reshape x3 -> x4, local copies, waits for them, and re-layouts: 7.74 us -> 12.6 us  [the longest x1 3.95 us: shards(): cholesky_vectors.reshape(rows * occ, vectors)]
    unnamed x6 -> x25, local copies, waits for them, and re-layouts: 3.32 us -> 7.61 us
    ppermute x0 -> x11, waiting for transfers between devices: none -> 4.23 us  [the longest x3 4.21 us: shards(): lax.ppermute(sent, 'x', shift(nx, d)).astype(jnp.float32)]
  transfers between devices with their start and end apart: 1 -> 13, of which waited for: 0 -> 1; matrix products, arithmetic and copies ran while one was open for 9% -> 43% of each run, Pallas kernels for 0% -> 0%
where the time goes in v1:
time: 121 us; the launch traced here: 120 us
  starting transfers between devices  37.9 us (31%)
  local copies, waits for them, and re-layouts  34 us (28%)
  matrix products  30.1 us (25%)
  other arithmetic  13 us (11%)
  waiting for transfers between devices  4.23 us (3%)
    dot_general x10, matrix products, product(): jnp.dot(a, b, preferred_element_type=jnp.float32)  24.1 us
    all_to_all x1, starting transfers between devices, shards(): lax.all_to_all(s.astype(jnp.bfloat16).reshape(group, chunk, columns), ('y...  10.6 us
    all_to_all x1, starting transfers between devices, shards(): lax.all_to_all(jnp.broadcast_to(s[None], (group, chunk, columns)), ('y',...  9.56 us
    unnamed x25, local copies, waits for them, and re-layouts  7.61 us
    ppermute x3, waiting for transfers between devices, shards(): lax.ppermute(sent, 'x', shift(nx, d)).astype(jnp.float32)  4.21 us
    ppermute x1, starting transfers between devices, pair_gather(): got = lax.ppermute(half, 'c', SWAP)  4.18 us
    reshape x1, local copies, waits for them, and re-layouts, shards(): cholesky_vectors.reshape(rows * occ, vectors)  3.95 us
    ppermute x3, starting transfers between devices, shards(): lax.ppermute(sent, 'x', shift(nx, d)).astype(jnp.float32)  3.93 us
  transfers between devices with their start and end apart: 13, of which 1 were waited for; matrix products, arithmetic and copies ran while one was open for 43% of the time, Pallas kernels for 0%

profile of v1, /device:TPU:1, one launch (start us, length us, event | category | flops | bytes accessed | tf_op | source)
XLA Modules:
  0.0 119.5 jit_solution(13100514661859394192)
XLA Ops:
  0.0 0.9 dynamic-slice_convert_fusion
  0.9 1.8 %broadcast_multiply_fusion = bf16[256,4,512]{2,1,0:T(4,128)(2,1)S(1)} fusion(bf16[256,4,512]{2,1,0:T(4,128)(2,1)} %param.6, bf16[256,4]{1,0:T(8,128)(2,1)S(1)} %bitcast.77), kind=kLoop, calls=%fused_computation.24 | loop fusion | flops 524288 | bytes 2099200 | tf_op jit(solution)/shard_map/mul | solution.py:49
  2.7 0.0 copy-start.6
  2.7 3.4 %fusion.9 = f32[1024,512]{0,1:T(8,128)} fusion(bf16[256,4,1024]{2,1,0:T(4,128)(2,1)S(1)} %copy-done.7, bf16[256,4,512]{2,1,0:T(4,128)(2,1)S(1)} %broadcast_multiply_fusion), kind=kOutput, calls=%fused_computation.13 | convolution fusion | flops 1073741824 | bytes 5242880 | tf_op jit(solution)/shard_map/dot_general | solution.py:55
  6.1 3.0 %reshape.50 = f32[2,512,512]{1,0,2:T(2,128)S(1)} reshape(f32[1024,512]{0,1:T(8,128)} %fusion.9) | data formatting | bytes 4194304 | tf_op jit(solution)/shard_map/reshape | solution.py:17
  9.2 1.0 constant_dynamic-slice_fusion
  10.1 2.3 %copy.27 = bf16[1,512,512]{2,1,0:T(8,128)(2,1)} copy(bf16[1,512,512]{1,0,2:T(2,128)(2,1)S(1)} %constant_dynamic-slice_fusion) | data formatting | bytes 1048576
  12.4 3.2 %collective-permute-start.6 = (bf16[512,512]{1,0:T(8,128)(2,1)}, bf16[512,512]{1,0:T(8,128)(2,1)}, u32[]{:S(2)}, u32[]{:S(2)}) collective-permute-start(bf16[512,512]{1,0:T(8,128)(2,1)} %bitcast.74), channel_id=1, source_target_pairs={{0,1},{1,0},{2,3},{3,2},{4,5},{5,4},{6,7},{7,6},{8,9},{9,8},{10,11... | collective-permute-start | bytes 1572872 | tf_op jit(solution)/shard_map/ppermute | solution.py:20
  15.6 1.5 %copy.28 = bf16[32,8,4,512]{3,1,2,0:T(8,128)(2,1)S(1)} copy(bf16[32,8,4,512]{3,2,1,0:T(4,128)(2,1)} %bitcast.72) | data formatting | bytes 2097152
  17.1 0.8 collective-permute-start.1
  18.0 0.7 collective-permute-start
  18.7 1.9 %constant_dynamic-slice_fusion.1 = f32[1,512,512]{1,0,2:T(1,128)} fusion(f32[2,512,512]{1,0,2:T(2,128)S(1)} %reshape.50, s32[]{:T(128)S(6)} %select_n.93), kind=kLoop, calls=%fused_computation.53 | loop fusion | bytes 2097156 | tf_op jit(solution)/shard_map/jit(dynamic_index_in_dim)/dynamic_slice | solution.py:19
  20.6 0.8 fusion.46
  21.3 0.1 copy.10
  21.4 0.1 broadcast_in_dim.16
  21.5 0.1 convert_element_type.66
  21.6 2.3 %copy.11 = bf16[256,2048]{0,1:T(8,128)(2,1)} copy(bf16[256,2048]{1,0:T(8,128)(2,1)} %param.8) | data formatting | bytes 2097152 | tf_op args[2]
  23.9 1.3 %copy.19 = f32[1,512,512]{2,1,0:T(8,128)S(1)} copy(f32[1,512,512]{1,0,2:T(1,128)S(1)} %copy-done.5) | data formatting | bytes 2097152 | tf_op jit(solution)/shard_map/jit(dynamic_index_in_dim)/dynamic_slice | solution.py:19
  25.2 1.3 %bitcast_multiply_fusion = bf16[256,2048]{0,1:T(8,128)(2,1)S(1)} fusion(bf16[256,2048]{0,1:T(8,128)(2,1)} %copy.11, bf16[256,32]{0,1:T(8,128)(2,1)S(1)} %convert_element_type.66), kind=kLoop, calls=%fused_computation.20 | loop fusion | flops 524288 | bytes 2113536 | tf_op jit(solution)/shard_map/mul | solution.py:66
  26.5 0.0 copy-start.4
  26.5 0.0 collective-permute-done.6
  26.5 2.4 %fusion.15 = bf16[512,512]{1,0:T(8,128)(2,1)} fusion(f32[1,512,512]{2,1,0:T(8,128)S(1)} %copy.19, bf16[512,512]{1,0:T(8,128)(2,1)} %collective-permute-done.6), kind=kLoop, calls=%fused_computation.19 | loop fusion | flops 786432 | bytes 2097152 | tf_op jit(solution)/shard_map/convert_element_type | solution.py:75
  28.9 10.6 %all-to-all-start = ((bf16[32,16,512]{2,1,0:T(8,128)(2,1)}), bf16[32,16,512]{2,1,0:T(8,128)(2,1)}, u32[]{:S(2)}, u32[]{:S(2)}) async-start(bf16[32,16,512]{2,1,0:T(8,128)(2,1)} %bitcast.73), calls=%async_computation | async-start | bytes 1048576 | tf_op jit(solution)/shard_map/all_to_all | solution.py:74
  39.6 1.0 copy.26
  40.6 0.6 collective-permute-start.4
  41.2 3.9 %reshape.53 = bf16[1024,1024]{1,0:T(8,128)(2,1)} reshape(bf16[256,4,1024]{2,1,0:T(4,128)(2,1)} %param.9) | data formatting | bytes 4194304 | tf_op jit(solution)/shard_map/reshape | solution.py:88
  45.1 1.4 %fusion.19 = f32[256,2048]{1,0:T(8,128)S(1)} fusion(bf16[256,2048]{1,0:T(8,128)(2,1)S(1)} %bitcast.65, bf16[256,4,2,256]{0,3,2,1:T(8,128)(2,1)} %bitcast.68, s32[]{:T(128)S(6)} %select_n.92, s32[]{:T(128)S(6)} %select_n.94), kind=kOutput, calls=%fused_computation.29 | convolution fusion | flops 268435456 | bytes 3276808 | tf_op jit(solution)/shard_map/dot_general | solution.py:108
  46.5 0.0 collective-permute-done.4
  46.5 0.9 dynamic-slice_bitcast_fusion
  47.4 0.0 collective-permute-done.1
  47.4 1.9 %slice.27 = bf16[128,2048]{1,0:T(8,128)(2,1)} slice(bf16[256,2048]{1,0:T(8,128)(2,1)} %collective-permute-done.1), slice={[128:256], [0:2048]} | slice | bytes 1048576 | tf_op jit(solution)/shard_map/slice | solution.py:95
  49.3 3.0 %collective-permute-start.3 = (bf16[128,2048]{1,0:T(8,128)(2,1)}, bf16[128,2048]{1,0:T(8,128)(2,1)}, u32[]{:S(2)}, u32[]{:S(2)}) collective-permute-start(bf16[128,2048]{1,0:T(8,128)(2,1)} %slice.27), channel_id=1, source_target_pairs={{0,6},{2,0},{4,2},{6,4},{1,7},{3,1},{5,3},{7,5},{8,14},{10,8},{12,... | collective-permute-start | bytes 1572872 | tf_op jit(solution)/shard_map/ppermute | solution.py:95
  52.3 0.0 collective-permute-done
  52.3 1.9 %slice.25 = bf16[128,2048]{1,0:T(8,128)(2,1)} slice(bf16[256,2048]{1,0:T(8,128)(2,1)} %collective-permute-done), slice={[0:128], [0:2048]} | slice | bytes 1048576 | tf_op jit(solution)/shard_map/slice | solution.py:94
  54.1 0.0 collective-permute-start.2
  54.1 3.1 %fusion.21 = f32[256,2048]{1,0:T(8,128)} fusion(bf16[256,2048]{1,0:T(8,128)(2,1)} %collective-permute-done.1, bf16[256,4,256]{2,0,1:T(8,128)(2,1)} %collective-permute-done.4, s32[]{:T(128)S(6)} %select_n.100), kind=kOutput, calls=%fused_computation.31 | convolution fusion | flops 268435456 | bytes 3276804 | tf_op jit(solution)/shard_map/dot_general | solution.py:108
  57.3 0.0 all-to-all-done
  57.3 1.1 convert_reduce_fusion
  58.4 0.1 collective-permute-start.7
  58.5 3.8 %collective-permute-start.8 = (bf16[16,512]{1,0:T(8,128)(2,1)S(1)}, bf16[16,512]{1,0:T(8,128)(2,1)S(1)}, u32[]{:S(2)}, u32[]{:S(2)}) collective-permute-start(bf16[16,512]{1,0:T(8,128)(2,1)S(1)} %convert_element_type.77), channel_id=1, source_target_pairs={{0,4},{2,6},{4,0},{6,2},{1,5},{3,7},{5,1},{7,3},{8,12},{10,14},{12... | collective-permute-start | bytes 49160 | tf_op jit(solution)/shard_map/ppermute | solution.py:80
  62.4 0.0 collective-permute-start.9
  62.4 3.0 %fusion.23 = f32[256,2048]{1,0:T(8,128)} fusion(bf16[256,2048]{1,0:T(8,128)(2,1)} %collective-permute-done, bf16[256,4,256]{2,0,1:T(8,128)(2,1)} %collective-permute-done.4, s32[]{:T(128)S(6)} %select_n.97), kind=kOutput, calls=%fused_computation.33 | convolution fusion | flops 268435456 | bytes 3276804 | tf_op jit(solution)/shard_map/dot_general | solution.py:108
  65.4 4.2 %collective-permute-done.7 = bf16[16,512]{1,0:T(8,128)(2,1)S(1)} collective-permute-done((bf16[16,512]{1,0:T(8,128)(2,1)S(1)}, bf16[16,512]{1,0:T(8,128)(2,1)S(1)}, u32[]{:S(2)}, u32[]{:S(2)}) %collective-permute-start.7) | collective-permute-done | bytes 16416 | tf_op jit(solution)/shard_map/ppermute | solution.py:80
  69.6 0.0 collective-permute-done.8
  69.6 0.9 broadcast_in_dim.19
  70.5 9.6 %all-to-all-start.1 = ((bf16[32,16,512]{2,1,0:T(8,128)(2,1)}), bf16[32,16,512]{2,1,0:T(8,128)(2,1)}, u32[]{:S(2)}, u32[]{:S(2)}) async-start(bf16[32,16,512]{2,1,0:T(8,128)(2,1)} %broadcast_in_dim.19), calls=%async_computation.1 | async-start | bytes 1048576 | tf_op jit(solution)/shard_map/all_to_all | solution.py:83
  80.1 1.6 %fusion.32 = f32[256,2048]{1,0:T(8,128)S(1)} fusion(bf16[128,2048]{1,0:T(8,128)(2,1)} %collective-permute-done.3, bf16[256,256]{1,0:T(8,128)(2,1)S(1)} %dynamic-slice_bitcast_fusion), kind=kOutput, calls=%fused_computation.43 | convolution fusion | flops 134217728 | bytes 2686976 | tf_op jit(solution)/shard_map/dot_general | solution.py:108
  81.7 1.5 %fusion.34 = f32[256,2048]{1,0:T(8,128)S(1)} fusion(bf16[128,2048]{1,0:T(8,128)(2,1)} %collective-permute-done.2, bf16[256,256]{1,0:T(8,128)(2,1)S(1)} %dynamic-slice_bitcast_fusion), kind=kOutput, calls=%fused_computation.45 | convolution fusion | flops 134217728 | bytes 2686976 | tf_op jit(solution)/shard_map/dot_general | solution.py:108
  83.2 2.5 %fusion.6 = bf16[256,2048]{1,0:T(8,128)(2,1)} fusion(f32[256,2048]{1,0:T(8,128)S(1)} %fusion.32, f32[256,2048]{1,0:T(8,128)S(1)} %fusion.34, f32[256,2048]{1,0:T(8,128)S(1)} %copy-done, f32[256,2048]{1,0:T(8,128)S(1)} %copy-done.1, bf16[256,2048]{1,0:T(8,128)(2,1)S(1)} %bitcast.66, bf16[256,4,256]{2,0,1:T(8,128)(2,1)} %collective-permute-done.4, ...), kind=kOutput, calls=%fused_computation.9 | convolution fusion | flops 271056896 | bytes 10616836 | tf_op jit(solution)/shard_map/dot_general | solution.py:108
  85.7 1.3 %collective-permute-start.5 = (bf16[256,2048]{1,0:T(8,128)(2,1)}, bf16[256,2048]{1,0:T(8,128)(2,1)S(1)}, u32[]{:S(2)}, u32[]{:S(2)}) collective-permute-start(bf16[256,2048]{1,0:T(8,128)(2,1)} %fusion.6), channel_id=1, source_target_pairs={{0,1},{1,0},{2,3},{3,2},{4,5},{5,4},{6,7},{7,6},{8,9},{9,8},{10,11... | collective-permute-start | bytes 3145736 | tf_op jit(solution)/shard_map/ppermute | solution.py:110
  87.0 0.9 constant_dynamic-slice_fusion.3
  87.9 0.1 copy.25
  88.0 3.2 %convolution_add_fusion.2 = f32[256,2048]{1,0:T(8,128)} fusion(f32[256,2048]{1,0:T(8,128)S(1)} %fusion.19, bf16[256,2048]{1,0:T(8,128)(2,1)} %collective-permute-done, bf16[256,4,2,256]{0,3,2,1:T(8,128)(2,1)} %bitcast.70, s32[]{:T(128)S(6)} %select_n.98, s32[]{:T(128)S(6)} %select_n.94), kind=kOutput, calls=%fused_computation.8 | convolution fusion | flops 268959744 | bytes 5373960 | tf_op jit(solution)/shard_map/dot_general | solution.py:108
  91.2 2.9 %fusion.36 = f32[256,2048]{1,0:T(8,128)} fusion(bf16[128,2048]{1,0:T(8,128)(2,1)} %collective-permute-done.3, bf16[256,256]{1,0:T(8,128)(2,1)S(1)} %bitcast.75), kind=kOutput, calls=%fused_computation.47 | convolution fusion | flops 134217728 | bytes 2686976 | tf_op jit(solution)/shard_map/dot_general | solution.py:108
  94.1 4.2 %collective-permute-start.10 = (bf16[512,512]{1,0:T(8,128)(2,1)}, bf16[512,512]{1,0:T(8,128)(2,1)}, u32[]{:S(2)}, u32[]{:S(2)}) collective-permute-start(bf16[512,512]{1,0:T(8,128)(2,1)} %bitcast.17), channel_id=1, source_target_pairs={{0,1},{1,0},{2,3},{3,2},{4,5},{5,4},{6,7},{7,6},{8,9},{9,8},{10,11... | collective-permute-start | bytes 1572872 | tf_op jit(solution)/shard_map/ppermute | solution.py:26
  98.3 1.5 %fusion.38 = f32[256,2048]{1,0:T(8,128)S(1)} fusion(bf16[128,2048]{1,0:T(8,128)(2,1)} %collective-permute-done.2, bf16[256,256]{1,0:T(8,128)(2,1)S(1)} %bitcast.76), kind=kOutput, calls=%fused_computation.49 | convolution fusion | flops 134217728 | bytes 2686976 | tf_op jit(solution)/shard_map/dot_general | solution.py:108
  99.8 3.5 %fusion.5 = f32[256,2048]{1,0:T(8,128)} fusion(f32[256,2048]{1,0:T(8,128)S(1)} %copy-done.3, f32[256,2048]{1,0:T(8,128)S(1)} %fusion.38, f32[256,2048]{1,0:T(8,128)S(1)} %copy-done.2, bf16[256,2048]{1,0:T(8,128)(2,1)} %collective-permute-done.1, bf16[256,2048]{1,0:T(8,128)(2,1)S(1)} %collective-permute-done.5, bf16[256,4,2,256]{0,3,2,1:T(8,128)(2,1)} %bitcast.71, ...), kind=kOutput, calls=%fused_computation.7 | convolution fusion | flops 271056896 | bytes 10616840 | tf_op jit(solution)/shard_map/dot_general | solution.py:108
  103.2 2.7 %reshape.49 = f32[256,4,512]{2,1,0:T(4,128)S(1)} reshape(f32[256,2048]{1,0:T(8,128)} %fusion.5) | data formatting | bytes 4194304 | tf_op jit(solution)/shard_map/reshape | solution.py:114
  105.9 1.4 %broadcast_select_fusion.1 = (bf16[512,512]{1,0:T(8,128)(2,1)S(1)}, bf16[512,512]{1,0:T(8,128)(2,1)S(1)}) fusion(bf16[512,512]{1,0:T(8,128)(2,1)} %collective-permute-done.10, pred[]{:T(512)S(6)} %eq.15, bf16[32,16,512]{2,1,0:T(8,128)(2,1)} %all-to-all-done.1), kind=kLoop, calls=%fused_computation.26 | loop fusion | flops 524288 | bytes 2097153 | tf_op jit(solution)/shard_map/jit(_where)/select_n | solution.py:28
  107.4 0.5 copy-done.8
  107.8 2.6 %convolution_bitcast_fusion = f32[1024,512]{0,1:T(8,128)} fusion(bf16[1024,1024]{1,0:T(8,128)(2,1)S(1)} %copy-done.8, bf16[512,512]{1,0:T(8,128)(2,1)S(1)} %get-tuple-element.6, bf16[512,512]{1,0:T(8,128)(2,1)S(1)} %get-tuple-element.5), kind=kOutput, calls=%fused_computation.14 | convolution fusion | flops 1075838976 | bytes 5242880 | tf_op jit(solution)/shard_map/dot_general | solution.py:87
  110.4 2.9 %copy.21 = f32[1024,512]{1,0:T(8,128)} copy(f32[1024,512]{0,1:T(8,128)} %convolution_bitcast_fusion) | data formatting | bytes 4194304 | tf_op jit(solution)/shard_map/dot_general | solution.py:87
  113.3 2.9 %reshape.54 = f32[256,4,512]{2,1,0:T(4,128)} reshape(f32[1024,512]{1,0:T(8,128)} %copy.21) | data formatting | bytes 4194304 | tf_op jit(solution)/shard_map/reshape | solution.py:115
  116.2 3.3 %add_convert_fusion = bf16[256,4,512]{2,1,0:T(4,128)(2,1)} fusion(f32[256,4,512]{2,1,0:T(4,128)} %reshape.54, f32[256,4,512]{2,1,0:T(4,128)S(1)} %reshape.49, bf16[256,4,512]{2,1,0:T(4,128)(2,1)S(1)} %copy-done.9), kind=kLoop, calls=%fused_computation.12 | loop fusion | flops 2097152 | bytes 6291456 | tf_op jit(solution)/shard_map/convert_element_type | solution.py:117
  (27 shorter events, 0.1 us)
Async XLA Ops:
  0.0 2.7 %copy-start.7 = (bf16[256,4,1024]{2,1,0:T(4,128)(2,1)S(1)}, bf16[256,4,1024]{2,1,0:T(4,128)(2,1)}, u32[]{:S(2)}) copy-start(bf16[256,4,1024]{2,1,0:T(4,128)(2,1)} %param.9) | copy-start | bytes 6291460
  2.7 3.4 %copy-start.6 = (bf16[256,4,512]{2,1,0:T(4,128)(2,1)}, bf16[256,4,512]{2,1,0:T(4,128)(2,1)S(1)}, u32[]{:S(2)}) copy-start(bf16[256,4,512]{2,1,0:T(4,128)(2,1)S(1)} %broadcast_multiply_fusion) | copy-start | bytes 3145732
  12.4 14.1 %collective-permute-start.6 = (bf16[512,512]{1,0:T(8,128)(2,1)}, bf16[512,512]{1,0:T(8,128)(2,1)}, u32[]{:S(2)}, u32[]{:S(2)}) collective-permute-start(bf16[512,512]{1,0:T(8,128)(2,1)} %bitcast.74), channel_id=1, source_target_pairs={{0,1},{1,0},{2,3},{3,2},{4,5},{5,4},{6,7},{7,6},{8,9},{9,8},{10,11... | collective-permute-start | bytes 1572872 | tf_op jit(solution)/shard_map/ppermute | solution.py:20
  17.1 30.3 %collective-permute-start.1 = (bf16[256,2048]{1,0:T(8,128)(2,1)S(1)}, bf16[256,2048]{1,0:T(8,128)(2,1)}, u32[]{:S(2)}, u32[]{:S(2)}) collective-permute-start(bf16[256,2048]{1,0:T(8,128)(2,1)S(1)} %bitcast.63), channel_id=1, source_target_pairs={{0,6},{2,0},{4,2},{6,4},{1,7},{3,1},{5,3},{7,5},{8,14},{10,8},{12,... | collective-permute-start | bytes 3145736 | tf_op jit(solution)/shard_map/ppermute | solution.py:53
  18.0 34.3 %collective-permute-start = (bf16[256,2048]{1,0:T(8,128)(2,1)S(1)}, bf16[256,2048]{1,0:T(8,128)(2,1)}, u32[]{:S(2)}, u32[]{:S(2)}) collective-permute-start(bf16[256,2048]{1,0:T(8,128)(2,1)S(1)} %bitcast.64), channel_id=1, source_target_pairs={{0,2},{2,4},{4,6},{6,0},{1,3},{3,5},{5,7},{7,1},{8,10},{10,12},{12... | collective-permute-start | bytes 3145736 | tf_op jit(solution)/shard_map/ppermute | solution.py:52
  20.6 3.4 %copy-start.5 = (f32[1,512,512]{1,0,2:T(1,128)S(1)}, f32[1,512,512]{1,0,2:T(1,128)}, u32[]{:S(2)}) copy-start(f32[1,512,512]{1,0,2:T(1,128)} %constant_dynamic-slice_fusion.1) | copy-start | bytes 3145732
  26.5 13.1 %copy-start.4 = (bf16[256,2048]{0,1:T(8,128)(2,1)}, bf16[256,2048]{0,1:T(8,128)(2,1)S(1)}, u32[]{:S(2)}) copy-start(bf16[256,2048]{0,1:T(8,128)(2,1)S(1)} %bitcast_multiply_fusion) | copy-start | bytes 3145732
  28.9 28.3 %all-to-all-start = ((bf16[32,16,512]{2,1,0:T(8,128)(2,1)}), bf16[32,16,512]{2,1,0:T(8,128)(2,1)}, u32[]{:S(2)}, u32[]{:S(2)}) async-start(bf16[32,16,512]{2,1,0:T(8,128)(2,1)} %bitcast.73), calls=%async_computation | async-start | bytes 1048576 | tf_op jit(solution)/shard_map/all_to_all | solution.py:74
  40.6 5.9 %collective-permute-start.4 = (bf16[256,4,256]{2,0,1:T(8,128)(2,1)}, bf16[256,4,256]{2,0,1:T(8,128)(2,1)}, u32[]{:S(2)}, u32[]{:S(2)}) collective-permute-start(bf16[256,4,256]{2,0,1:T(8,128)(2,1)} %bitcast.7), channel_id=1, source_target_pairs={{0,1},{1,0},{2,3},{3,2},{4,5},{5,4},{6,7},{7,6},{8,9},{9,8},{10,11... | collective-permute-start | bytes 1572872 | tf_op jit(solution)/shard_map/ppermute | solution.py:69
  49.3 30.8 %collective-permute-start.3 = (bf16[128,2048]{1,0:T(8,128)(2,1)}, bf16[128,2048]{1,0:T(8,128)(2,1)}, u32[]{:S(2)}, u32[]{:S(2)}) collective-permute-start(bf16[128,2048]{1,0:T(8,128)(2,1)} %slice.27), channel_id=1, source_target_pairs={{0,6},{2,0},{4,2},{6,4},{1,7},{3,1},{5,3},{7,5},{8,14},{10,8},{12,... | collective-permute-start | bytes 1572872 | tf_op jit(solution)/shard_map/ppermute | solution.py:95
  54.1 27.6 %collective-permute-start.2 = (bf16[128,2048]{1,0:T(8,128)(2,1)}, bf16[128,2048]{1,0:T(8,128)(2,1)}, u32[]{:S(2)}, u32[]{:S(2)}) collective-permute-start(bf16[128,2048]{1,0:T(8,128)(2,1)} %slice.25), channel_id=1, source_target_pairs={{0,2},{2,4},{4,6},{6,0},{1,3},{3,5},{5,7},{7,1},{8,10},{10,12},{12... | collective-permute-start | bytes 1572872 | tf_op jit(solution)/shard_map/ppermute | solution.py:94
  58.4 11.2 %collective-permute-start.7 = (bf16[16,512]{1,0:T(8,128)(2,1)S(1)}, bf16[16,512]{1,0:T(8,128)(2,1)S(1)}, u32[]{:S(2)}, u32[]{:S(2)}) collective-permute-start(bf16[16,512]{1,0:T(8,128)(2,1)S(1)} %convert_element_type.77), channel_id=1, source_target_pairs={{0,2},{2,4},{4,6},{6,0},{1,3},{3,5},{5,7},{7,1},{8,10},{10,12},{12... | collective-permute-start | bytes 49160 | tf_op jit(solution)/shard_map/ppermute | solution.py:80
  58.5 11.1 %collective-permute-start.8 = (bf16[16,512]{1,0:T(8,128)(2,1)S(1)}, bf16[16,512]{1,0:T(8,128)(2,1)S(1)}, u32[]{:S(2)}, u32[]{:S(2)}) collective-permute-start(bf16[16,512]{1,0:T(8,128)(2,1)S(1)} %convert_element_type.77), channel_id=1, source_target_pairs={{0,4},{2,6},{4,0},{6,2},{1,5},{3,7},{5,1},{7,3},{8,12},{10,14},{12... | collective-permute-start | bytes 49160 | tf_op jit(solution)/shard_map/ppermute | solution.py:80
  62.4 7.3 %collective-permute-start.9 = (bf16[16,512]{1,0:T(8,128)(2,1)S(1)}, bf16[16,512]{1,0:T(8,128)(2,1)S(1)}, u32[]{:S(2)}, u32[]{:S(2)}) collective-permute-start(bf16[16,512]{1,0:T(8,128)(2,1)S(1)} %convert_element_type.77), channel_id=1, source_target_pairs={{0,6},{2,0},{4,2},{6,4},{1,7},{3,1},{5,3},{7,5},{8,14},{10,8},{12,... | collective-permute-start | bytes 49160 | tf_op jit(solution)/shard_map/ppermute | solution.py:80
  70.5 23.6 %all-to-all-start.1 = ((bf16[32,16,512]{2,1,0:T(8,128)(2,1)}), bf16[32,16,512]{2,1,0:T(8,128)(2,1)}, u32[]{:S(2)}, u32[]{:S(2)}) async-start(bf16[32,16,512]{2,1,0:T(8,128)(2,1)} %broadcast_in_dim.19), calls=%async_computation.1 | async-start | bytes 1048576 | tf_op jit(solution)/shard_map/all_to_all | solution.py:83
  80.0 3.1 %copy-start = (f32[256,2048]{1,0:T(8,128)S(1)}, f32[256,2048]{1,0:T(8,128)}, u32[]{:S(2)}) copy-start(f32[256,2048]{1,0:T(8,128)} %fusion.21) | copy-start | bytes 6291460
  80.1 3.1 %copy-start.1 = (f32[256,2048]{1,0:T(8,128)S(1)}, f32[256,2048]{1,0:T(8,128)}, u32[]{:S(2)}) copy-start(f32[256,2048]{1,0:T(8,128)} %fusion.23) | copy-start | bytes 6291460
  85.7 14.0 %collective-permute-start.5 = (bf16[256,2048]{1,0:T(8,128)(2,1)}, bf16[256,2048]{1,0:T(8,128)(2,1)S(1)}, u32[]{:S(2)}, u32[]{:S(2)}) collective-permute-start(bf16[256,2048]{1,0:T(8,128)(2,1)} %fusion.6), channel_id=1, source_target_pairs={{0,1},{1,0},{2,3},{3,2},{4,5},{5,4},{6,7},{7,6},{8,9},{9,8},{10,11... | collective-permute-start | bytes 3145736 | tf_op jit(solution)/shard_map/ppermute | solution.py:110
  91.2 8.6 %copy-start.2 = (f32[256,2048]{1,0:T(8,128)S(1)}, f32[256,2048]{1,0:T(8,128)}, u32[]{:S(2)}) copy-start(f32[256,2048]{1,0:T(8,128)} %convolution_add_fusion.2) | copy-start | bytes 6291460
  94.1 5.7 %copy-start.3 = (f32[256,2048]{1,0:T(8,128)S(1)}, f32[256,2048]{1,0:T(8,128)}, u32[]{:S(2)}) copy-start(f32[256,2048]{1,0:T(8,128)} %fusion.36) | copy-start | bytes 6291460
  94.1 11.8 %collective-permute-start.10 = (bf16[512,512]{1,0:T(8,128)(2,1)}, bf16[512,512]{1,0:T(8,128)(2,1)}, u32[]{:S(2)}, u32[]{:S(2)}) collective-permute-start(bf16[512,512]{1,0:T(8,128)(2,1)} %bitcast.17), channel_id=1, source_target_pairs={{0,1},{1,0},{2,3},{3,2},{4,5},{5,4},{6,7},{7,6},{8,9},{9,8},{10,11... | collective-permute-start | bytes 1572872 | tf_op jit(solution)/shard_map/ppermute | solution.py:26
  105.9 1.9 %copy-start.8 = (bf16[1024,1024]{1,0:T(8,128)(2,1)S(1)}, bf16[1024,1024]{1,0:T(8,128)(2,1)}, u32[]{:S(2)}) copy-start(bf16[1024,1024]{1,0:T(8,128)(2,1)} %reshape.53) | copy-start | bytes 6291460
  113.3 2.9 %copy-start.9 = (bf16[256,4,512]{2,1,0:T(4,128)(2,1)S(1)}, bf16[256,4,512]{2,1,0:T(4,128)(2,1)}, u32[]{:S(2)}) copy-start(bf16[256,4,512]{2,1,0:T(4,128)(2,1)} %param.7) | copy-start | bytes 3145732

commit v2 on v0

v2 whole, which is shorter than its diff:
```python
import functools

import jax
import jax.numpy as jnp
from jax import lax
from jax.experimental import pallas as pl
from jax.experimental.pallas import tpu as pltpu
from jax.sharding import Mesh, PartitionSpec as P

TILE = 64
SWAP = [(0, 1), (1, 0)]
F32, BF16 = jnp.float32, jnp.bfloat16
VMEM = pl.BlockSpec(memory_space=pltpu.VMEM)
SMEM = pl.BlockSpec(memory_space=pltpu.SMEM)


def shift(n, d):
    return [(i, (i + d) % n) for i in range(n)]


def call(kernel, outs, specs, flops, moved):
    return pl.pallas_call(
        kernel,
        out_shape=outs,
        in_specs=specs,
        out_specs=jax.tree.map(lambda _: VMEM, outs),
        compiler_params=pltpu.CompilerParams(vmem_limit_bytes=40 * 2**20),
        cost_estimate=pl.CostEstimate(flops=flops, bytes_accessed=moved, transcendentals=0),
    )


def column_kernel(mask, half, t, chol, out):
    rows, occ, cols = t.shape
    width = out.shape[0]
    place = lax.broadcasted_iota(jnp.int32, (occ, cols), 0)
    parts = []
    for v in range(rows // TILE):
        keep = jnp.zeros((occ, cols), F32)
        for k in range(occ):
            keep = jnp.where(place == k, mask[v, k].astype(F32), keep)
        parts.append(t[v * TILE:(v + 1) * TILE] * keep.astype(BF16)[None])
    masked = jnp.concatenate(parts, 0).reshape(rows * occ, cols)
    start = pl.multiple_of(half[0] * width, width)
    left = chol[:, :, pl.ds(start, width)].reshape(rows * occ, width)
    out[...] = lax.dot_general(
        left, masked, (((0,), (0,)), ((), ())), preferred_element_type=F32
    ).astype(out.dtype)


def ladder_kernel(n, mask, w_keep, w_send, *refs):
    blocks, (kept, sent) = refs[:n], refs[n:]
    rows, cols = kept.shape[0], blocks[0].shape[2]
    occ = blocks[0].shape[1]
    for k in range(occ):
        parts = []
        for b, block in enumerate(blocks):
            for v in range(block.shape[0] // TILE):
                part = block[v * TILE:(v + 1) * TILE, k, :]
                parts.append(part * mask[b, v, k].astype(F32).astype(BF16))
        right = jnp.concatenate(parts, 0)
        at = slice(k * cols, (k + 1) * cols)
        kept[:, at] = jnp.dot(w_keep[...], right, preferred_element_type=F32).astype(kept.dtype)
        sent[:, at] = jnp.dot(w_send[...], right, preferred_element_type=F32).astype(sent.dtype)


def base_kernel(source, near, far, got_near, got_far, out):
    occ, cols = source.shape[1:]
    for k in range(occ):
        at = slice(k * cols, (k + 1) * cols)
        out[:, k, :] = (
            source[:, k, :].astype(F32)
            + near[:, at]
            + far[:, at]
            + got_near[:, at].astype(F32)
            + got_far[:, at].astype(F32)
        )


def first_kernel(half, chol, ct, out):
    rows, occ, _ = chol.shape
    width = ct.shape[0]
    start = pl.multiple_of(half[0] * width, width)
    left = chol[:, :, pl.ds(start, width)].reshape(rows * occ, width)
    out[...] = jnp.dot(left, ct[...], preferred_element_type=F32)


def last_kernel(half, chol, ct, first, base, out):
    rows, occ, _ = chol.shape
    width = ct.shape[0]
    start = pl.multiple_of(half[0] * width, width)
    left = chol[:, :, pl.ds(start, width)].reshape(rows * occ, width)
    total = first[...] + jnp.dot(left, ct[...], preferred_element_type=F32)
    out[...] = (base[...].reshape(total.shape) + total).astype(BF16).reshape(out.shape)


def shards(
    amplitudes, source_block, ladder_integrals, cholesky_vectors, integral_tiles, amplitude_tiles
):
    rows, occ, columns = amplitudes.shape
    total = ladder_integrals.shape[1]
    vectors = cholesky_vectors.shape[2]
    wide = vectors // 2
    tiles = rows // TILE
    ny, nz, nx = lax.axis_size("y"), lax.axis_size("z"), lax.axis_size("x")
    core, x = lax.axis_index("c"), lax.axis_index("x")
    tile = lax.axis_index("y") * nz + lax.axis_index("z")
    shape = jax.ShapeDtypeStruct

    from_left = lax.ppermute(amplitudes, "x", shift(nx, 1))
    from_right = lax.ppermute(amplitudes, "x", shift(nx, -1))

    masks = lax.dynamic_slice(
        amplitude_tiles.reshape(nx, 2, tiles, -1), (0, core, 0, tile * occ), (nx, 1, tiles, occ)
    )[:, 0]

    def mask_of(place):
        return lax.dynamic_index_in_dim(masks, (place + nx) % nx, 0, keepdims=False)

    mine, other = core[None], 1 - core[None]
    column_flops = 2 * wide * rows * occ * columns
    sent = call(
        column_kernel, shape((wide, columns), BF16), [SMEM, SMEM, VMEM, VMEM], column_flops, 3 << 20
    )(mask_of(x), other, amplitudes, cholesky_vectors)
    got = lax.ppermute(sent, "c", SWAP)
    kept = call(
        column_kernel, shape((wide, columns), F32), [SMEM, SMEM, VMEM, VMEM], column_flops, 3 << 20
    )(mask_of(x), mine, amplitudes, cholesky_vectors)

    group = ny * nx
    chunk = wide // group
    s = (kept + got.astype(F32)).astype(BF16)
    s = lax.all_to_all(s.reshape(group, chunk, columns), ("y", "x"), 0, 0, tiled=True)
    s = s.astype(F32).sum(0).astype(BF16)
    s = lax.all_to_all(
        jnp.broadcast_to(s[None], (nz, chunk, columns)), "z", 0, 0, tiled=True
    )
    s = s.astype(F32).sum(0).astype(BF16)
    s = lax.all_to_all(
        jnp.broadcast_to(s[None], (group, chunk, columns)), ("y", "x"), 0, 0, tiled=True
    )
    ct_mine = s.reshape(wide, columns)
    ct_other = lax.ppermute(ct_mine, "c", SWAP)

    row_tiles = lax.dynamic_slice(
        integral_tiles, ((x * 2 + core) * tiles, 0), (tiles, total // TILE)
    )
    w_mask = jnp.repeat(jnp.repeat(row_tiles, TILE, axis=0), TILE, axis=1).astype(BF16)
    w_parts = (ladder_integrals * w_mask).reshape(rows, nx, 2, rows)
    w_mine = lax.dynamic_index_in_dim(w_parts, core, 2, keepdims=False)
    w_swap = lax.dynamic_index_in_dim(w_parts, 1 - core, 2, keepdims=False)
    w_other = lax.ppermute(w_swap, "c", SWAP)

    def columns_of(w, places):
        return jnp.concatenate(
            [lax.dynamic_index_in_dim(w, (p + nx) % nx, 1, keepdims=False) for p in places], 1
        )

    def products(blocks, places, mask):
        n = len(blocks)
        size = rows * occ * columns
        flops = 4 * size * rows * len(places)
        return call(
            functools.partial(ladder_kernel, n),
            (shape((rows, occ * columns), F32), shape((rows, occ * columns), BF16)),
            [SMEM] + [VMEM] * (2 + n),
            flops,
            len(places) * 4 << 20,
        )(mask, columns_of(w_mine, places), columns_of(w_other, places), *blocks)

    half = rows // 2
    far_a = lax.ppermute(from_left[:half], "x", shift(nx, 1))
    far_b = lax.ppermute(from_right[half:], "x", shift(nx, -1))
    near_places = (x, x - 1, x + 1)
    near, near_sent = products(
        (amplitudes, from_left, from_right),
        near_places,
        jnp.stack([mask_of(p) for p in near_places]),
    )
    got_near = lax.ppermute(near_sent, "c", SWAP)
    far, far_sent = products(
        (far_a, far_b), (x + 2,), mask_of(x + 2).reshape(2, tiles // 2, occ)
    )
    got_far = lax.ppermute(far_sent, "c", SWAP)
    base = call(base_kernel, shape((rows, occ, columns), F32), [VMEM] * 5, 0, 8 << 20)(
        source_block, near, far, got_near, got_far
    )

    first = call(
        first_kernel, shape((rows * occ, columns), F32), [SMEM, VMEM, VMEM], column_flops, 4 << 20
    )(mine, cholesky_vectors, ct_mine)
    return call(
        last_kernel,
        shape((rows, occ, columns), BF16),
        [SMEM, VMEM, VMEM, VMEM, VMEM],
        column_flops,
        6 << 20,
    )(other, cholesky_vectors, ct_other, first, base)


def solution(mesh):
    split = Mesh(mesh.devices.reshape(4, 8, 4, 2), ("y", "z", "x", "c"))
    rows, cols = ("x", "c"), ("y", "z")
    return jax.shard_map(
        shards,
        mesh=split,
        in_specs=(
            P(rows, cols, None),
            P(rows, cols, None),
            P(rows, None),
            P(rows, cols, None),
            P(),
            P(),
        ),
        out_specs=P(rows, cols, None),
        check_vma=False,
    )
```

time: 145 us -> 96.1 us (0.66)
  blocking collectives: 95.8 us -> 15.5 us
  Pallas kernels: 0 us -> 24.7 us
  starting transfers between devices: 0.01 us -> 23.6 us
  matrix products: 14.6 us -> 0 us
  between operations: 13.5 us -> 0.21 us
  waiting for transfers between devices: 0.04 us -> 7.98 us
  local copies, waits for them, and re-layouts: 13.3 us -> 16.7 us
    psum x1 -> x0, blocking collectives: 95.8 us -> none  [shards(): cycle_total = lax.psum(partial_value, ('tile', 'vir')).astype(jnp.bfloat16)]
    pallas_call x0 -> x7, Pallas kernels: none -> 24.7 us  [the longest x2 15.2 us: products(): call(functools.partial(ladder_kernel, n), (shape((rows, occ * columns), F...]
    all_to_all x0 -> x1, blocking collectives: none -> 15.5 us  [shards(): lax.all_to_all(jnp.broadcast_to(s[None], (group, chunk, columns)), ('y',...]
    dot_general x3 -> x0, matrix products: 14.6 us -> none  [the longest x1 8.07 us: shards(): lax.dot_general(w_eff, flat_amps, (((0,), (0,)), ((), ())), preferred_ele...]
    ppermute x0 -> x9, starting transfers between devices: none -> 13.2 us  [the longest x1 3.32 us: shards(): got = lax.ppermute(sent, 'c', SWAP)]
    all_to_all x0 -> x2, starting transfers between devices: none -> 10.4 us  [the longest x1 6.2 us: shards(): lax.all_to_all(jnp.broadcast_to(s[None], (nz, chunk, columns)), 'z', 0, 0...]
    ppermute x0 -> x9, waiting for transfers between devices: none -> 7.97 us  [the longest x1 7.95 us: shards(): from_left = lax.ppermute(amplitudes, 'x', shift(nx, 1))]
    reshape x3 -> x0, local copies, waits for them, and re-layouts: 7.74 us -> none  [the longest x1 3.77 us: shards(): ladder.reshape(local_rows, occ_local, columns)]
  transfers between devices with their start and end apart: 1 -> 11, of which waited for: 0 -> 1; matrix products, arithmetic and copies ran while one was open for 9% -> 19% of each run, Pallas kernels for 0% -> 22%
where the time goes in v2:
time: 96.1 us; the launch traced here: 95.2 us
  Pallas kernels  24.7 us (26%)
  starting transfers between devices  23.6 us (25%)
  local copies, waits for them, and re-layouts  16.7 us (17%)
  blocking collectives  15.5 us (16%)
  waiting for transfers between devices  7.98 us (8%)
  other arithmetic  6.44 us (7%)
    all_to_all x1, blocking collectives, shards(): lax.all_to_all(jnp.broadcast_to(s[None], (group, chunk, columns)), ('y',...  15.5 us
    pallas_call x2, Pallas kernels, products(): call(functools.partial(ladder_kernel, n), (shape((rows, occ * columns), F...  15.2 us
    ppermute x1, waiting for transfers between devices, shards(): from_left = lax.ppermute(amplitudes, 'x', shift(nx, 1))  7.95 us
    unnamed x23, local copies, waits for them, and re-layouts  6.91 us
    all_to_all x1, starting transfers between devices, shards(): lax.all_to_all(jnp.broadcast_to(s[None], (nz, chunk, columns)), 'z', 0, 0...  6.2 us
    all_to_all x1, starting transfers between devices, shards(): lax.all_to_all(s.reshape(group, chunk, columns), ('y', 'x'), 0, 0, tiled=...  4.24 us
    ppermute x1, starting transfers between devices, shards(): got = lax.ppermute(sent, 'c', SWAP)  3.32 us
    pallas_call x1, Pallas kernels, shards(): call(base_kernel, shape((rows, occ, columns), F32), [VMEM] * 5, 0, 8 << 20)  2.95 us
  transfers between devices with their start and end apart: 11, of which 1 were waited for; matrix products, arithmetic and copies ran while one was open for 19% of the time, Pallas kernels for 22%

profile of v2, /device:TPU:1, one launch (start us, length us, event | category | flops | bytes accessed | tf_op | source)
XLA Modules:
  0.0 95.2 jit_solution(13766113403324376776)
XLA Ops:
  0.0 0.8 constant_dynamic-slice_fusion.1
  0.8 0.0 copy-start
  0.8 1.6 %copy-done = bf16[256,4,1024]{2,1,0:T(4,128)(2,1)S(1)} copy-done((bf16[256,4,1024]{2,1,0:T(4,128)(2,1)S(1)}, bf16[256,4,1024]{2,1,0:T(4,128)(2,1)}, u32[]{:S(2)}) %copy-start) | copy-done | bytes 2097176
  2.4 2.0 %shard_map.65 = bf16[512,512]{1,0:T(8,128)(2,1)S(1)} custom-call(s32[4,4]{1,0:T(4,128)S(1)} %get-tuple-element.25.mask, s32[1]{0:T(128)S(6)} %sub.7.half, bf16[256,4,512]{2,1,0:T(4,128)(2,1)} %refs_0_.1, bf16[256,4,1024]{2,1,0:T(4,128)(2,1)S(1)} %copy-done), custom_call_target="tpu_custom_call" | custom-call | flops 536870912 | bytes 3145728 | tf_op jit(solution)/shard_map/pallas_call | solution.py:121
  4.4 3.3 %collective-permute-start = (bf16[512,512]{1,0:T(8,128)(2,1)S(1)}, bf16[512,512]{1,0:T(8,128)(2,1)}, u32[]{:S(2)}, u32[]{:S(2)}) collective-permute-start(bf16[512,512]{1,0:T(8,128)(2,1)S(1)} %shard_map.65), channel_id=1, source_target_pairs={{0,1},{1,0},{2,3},{3,2},{4,5},{5,4},{6,7},{7,6},{8,9},{9,8},{10,11... | collective-permute-start | bytes 1572872 | tf_op jit(solution)/shard_map/ppermute | solution.py:124
  7.7 0.0 collective-permute-start.3
  7.7 2.7 %collective-permute-start.4 = (bf16[256,4,512]{2,1,0:T(4,128)(2,1)}, bf16[256,4,512]{2,1,0:T(4,128)(2,1)}, u32[]{:S(2)}, u32[]{:S(2)}) collective-permute-start(bf16[256,4,512]{2,1,0:T(4,128)(2,1)} %refs_0_.1), channel_id=1, source_target_pairs={{0,6},{2,0},{4,2},{6,4},{1,7},{3,1},{5,3},{7,5},{8,14},{10,8},{12,... | collective-permute-start | bytes 3145736 | tf_op jit(solution)/shard_map/ppermute | solution.py:110
  10.4 0.7 fusion.2
  11.1 0.1 copy.19
  11.2 0.1 broadcast_in_dim.25
  11.3 0.1 convert_element_type.24
  11.4 2.3 %copy.20 = bf16[256,2048]{0,1:T(8,128)(2,1)} copy(bf16[256,2048]{1,0:T(8,128)(2,1)} %param.8) | data formatting | bytes 2097152 | tf_op args[2]
  13.7 0.0 copy-start.1
  13.7 2.4 %bitcast_multiply_fusion = bf16[256,2048]{0,1:T(8,128)(2,1)} fusion(bf16[256,2048]{0,1:T(8,128)(2,1)} %copy.20, bf16[256,32]{0,1:T(8,128)(2,1)S(1)} %convert_element_type.24), kind=kLoop, calls=%fused_computation | loop fusion | flops 524288 | bytes 2113536 | tf_op jit(solution)/shard_map/mul | solution.py:148
  16.1 1.1 %constant_dynamic-slice_fusion.2 = bf16[256,4,1,256]{0,3,2,1:T(8,128)(2,1)S(1)} fusion(bf16[256,4,2,256]{0,3,2,1:T(8,128)(2,1)} %bitcast.35, s32[]{:T(128)S(6)} %select_n.103), kind=kLoop, calls=%fused_computation.11 | loop fusion | bytes 1048580 | tf_op jit(solution)/shard_map/jit(dynamic_index_in_dim)/dynamic_slice | solution.py:150
  17.2 1.0 %copy.24 = bf16[256,4,1,256]{3,0,1,2:T(8,128)(2,1)} copy(bf16[256,4,1,256]{0,3,2,1:T(8,128)(2,1)S(1)} %constant_dynamic-slice_fusion.2) | data formatting | bytes 1048576 | tf_op jit(solution)/shard_map/jit(dynamic_index_in_dim)/dynamic_slice | solution.py:150
  18.2 0.6 collective-permute-start.2
  18.8 0.0 copy-done.1
  18.8 2.0 %shard_map.64 = f32[512,512]{1,0:T(8,128)S(1)} custom-call(s32[4,4]{1,0:T(4,128)S(1)} %get-tuple-element.25.mask, s32[1]{0:T(128)} %bitcast.half, bf16[256,4,512]{2,1,0:T(4,128)(2,1)} %refs_0_.1, bf16[256,4,1024]{2,1,0:T(4,128)(2,1)S(1)} %copy-done.1), custom_call_target="tpu_custom_call" | custom-call | flops 536870912 | bytes 3145728 | tf_op jit(solution)/shard_map/pallas_call | solution.py:125
  20.8 0.0 collective-permute-done
  20.8 0.0 copy-start.7
  20.8 2.1 %add_convert_fusion = bf16[512,512]{1,0:T(8,128)(2,1)} fusion(f32[512,512]{1,0:T(8,128)S(1)} %shard_map.64, bf16[512,512]{1,0:T(8,128)(2,1)} %collective-permute-done), kind=kLoop, calls=%fused_computation.1 | loop fusion | flops 786432 | bytes 2097152 | tf_op jit(solution)/shard_map/convert_element_type | solution.py:131
  22.9 4.2 %all-to-all-start = ((bf16[16,32,512]{2,1,0:T(8,128)(2,1)}), bf16[16,32,512]{2,1,0:T(8,128)(2,1)}, u32[]{:S(2)}, u32[]{:S(2)}) async-start(bf16[16,32,512]{2,1,0:T(8,128)(2,1)} %bitcast.37), calls=%async_computation | async-start | bytes 1048576 | tf_op jit(solution)/shard_map/all_to_all | solution.py:132
  27.2 0.0 copy-done.7
  27.2 0.7 constant_dynamic-slice_fusion
  27.9 0.0 copy-start.8
  27.9 8.0 %collective-permute-done.3.refs_1_ = bf16[256,4,512]{2,1,0:T(4,128)(2,1)} collective-permute-done((bf16[256,4,512]{2,1,0:T(4,128)(2,1)}, bf16[256,4,512]{2,1,0:T(4,128)(2,1)}, u32[]{:S(2)}, u32[]{:S(2)}) %collective-permute-start.3) | collective-permute-done | bytes 1048608 | tf_op jit(solution)/shard_map/ppermute | solution.py:109
  35.8 2.0 %slice.8 = bf16[128,4,512]{2,1,0:T(4,128)(2,1)} slice(bf16[256,4,512]{2,1,0:T(4,128)(2,1)} %collective-permute-done.3.refs_1_), slice={[0:128], [0:4], [0:512]} | slice | bytes 1048576 | tf_op jit(solution)/shard_map/slice | solution.py:171
  37.8 0.0 collective-permute-start.5
  37.8 0.0 collective-permute-done.4.refs_2_
  37.8 2.0 %slice.9 = bf16[128,4,512]{2,1,0:T(4,128)(2,1)} slice(bf16[256,4,512]{2,1,0:T(4,128)(2,1)} %collective-permute-done.4.refs_2_), slice={[128:256], [0:4], [0:512]} | slice | bytes 1048576 | tf_op jit(solution)/shard_map/slice | solution.py:172
  39.9 2.7 %collective-permute-start.6 = (bf16[128,4,512]{2,1,0:T(4,128)(2,1)}, bf16[128,4,512]{2,1,0:T(4,128)(2,1)}, u32[]{:S(2)}, u32[]{:S(2)}) collective-permute-start(bf16[128,4,512]{2,1,0:T(4,128)(2,1)} %slice.9), channel_id=1, source_target_pairs={{0,6},{2,0},{4,2},{6,4},{1,7},{3,1},{5,3},{7,5},{8,14},{10,8},{12,... | collective-permute-start | bytes 1572872 | tf_op jit(solution)/shard_map/ppermute | solution.py:172
  42.5 0.0 copy-done.8
  42.5 0.1 copy.26
  42.6 0.1 copy.27
  42.7 0.1 copy.28
  42.9 0.1 copy.29
  43.0 0.0 all-to-all-done
  43.0 1.1 %reduce_sum.24 = bf16[32,512]{1,0:T(8,128)(2,1)S(1)} reduce(bf16[16,32,512]{2,1,0:T(8,128)(2,1)} %all-to-all-done, bf16[]{:T(256)} %constant.284.clone.1), dimensions={0}, to_apply=%region_0.1 | reduce | flops 245760 | bytes 557058 | tf_op jit(solution)/shard_map/reduce_sum | solution.py:133
  44.1 0.7 broadcast_in_dim.11
  44.9 6.2 %all-to-all-start.1 = ((bf16[8,32,512]{2,1,0:T(8,128)(2,1)}), bf16[8,32,512]{2,1,0:T(8,128)(2,1)S(1)}, u32[]{:S(2)}, u32[]{:S(2)}) async-start(bf16[8,32,512]{2,1,0:T(8,128)(2,1)} %broadcast_in_dim.11), calls=%async_computation.1 | async-start | bytes 524288 | tf_op jit(solution)/shard_map/all_to_all | solution.py:134
  51.1 0.0 collective-permute-done.2
  51.1 1.1 %dynamic-slice_bitcast_fusion = (bf16[256,256]{1,0:T(8,128)(2,1)S(1)}, bf16[256,256]{1,0:T(8,128)(2,1)S(1)}, bf16[256,256]{1,0:T(8,128)(2,1)S(1)}, bf16[256,256]{1,0:T(8,128)(2,1)S(1)}) fusion(bf16[256,4,256]{2,0,1:T(8,128)(2,1)} %collective-permute-done.2, s32[]{:T(128)S(6)} %select_n.105, s32[]{:T(128)S(6)} %select_n.100, s32[]{:T(128)S(6)} %select_n.97, ...), kind=kLoop, calls=%fused_computation.4 | loop fusion | bytes 1048592 | tf_op jit(solution)/shard_map/jit(dynamic_index_in_dim)/squeeze | solution.py:155
  52.3 10.5 %shard_map.67 = (f32[256,2048]{1,0:T(8,128)S(1)}, bf16[256,2048]{1,0:T(8,128)(2,1)}) custom-call(s32[3,4,4]{2,1,0:T(4,128)S(1)} %pad_add_fusion.mask, bf16[256,768]{1,0:T(8,128)(2,1)S(1)} %pad_maximum_fusion.w_keep, bf16[256,768]{1,0:T(8,128)(2,1)S(1)} %pad_maximum_fusion.1.w_send, bf16[256,4,512]{2,1,0:T(4,128)(2,1)} %refs_0_.1, ...), custom_call_target="tpu_custom_call" | custom-call | flops 1610612736 | bytes 12582912 | tf_op jit(solution)/shard_map/pallas_call | solution.py:162
  62.7 1.3 %copy-done.2 = f32[256,2048]{1,0:T(8,128)} copy-done((f32[256,2048]{1,0:T(8,128)}, f32[256,2048]{1,0:T(8,128)S(1)}, u32[]{:S(2)}) %copy-start.2) | copy-done | bytes 2097176
  64.0 1.9 %collective-permute-start.7 = (bf16[256,2048]{1,0:T(8,128)(2,1)}, bf16[256,2048]{1,0:T(8,128)(2,1)S(1)}, u32[]{:S(2)}, u32[]{:S(2)}) collective-permute-start(bf16[256,2048]{1,0:T(8,128)(2,1)} %get-tuple-element.11), channel_id=1, source_target_pairs={{0,1},{1,0},{2,3},{3,2},{4,5},{5,4},{6,7},{7,6},{8,9},{9,8},{10,11... | collective-permute-start | bytes 3145736 | tf_op jit(solution)/shard_map/ppermute | solution.py:179
  66.0 0.0 collective-permute-done.5.refs_0_
  66.0 0.0 collective-permute-done.6.refs_1_
  66.0 4.8 %shard_map.68 = (f32[256,2048]{1,0:T(8,128)S(1)}, bf16[256,2048]{1,0:T(8,128)(2,1)}) custom-call(s32[2,2,4]{2,1,0:T(2,128)S(1)} %bitcast.34, bf16[256,256]{1,0:T(8,128)(2,1)S(1)} %bitcast.33, bf16[256,256]{1,0:T(8,128)(2,1)S(1)} %get-tuple-element.17.w_send, bf16[128,4,512]{2,1,0:T(4,128)(2,1)} %collective-permute-done.5.refs_0_, ...), custom_call_target="tpu_custom_call" | custom-call | flops 536870912 | bytes 4194304 | tf_op jit(solution)/shard_map/pallas_call | solution.py:162
  70.7 1.3 %copy-done.4 = f32[256,2048]{1,0:T(8,128)} copy-done((f32[256,2048]{1,0:T(8,128)}, f32[256,2048]{1,0:T(8,128)S(1)}, u32[]{:S(2)}) %copy-start.4) | copy-done | bytes 2097176
  72.0 0.0 collective-permute-start.8
  72.1 0.0 all-to-all-done.1
  72.2 0.0 copy-start.6
  72.2 15.5 %all_to_all.15 = bf16[16,32,512]{2,1,0:T(8,128)(2,1)S(1)} all-to-all(bf16[16,32,512]{2,1,0:T(8,128)(2,1)S(1)} %broadcast_in_dim.24), channel_id=1, replica_groups=mesh['y'=4,'z'=8,'x'=4,'c'=2] {'y','x'}, dimensions={0} | all-to-all | bytes 1048576 | tf_op jit(solution)/shard_map/all_to_all | solution.py:138
  87.7 1.9 %collective-permute-start.1 = (bf16[512,512]{1,0:T(8,128)(2,1)S(1)}, bf16[512,512]{1,0:T(8,128)(2,1)S(1)}, u32[]{:S(2)}, u32[]{:S(2)}) collective-permute-start(bf16[512,512]{1,0:T(8,128)(2,1)S(1)} %bitcast.31), channel_id=1, source_target_pairs={{0,1},{1,0},{2,3},{3,2},{4,5},{5,4},{6,7},{7,6},{8,9},{9,8},{10,11... | collective-permute-start | bytes 1572872 | tf_op jit(solution)/shard_map/ppermute | solution.py:142
  89.6 0.7 shard_map.66.first
  90.3 0.0 collective-permute-done.7.got_near
  90.3 0.0 collective-permute-done.8.got_far
  90.4 0.0 copy-done.6
  90.4 0.0 copy-done.3
  90.4 0.0 copy-done.5
  90.4 3.0 %shard_map.69.base = f32[256,4,512]{2,1,0:T(4,128)S(1)} custom-call(bf16[256,4,512]{2,1,0:T(4,128)(2,1)S(1)} %copy-done.6, f32[256,2048]{1,0:T(8,128)S(1)} %copy-done.3, f32[256,2048]{1,0:T(8,128)S(1)} %copy-done.5, bf16[256,2048]{1,0:T(8,128)(2,1)S(1)} %collective-permute-done.7.got_near, bf16[256,2048]{1,0:T(8,128)(2,1)} %collective-permute-done.8.got_far), custom_call_target="tpu_custom_call" | custom-call | bytes 8388608 | tf_op jit(solution)/shard_map/pallas_call | solution.py:184
  93.3 0.0 collective-permute-done.1.ct
  93.4 1.9 %shard_map.70 = bf16[256,4,512]{2,1,0:T(4,128)(2,1)} custom-call(s32[1]{0:T(128)S(6)} %sub.7.half, bf16[256,4,1024]{2,1,0:T(4,128)(2,1)S(1)} %copy-done.1, bf16[512,512]{1,0:T(8,128)(2,1)S(1)} %collective-permute-done.1.ct, f32[1024,512]{1,0:T(8,128)S(1)} %shard_map.66.first, f32[256,4,512]{2,1,0:T(4,128)S(1)} %shard_map.69.base), custom_call_target="tpu_custom_call" | custom-call | flops 536870912 | bytes 6291456 | tf_op jit(solution)/shard_map/pallas_call | solution.py:191
  (9 shorter events, 0.2 us)
Async XLA Ops:
  0.8 1.6 %copy-start = (bf16[256,4,1024]{2,1,0:T(4,128)(2,1)S(1)}, bf16[256,4,1024]{2,1,0:T(4,128)(2,1)}, u32[]{:S(2)}) copy-start(bf16[256,4,1024]{2,1,0:T(4,128)(2,1)} %chol.7) | copy-start | bytes 6291460
  4.4 16.4 %collective-permute-start = (bf16[512,512]{1,0:T(8,128)(2,1)S(1)}, bf16[512,512]{1,0:T(8,128)(2,1)}, u32[]{:S(2)}, u32[]{:S(2)}) collective-permute-start(bf16[512,512]{1,0:T(8,128)(2,1)S(1)} %shard_map.65), channel_id=1, source_target_pairs={{0,1},{1,0},{2,3},{3,2},{4,5},{5,4},{6,7},{7,6},{8,9},{9,8},{10,11... | collective-permute-start | bytes 1572872 | tf_op jit(solution)/shard_map/ppermute | solution.py:124
  7.7 28.1 %collective-permute-start.3 = (bf16[256,4,512]{2,1,0:T(4,128)(2,1)}, bf16[256,4,512]{2,1,0:T(4,128)(2,1)}, u32[]{:S(2)}, u32[]{:S(2)}) collective-permute-start(bf16[256,4,512]{2,1,0:T(4,128)(2,1)} %refs_0_.1), channel_id=1, source_target_pairs={{0,2},{2,4},{4,6},{6,0},{1,3},{3,5},{5,7},{7,1},{8,10},{10,12},{12... | collective-permute-start | bytes 3145736 | tf_op jit(solution)/shard_map/ppermute | solution.py:109
  7.7 30.1 %collective-permute-start.4 = (bf16[256,4,512]{2,1,0:T(4,128)(2,1)}, bf16[256,4,512]{2,1,0:T(4,128)(2,1)}, u32[]{:S(2)}, u32[]{:S(2)}) collective-permute-start(bf16[256,4,512]{2,1,0:T(4,128)(2,1)} %refs_0_.1), channel_id=1, source_target_pairs={{0,6},{2,0},{4,2},{6,4},{1,7},{3,1},{5,3},{7,5},{8,14},{10,8},{12,... | collective-permute-start | bytes 3145736 | tf_op jit(solution)/shard_map/ppermute | solution.py:110
  13.7 5.1 %copy-start.1 = (bf16[256,4,1024]{2,1,0:T(4,128)(2,1)S(1)}, bf16[256,4,1024]{2,1,0:T(4,128)(2,1)}, u32[]{:S(2)}) copy-start(bf16[256,4,1024]{2,1,0:T(4,128)(2,1)} %chol.7) | copy-start | bytes 6291460
  18.2 32.9 %collective-permute-start.2 = (bf16[256,4,256]{2,0,1:T(8,128)(2,1)}, bf16[256,4,256]{2,0,1:T(8,128)(2,1)}, u32[]{:S(2)}, u32[]{:S(2)}) collective-permute-start(bf16[256,4,256]{2,0,1:T(8,128)(2,1)} %bitcast.38), channel_id=1, source_target_pairs={{0,1},{1,0},{2,3},{3,2},{4,5},{5,4},{6,7},{7,6},{8,9},{9,8},{10,11... | collective-permute-start | bytes 1572872 | tf_op jit(solution)/shard_map/ppermute | solution.py:151
  20.8 6.4 %copy-start.7 = (bf16[256,2048]{0,1:T(8,128)(2,1)S(1)}, bf16[256,2048]{0,1:T(8,128)(2,1)}, u32[]{:S(2)}) copy-start(bf16[256,2048]{0,1:T(8,128)(2,1)} %bitcast_multiply_fusion) | copy-start | bytes 3145732
  22.9 20.1 %all-to-all-start = ((bf16[16,32,512]{2,1,0:T(8,128)(2,1)}), bf16[16,32,512]{2,1,0:T(8,128)(2,1)}, u32[]{:S(2)}, u32[]{:S(2)}) async-start(bf16[16,32,512]{2,1,0:T(8,128)(2,1)} %bitcast.37), calls=%async_computation | async-start | bytes 1048576 | tf_op jit(solution)/shard_map/all_to_all | solution.py:132
  27.9 14.7 %copy-start.8 = (bf16[256,1,1,256]{0,3,2,1:T(8,128)(2,1)S(1)}, bf16[256,1,1,256]{0,3,2,1:T(8,128)(2,1)}, u32[]{:S(2)}) copy-start(bf16[256,1,1,256]{0,3,2,1:T(8,128)(2,1)} %get-tuple-element.16) | copy-start | bytes 393220
  37.8 28.1 %collective-permute-start.5 = (bf16[128,4,512]{2,1,0:T(4,128)(2,1)}, bf16[128,4,512]{2,1,0:T(4,128)(2,1)}, u32[]{:S(2)}, u32[]{:S(2)}) collective-permute-start(bf16[128,4,512]{2,1,0:T(4,128)(2,1)} %slice.8), channel_id=1, source_target_pairs={{0,2},{2,4},{4,6},{6,0},{1,3},{3,5},{5,7},{7,1},{8,10},{10,12},{12... | collective-permute-start | bytes 1572872 | tf_op jit(solution)/shard_map/ppermute | solution.py:171
  39.9 26.1 %collective-permute-start.6 = (bf16[128,4,512]{2,1,0:T(4,128)(2,1)}, bf16[128,4,512]{2,1,0:T(4,128)(2,1)}, u32[]{:S(2)}, u32[]{:S(2)}) collective-permute-start(bf16[128,4,512]{2,1,0:T(4,128)(2,1)} %slice.9), channel_id=1, source_target_pairs={{0,6},{2,0},{4,2},{6,4},{1,7},{3,1},{5,3},{7,5},{8,14},{10,8},{12,... | collective-permute-start | bytes 1572872 | tf_op jit(solution)/shard_map/ppermute | solution.py:172
  44.9 27.2 %all-to-all-start.1 = ((bf16[8,32,512]{2,1,0:T(8,128)(2,1)}), bf16[8,32,512]{2,1,0:T(8,128)(2,1)S(1)}, u32[]{:S(2)}, u32[]{:S(2)}) async-start(bf16[8,32,512]{2,1,0:T(8,128)(2,1)} %broadcast_in_dim.11), calls=%async_computation.1 | async-start | bytes 524288 | tf_op jit(solution)/shard_map/all_to_all | solution.py:134
  62.7 1.3 %copy-start.2 = (f32[256,2048]{1,0:T(8,128)}, f32[256,2048]{1,0:T(8,128)S(1)}, u32[]{:S(2)}) copy-start(f32[256,2048]{1,0:T(8,128)S(1)} %get-tuple-element.9.near) | copy-start | bytes 6291460
  64.0 26.3 %collective-permute-start.7 = (bf16[256,2048]{1,0:T(8,128)(2,1)}, bf16[256,2048]{1,0:T(8,128)(2,1)S(1)}, u32[]{:S(2)}, u32[]{:S(2)}) collective-permute-start(bf16[256,2048]{1,0:T(8,128)(2,1)} %get-tuple-element.11), channel_id=1, source_target_pairs={{0,1},{1,0},{2,3},{3,2},{4,5},{5,4},{6,7},{7,6},{8,9},{9,8},{10,11... | collective-permute-start | bytes 3145736 | tf_op jit(solution)/shard_map/ppermute | solution.py:179
  70.7 1.3 %copy-start.4 = (f32[256,2048]{1,0:T(8,128)}, f32[256,2048]{1,0:T(8,128)S(1)}, u32[]{:S(2)}) copy-start(f32[256,2048]{1,0:T(8,128)S(1)} %get-tuple-element.10.far) | copy-start | bytes 6291460
  72.0 18.3 %collective-permute-start.8 = (bf16[256,2048]{1,0:T(8,128)(2,1)}, bf16[256,2048]{1,0:T(8,128)(2,1)}, u32[]{:S(2)}, u32[]{:S(2)}) collective-permute-start(bf16[256,2048]{1,0:T(8,128)(2,1)} %get-tuple-element.12), channel_id=1, source_target_pairs={{0,1},{1,0},{2,3},{3,2},{4,5},{5,4},{6,7},{7,6},{8,9},{9,8},{10,11... | collective-permute-start | bytes 3145736 | tf_op jit(solution)/shard_map/ppermute | solution.py:183
  72.2 18.2 %copy-start.6 = (bf16[256,4,512]{2,1,0:T(4,128)(2,1)S(1)}, bf16[256,4,512]{2,1,0:T(4,128)(2,1)}, u32[]{:S(2)}) copy-start(bf16[256,4,512]{2,1,0:T(4,128)(2,1)} %source.1) | copy-start | bytes 3145732
  87.7 2.7 %copy-start.3 = (f32[256,2048]{1,0:T(8,128)S(1)}, f32[256,2048]{1,0:T(8,128)}, u32[]{:S(2)}) copy-start(f32[256,2048]{1,0:T(8,128)} %copy-done.2) | copy-start | bytes 6291460
  87.7 2.7 %copy-start.5 = (f32[256,2048]{1,0:T(8,128)S(1)}, f32[256,2048]{1,0:T(8,128)}, u32[]{:S(2)}) copy-start(f32[256,2048]{1,0:T(8,128)} %copy-done.4) | copy-start | bytes 6291460
  87.7 5.6 %collective-permute-start.1 = (bf16[512,512]{1,0:T(8,128)(2,1)S(1)}, bf16[512,512]{1,0:T(8,128)(2,1)S(1)}, u32[]{:S(2)}, u32[]{:S(2)}) collective-permute-start(bf16[512,512]{1,0:T(8,128)(2,1)S(1)} %bitcast.31), channel_id=1, source_target_pairs={{0,1},{1,0},{2,3},{3,2},{4,5},{5,4},{6,7},{7,6},{8,9},{9,8},{10,11... | collective-permute-start | bytes 1572872 | tf_op jit(solution)/shard_map/ppermute | solution.py:142

commit v3 on v0

v3 whole, which is shorter than its diff:
```python
import functools

import jax
import jax.numpy as jnp
from jax import lax
from jax.experimental import pallas as pl
from jax.experimental.pallas import tpu as pltpu
from jax.sharding import Mesh, PartitionSpec as P

TILE = 64
SWAP = [(0, 1), (1, 0)]
F32, BF16 = jnp.float32, jnp.bfloat16
VMEM = pl.BlockSpec(memory_space=pltpu.VMEM)
SMEM = pl.BlockSpec(memory_space=pltpu.SMEM)
ANY = pl.BlockSpec(memory_space=pl.ANY)
shape = jax.ShapeDtypeStruct


def shift(n, d):
    return [(i, (i + d) % n) for i in range(n)]


def call(kernel, outs, specs, micros, scratch=(), out_space=VMEM):
    return pl.pallas_call(
        kernel,
        out_shape=outs,
        in_specs=specs,
        out_specs=jax.tree.map(lambda _: out_space, outs),
        scratch_shapes=scratch,
        compiler_params=pltpu.CompilerParams(vmem_limit_bytes=24 * 2**20),
        cost_estimate=pl.CostEstimate(
            flops=0, bytes_accessed=int(micros * 3.4e6), transcendentals=0
        ),
    )


def dot(a, b, over=1):
    return lax.dot_general(a, b, (((over,), (0,)), ((), ())), preferred_element_type=F32)


def column_kernel(place, half, mask, t, chol, out, t_buf, chol_buf, sems):
    rows, occ, cols = t.shape
    width = out.shape[0]
    steps = rows // TILE
    start = pl.multiple_of(half[0] * width, width)
    copies = []
    for v in range(steps):
        at = pl.ds(v * TILE, TILE)
        copies.append((
            pltpu.make_async_copy(t.at[at], t_buf.at[v], sems.at[0, v]),
            pltpu.make_async_copy(
                chol.at[at, :, pl.ds(start, width)], chol_buf.at[v], sems.at[1, v]
            ),
        ))
    for pair in copies:
        for copy in pair:
            copy.start()
    k_id = lax.broadcasted_iota(jnp.int32, (occ, cols), 0)
    total = None
    for v in range(steps):
        keep = jnp.zeros((occ, cols), F32)
        for k in range(occ):
            kept = mask[place[0] * steps + v, place[1] * occ + k]
            keep = jnp.where(k_id == k, kept.astype(F32), keep)
        for copy in copies[v]:
            copy.wait()
        masked = (t_buf[v] * keep.astype(BF16)[None]).reshape(TILE * occ, cols)
        term = dot(chol_buf[v].reshape(TILE * occ, width), masked, 0)
        total = term if total is None else total + term
    out[...] = total.astype(out.dtype)


def w_kernel(place, tiles, w, after, mine, other):
    rows = w.shape[0]
    steps = rows // TILE
    ring = mine.shape[1] // rows
    lane = lax.broadcasted_iota(jnp.int32, (TILE, 2 * TILE), 1)
    for d in range(ring):
        for out, core in ((mine, place[3]), (other, 1 - place[3])):
            block = ((place[2] + d) % ring) * 2 + core
            for j in range(rows // (2 * TILE)):
                at = pl.ds(pl.multiple_of(block * rows + j * 2 * TILE, 2 * TILE), 2 * TILE)
                col = block * steps + 2 * j
                for v in range(steps):
                    row = place[0] * steps + v
                    keep = jnp.where(
                        lane < TILE, tiles[row, col].astype(F32), tiles[row, col + 1].astype(F32)
                    )
                    here = slice(v * TILE, (v + 1) * TILE)
                    to = slice(d * rows + j * 2 * TILE, d * rows + (j + 1) * 2 * TILE)
                    out[here, to] = w[here, at] * keep.astype(BF16)


def split_kernel(left, right, after, low, high, sems):
    half = low.shape[0]
    first = pltpu.make_async_copy(left.at[pl.ds(0, half)], low, sems.at[0])
    second = pltpu.make_async_copy(right.at[pl.ds(half, half)], high, sems.at[1])
    first.start()
    second.start()
    first.wait()
    second.wait()


def order(occ):
    n = TILE * occ
    row = lax.broadcasted_iota(jnp.int32, (n, n), 0)
    col = lax.broadcasted_iota(jnp.int32, (n, n), 1)
    return jnp.where(col == (row % TILE) * occ + row // TILE, 1.0, 0.0)


def ladder_kernel(ring, n, last, place, mask, w_mine, w_other, *refs):
    blocks, (kept, sent) = refs[:n], refs[-2:]
    rows = kept.shape[0]
    occ, cols = blocks[0].shape[1:]
    steps = rows // TILE
    perm = order(occ)
    k_id = lax.broadcasted_iota(jnp.int32, perm.shape, 0) // TILE
    right = [[] for _ in range(occ)]
    for b, v0, d in ring:
        block = blocks[b]
        chip = (place[2] + d) % 4
        for v in range(block.shape[0] // TILE):
            scale = jnp.zeros(perm.shape, F32)
            for k in range(occ):
                kept_one = mask[(chip * 2 + place[3]) * steps + v0 + v, place[1] * occ + k]
                scale = jnp.where(k_id == k, kept_one.astype(F32), scale)
            laid = dot(
                (perm * scale).astype(BF16),
                block[v * TILE:(v + 1) * TILE].reshape(TILE * occ, cols),
            ).astype(BF16)
            for k in range(occ):
                right[k].append(laid[k * TILE:(k + 1) * TILE])
    ds = [d for i, (_, _, d) in enumerate(ring) if i == 0 or ring[i - 1][2] != d]
    for k in range(occ):
        at = slice(k * cols, (k + 1) * cols)
        for w, out in ((w_mine, kept), (w_other, sent)):
            total = refs[n + (out is sent)][:, at] if last else None
            for i, d in enumerate(ds):
                part = jnp.concatenate(right[k][i * steps:(i + 1) * steps], 0)
                term = dot(w[:, d * rows:(d + 1) * rows], part)
                total = term if total is None else total + term
            out[:, at] = total.astype(out.dtype)


def base_kernel(source, kept, got, out):
    occ, cols = source.shape[1:]
    rows = source.shape[0]
    back = order(occ).astype(BF16)
    for v in range(rows // TILE):
        here = slice(v * TILE, (v + 1) * TILE)
        whole = jnp.concatenate(
            [
                kept[here, k * cols:(k + 1) * cols]
                + got[here, k * cols:(k + 1) * cols].astype(F32)
                for k in range(occ)
            ],
            0,
        )
        high = whole.astype(BF16)
        low = (whole - high.astype(F32)).astype(BF16)
        out[v * TILE * occ:(v + 1) * TILE * occ] = (
            source[here].reshape(TILE * occ, cols).astype(F32)
            + dot(back, high, 0)
            + dot(back, low, 0)
        )


def first_kernel(half, chol, ct, out):
    rows, occ, _ = chol.shape
    width = ct.shape[0]
    start = pl.multiple_of(half[0] * width, width)
    out[...] = dot(chol[:, :, pl.ds(start, width)].reshape(rows * occ, width), ct[...])


def last_kernel(half, chol, ct, first, base, out):
    rows, occ, _ = chol.shape
    width = ct.shape[0]
    start = pl.multiple_of(half[0] * width, width)
    total = dot(chol[:, :, pl.ds(start, width)].reshape(rows * occ, width), ct[...])
    out[...] = (total + first[...] + base[...]).astype(BF16).reshape(out.shape)


def shards(
    amplitudes, source_block, ladder_integrals, cholesky_vectors, integral_tiles, amplitude_tiles
):
    rows, occ, columns = amplitudes.shape
    vectors = cholesky_vectors.shape[2]
    wide = vectors // 2
    steps = rows // TILE
    ny, nz, nx = lax.axis_size("y"), lax.axis_size("z"), lax.axis_size("x")
    core, x = lax.axis_index("c"), lax.axis_index("x")
    tile = lax.axis_index("y") * nz + lax.axis_index("z")
    place = jnp.stack([x * 2 + core, tile, x, core])
    mine, other = core[None], 1 - core[None]

    from_left = lax.ppermute(amplitudes, "x", shift(nx, 1))
    from_right = lax.ppermute(amplitudes, "x", shift(nx, -1))

    def column(half, kind):
        return call(
            column_kernel,
            shape((wide, columns), kind),
            [SMEM, SMEM, SMEM, ANY, ANY],
            1.5,
            [
                pltpu.VMEM((steps, TILE, occ, columns), BF16),
                pltpu.VMEM((steps, TILE, occ, wide), BF16),
                pltpu.SemaphoreType.DMA((2, steps)),
            ],
        )(place, half, amplitude_tiles, amplitudes, cholesky_vectors)

    got = lax.ppermute(column(other, BF16), "c", SWAP)
    kept = column(mine, F32)

    group = ny * nx
    chunk = wide // group
    s1 = (kept + got.astype(F32)).astype(BF16)
    s = lax.all_to_all(s1.reshape(group, chunk, columns), ("y", "x"), 0, 0, tiled=True)
    s2 = s.astype(F32).sum(0).astype(BF16)
    s = lax.all_to_all(
        jnp.broadcast_to(s2[None], (nz, chunk, columns)), "z", 0, 0, tiled=True
    )
    s3 = s.astype(F32).sum(0).astype(BF16)
    s = lax.all_to_all(
        jnp.broadcast_to(s3[None], (group, chunk, columns)), ("y", "x"), 0, 0, tiled=True
    )
    ct_mine = s.reshape(wide, columns)
    ct_other = lax.ppermute(ct_mine, "c", SWAP)

    w_mine, w_swap = call(
        w_kernel, (shape((rows, nx * rows), BF16),) * 2, [SMEM, SMEM, VMEM, ANY], 1.0
    )(place, integral_tiles, ladder_integrals, s1)
    w_other = lax.ppermute(w_swap, "c", SWAP)

    half = rows // 2
    low, high = call(
        split_kernel,
        (shape((half, occ, columns), BF16),) * 2,
        [ANY, ANY, ANY],
        0.5,
        [pltpu.SemaphoreType.DMA((2,))],
        ANY,
    )(from_left, from_right, s2)
    far_low = lax.ppermute(low, "x", shift(nx, 1))
    far_high = lax.ppermute(high, "x", shift(nx, -1))

    near_kept, near_sent = call(
        functools.partial(ladder_kernel, ((0, 0, 0), (1, 0, -1 % nx), (2, 0, 1)), 3, False),
        (shape((rows, occ * columns), F32),) * 2,
        [SMEM, SMEM] + [VMEM] * 5 + [ANY],
        3.0,
    )(place, amplitude_tiles, w_mine, w_other, amplitudes, from_left, from_right, s3)
    all_kept, all_sent = call(
        functools.partial(ladder_kernel, ((0, 0, 2), (1, steps // 2, 2)), 2, True),
        (shape((rows, occ * columns), F32), shape((rows, occ * columns), BF16)),
        [SMEM, SMEM] + [VMEM] * 6,
        1.2,
    )(place, amplitude_tiles, w_mine, w_other, far_low, far_high, near_kept, near_sent)
    all_got = lax.ppermute(all_sent, "c", SWAP)
    base = call(base_kernel, shape((rows * occ, columns), F32), [VMEM] * 3, 1.2)(
        source_block, all_kept, all_got
    )

    first = call(
        first_kernel, shape((rows * occ, columns), F32), [SMEM, VMEM, VMEM], 0.7
    )(mine, cholesky_vectors, ct_mine)
    return call(
        last_kernel,
        shape((rows, occ, columns), BF16),
        [SMEM, VMEM, VMEM, VMEM, VMEM],
        1.5,
    )(other, cholesky_vectors, ct_other, first, base)


def solution(mesh):
    split = Mesh(mesh.devices.reshape(4, 8, 4, 2), ("y", "z", "x", "c"))
    rows, cols = ("x", "c"), ("y", "z")
    return jax.shard_map(
        shards,
        mesh=split,
        in_specs=(
            P(rows, cols, None),
            P(rows, cols, None),
            P(rows, None),
            P(rows, cols, None),
            P(),
            P(),
        ),
        out_specs=P(rows, cols, None),
        check_vma=False,
    )
```

time: 145 us -> 111 us (0.77)
  blocking collectives: 95.8 us -> 31.2 us
  Pallas kernels: 0 us -> 34.9 us
  starting transfers between devices: 0.01 us -> 18.5 us
  waiting for transfers between devices: 0.04 us -> 17.9 us
  matrix products: 14.6 us -> 0 us
  between operations: 13.5 us -> 0.19 us
  local copies, waits for them, and re-layouts: 13.3 us -> 5.46 us
  other arithmetic: 6.64 us -> 2.2 us
    psum x1 -> x0, blocking collectives: 95.8 us -> none  [shards(): cycle_total = lax.psum(partial_value, ('tile', 'vir')).astype(jnp.bfloat16)]
    pallas_call x0 -> x9, Pallas kernels: none -> 34.9 us  [the longest x1 17 us: shards(): call(split_kernel, (shape((half, occ, columns), BF16),) * 2, [ANY, ANY, A...]
    all_to_all x0 -> x2, blocking collectives: none -> 31.2 us  [the longest x1 17.2 us: shards(): lax.all_to_all(jnp.broadcast_to(s2[None], (nz, chunk, columns)), 'z', 0,...]
    all_to_all x0 -> x1, waiting for transfers between devices: none -> 17.9 us  [shards(): lax.all_to_all(s1.reshape(group, chunk, columns), ('y', 'x'), 0, 0, tiled...]
    dot_general x3 -> x0, matrix products: 14.6 us -> none  [the longest x1 8.07 us: shards(): lax.dot_general(w_eff, flat_amps, (((0,), (0,)), ((), ())), preferred_ele...]
    ppermute x0 -> x8, starting transfers between devices: none -> 14.2 us  [the longest x1 3.73 us: shards(): all_got = lax.ppermute(all_sent, 'c', SWAP)]
    reshape x3 -> x0, local copies, waits for them, and re-layouts: 7.74 us -> none  [the longest x1 3.77 us: shards(): ladder.reshape(local_rows, occ_local, columns)]
    all_to_all x0 -> x1, starting transfers between devices: none -> 4.24 us  [shards(): lax.all_to_all(s1.reshape(group, chunk, columns), ('y', 'x'), 0, 0, tiled...]
  transfers between devices with their start and end apart: 1 -> 9, of which waited for: 0 -> 1; matrix products, arithmetic and copies ran while one was open for 9% -> 2% of each run, Pallas kernels for 0% -> 25%
where the time goes in v3:
time: 111 us; the launch traced here: 110 us
  Pallas kernels  34.9 us (31%)
  blocking collectives  31.2 us (28%)
  starting transfers between devices  18.5 us (17%)
  waiting for transfers between devices  17.9 us (16%)
  local copies, waits for them, and re-layouts  5.46 us (5%)
  other arithmetic  2.2 us (2%)
    all_to_all x1, waiting for transfers between devices, shards(): lax.all_to_all(s1.reshape(group, chunk, columns), ('y', 'x'), 0, 0, tiled...  17.9 us
    all_to_all x1, blocking collectives, shards(): lax.all_to_all(jnp.broadcast_to(s2[None], (nz, chunk, columns)), 'z', 0,...  17.2 us
    pallas_call x1, Pallas kernels, shards(): call(split_kernel, (shape((half, occ, columns), BF16),) * 2, [ANY, ANY, A...  17 us
    all_to_all x1, blocking collectives, shards(): lax.all_to_all(jnp.broadcast_to(s3[None], (group, chunk, columns)), ('y',...  14 us
    pallas_call x2, Pallas kernels, column(): call(column_kernel, shape((wide, columns), kind), [SMEM, SMEM, SMEM, ANY,...  5.62 us
    unnamed x18, local copies, waits for them, and re-layouts  5.4 us
    pallas_call x1, Pallas kernels, shards(): call(functools.partial(ladder_kernel, ((0, 0, 0), (1, 0, -1 % nx), (2, 0,...  4.34 us
    all_to_all x1, starting transfers between devices, shards(): lax.all_to_all(s1.reshape(group, chunk, columns), ('y', 'x'), 0, 0, tiled...  4.24 us
  transfers between devices with their start and end apart: 9, of which 1 were waited for; matrix products, arithmetic and copies ran while one was open for 2% of the time, Pallas kernels for 25%

profile of v3, /device:TPU:1, one launch (start us, length us, event | category | flops | bytes accessed | tf_op | source)
XLA Modules:
  0.0 110.4 jit_solution(13199507821653152397)
XLA Ops:
  0.0 0.0 copy-start.7
  0.0 0.1 pad_add_fusion.place
  0.1 0.0 copy-start
  0.1 1.6 %copy-done = bf16[256,4,1024]{2,1,0:T(4,128)(2,1)S(1)} copy-done((bf16[256,4,1024]{2,1,0:T(4,128)(2,1)S(1)}, bf16[256,4,1024]{2,1,0:T(4,128)(2,1)}, u32[]{:S(2)}) %copy-start) | copy-done | bytes 2097176
  1.7 0.0 copy-start.6
  1.7 0.7 copy-done.6
  2.4 0.0 copy-start.1
  2.4 2.8 %shard_map.65 = bf16[512,512]{1,0:T(8,128)(2,1)S(1)} custom-call(s32[4]{0:T(128)S(1)} %pad_add_fusion.place, s32[1]{0:T(128)S(6)} %sub.3.half, s32[32,128]{1,0:T(8,128)S(1)} %copy-done.6, bf16[256,4,512]{2,1,0:T(4,128)(2,1)} %refs_0_.1, bf16[256,4,1024]{2,1,0:T(4,128)(2,1)S(1)} %copy-done), custom_call_target="tpu_custom_call" | custom-call | bytes 5100000 | tf_op jit(solution)/shard_map/pallas_call | solution.py:200
  5.2 3.3 %collective-permute-start = (bf16[512,512]{1,0:T(8,128)(2,1)S(1)}, bf16[512,512]{1,0:T(8,128)(2,1)S(1)}, u32[]{:S(2)}, u32[]{:S(2)}) collective-permute-start(bf16[512,512]{1,0:T(8,128)(2,1)S(1)} %shard_map.65), channel_id=1, source_target_pairs={{0,1},{1,0},{2,3},{3,2},{4,5},{5,4},{6,7},{7,6},{8,9},{9,8},{10,11... | collective-permute-start | bytes 1572872 | tf_op jit(solution)/shard_map/ppermute | solution.py:212
  8.5 0.0 collective-permute-start.3
  8.5 2.7 %collective-permute-start.4 = (bf16[256,4,512]{2,1,0:T(4,128)(2,1)}, bf16[256,4,512]{2,1,0:T(4,128)(2,1)}, u32[]{:S(2)}, u32[]{:S(2)}) collective-permute-start(bf16[256,4,512]{2,1,0:T(4,128)(2,1)} %refs_0_.1), channel_id=1, source_target_pairs={{0,6},{2,0},{4,2},{6,4},{1,7},{3,1},{5,3},{7,5},{8,14},{10,8},{12,... | collective-permute-start | bytes 3145736 | tf_op jit(solution)/shard_map/ppermute | solution.py:197
  11.2 0.0 copy-done.7
  11.2 0.0 copy-done.1
  11.2 2.8 %shard_map.64 = f32[512,512]{1,0:T(8,128)S(1)} custom-call(s32[4]{0:T(128)S(1)} %pad_add_fusion.place, s32[1]{0:T(128)} %bitcast.half, s32[32,128]{1,0:T(8,128)S(1)} %copy-done.7, bf16[256,4,512]{2,1,0:T(4,128)(2,1)} %refs_0_.1, bf16[256,4,1024]{2,1,0:T(4,128)(2,1)S(1)} %copy-done.1), custom_call_target="tpu_custom_call" | custom-call | bytes 5100000 | tf_op jit(solution)/shard_map/pallas_call | solution.py:200
  14.1 0.0 copy-start.8
  14.1 0.0 collective-permute-done
  14.1 1.0 add_convert_fusion.after
  15.0 4.2 %all-to-all-start = ((bf16[16,32,512]{2,1,0:T(8,128)(2,1)}), bf16[16,32,512]{2,1,0:T(8,128)(2,1)}, u32[]{:S(2)}, u32[]{:S(2)}) async-start(bf16[16,32,512]{2,1,0:T(8,128)(2,1)} %bitcast.4), calls=%async_computation | async-start | bytes 1048576 | tf_op jit(solution)/shard_map/all_to_all | solution.py:218
  19.3 0.0 copy-done.8
  19.3 0.0 copy-start.4
  19.3 1.2 %copy-done.4 = bf16[256,2048]{1,0:T(8,128)(2,1)S(1)} copy-done((bf16[256,2048]{1,0:T(8,128)(2,1)S(1)}, bf16[256,2048]{1,0:T(8,128)(2,1)}, u32[]{:S(2)}) %copy-start.4) | copy-done | bytes 1048600
  20.5 2.0 %shard_map.67 = (bf16[256,1024]{1,0:T(8,128)(2,1)S(1)}, bf16[256,1024]{1,0:T(8,128)(2,1)}) custom-call(s32[4]{0:T(128)S(1)} %pad_add_fusion.place, s32[32,32]{1,0:T(8,128)S(1)} %copy-done.8, bf16[256,2048]{1,0:T(8,128)(2,1)S(1)} %copy-done.4, bf16[512,512]{1,0:T(8,128)(2,1)} %add_convert_fusion.after), custom_call_target="tpu_custom_call" | custom-call | bytes 3400000 | tf_op jit(solution)/shard_map/pallas_call | solution.py:230
  22.5 0.0 copy-start.2
  22.5 0.8 copy-done.2
  23.3 0.6 collective-permute-start.2
  24.0 17.9 %all-to-all-done = bf16[16,32,512]{2,1,0:T(8,128)(2,1)} async-done(((bf16[16,32,512]{2,1,0:T(8,128)(2,1)}), bf16[16,32,512]{2,1,0:T(8,128)(2,1)}, u32[]{:S(2)}, u32[]{:S(2)}) %all-to-all-start) | async-done | bytes 524320 | tf_op jit(solution)/shard_map/all_to_all | solution.py:218
  41.8 1.1 %reduce_sum.24.after = bf16[32,512]{1,0:T(8,128)(2,1)S(1)} reduce(bf16[16,32,512]{2,1,0:T(8,128)(2,1)} %all-to-all-done, bf16[]{:T(256)} %constant.25.clone.1), dimensions={0}, to_apply=%region_0.0 | reduce | flops 245760 | bytes 557058 | tf_op jit(solution)/shard_map/reduce_sum | solution.py:219
  43.0 0.0 collective-permute-done.3.left.refs_1_
  43.0 0.0 collective-permute-done.4.right.refs_2_
  43.0 17.0 %shard_map.68 = (bf16[128,4,512]{2,1,0:T(4,128)(2,1)}, bf16[128,4,512]{2,1,0:T(4,128)(2,1)}) custom-call(bf16[256,4,512]{2,1,0:T(4,128)(2,1)S(1)} %collective-permute-done.3.left.refs_1_, bf16[256,4,512]{2,1,0:T(4,128)(2,1)} %collective-permute-done.4.right.refs_2_, bf16[32,512]{1,0:T(8,128)(2,1)S(1)} %reduce_sum.24.after), custom_call_target="tpu_custom_call" | custom-call | bytes 1700000 | tf_op jit(solution)/shard_map/pallas_call | solution.py:236
  60.0 0.6 collective-permute-start.5
  60.6 2.2 %collective-permute-start.6 = (bf16[128,4,512]{2,1,0:T(4,128)(2,1)}, bf16[128,4,512]{2,1,0:T(4,128)(2,1)}, u32[]{:S(2)}, u32[]{:S(2)}) collective-permute-start(bf16[128,4,512]{2,1,0:T(4,128)(2,1)} %get-tuple-element.16), channel_id=1, source_target_pairs={{0,6},{2,0},{4,2},{6,4},{1,7},{3,1},{5,3},{7,5},{8,14},{10,8},{12,... | collective-permute-start | bytes 1572872 | tf_op jit(solution)/shard_map/ppermute | solution.py:245
  62.8 17.2 %all_to_all.15 = bf16[8,32,512]{2,1,0:T(8,128)(2,1)S(1)} all-to-all(bf16[8,32,512]{2,1,0:T(8,128)(2,1)S(1)} %broadcast_in_dim.7), channel_id=1, replica_groups=mesh['y'=4,'z'=8,'x'=4,'c'=2] {'z'}, dimensions={0} | all-to-all | bytes 524288 | tf_op jit(solution)/shard_map/all_to_all | solution.py:220
  80.0 0.0 collective-permute-done.2.w_other
  80.0 0.0 copy-start.3
  80.0 1.0 copy-done.3
  81.1 4.3 %shard_map.69 = (f32[256,2048]{1,0:T(8,128)S(1)}, f32[256,2048]{1,0:T(8,128)S(1)}) custom-call(s32[4]{0:T(128)S(1)} %pad_add_fusion.place, s32[32,128]{1,0:T(8,128)S(1)} %copy-done.7, bf16[256,1024]{1,0:T(8,128)(2,1)S(1)} %copy-done.3, bf16[256,1024]{1,0:T(8,128)(2,1)} %collective-permute-done.2.w_other, bf16[256,4,512]{2,1,0:T(4,128)(2,1)} %refs_0_.1, ...), custom_call_target="tpu_custom_call" | custom-call | bytes 10200000 | tf_op jit(solution)/shard_map/pallas_call | solution.py:247
  85.4 0.0 collective-permute-done.5.refs_0_
  85.4 0.0 collective-permute-done.6.refs_1_
  85.4 2.5 %shard_map.70 = (f32[256,2048]{1,0:T(8,128)S(1)}, bf16[256,2048]{1,0:T(8,128)(2,1)S(1)}) custom-call(s32[4]{0:T(128)S(1)} %pad_add_fusion.place, s32[32,128]{1,0:T(8,128)S(1)} %copy-done.7, bf16[256,1024]{1,0:T(8,128)(2,1)S(1)} %copy-done.3, bf16[256,1024]{1,0:T(8,128)(2,1)} %collective-permute-done.2.w_other, ...), custom_call_target="tpu_custom_call" | custom-call | bytes 4080000 | tf_op jit(solution)/shard_map/pallas_call | solution.py:253
  87.9 3.7 %collective-permute-start.7 = (bf16[256,2048]{1,0:T(8,128)(2,1)S(1)}, bf16[256,2048]{1,0:T(8,128)(2,1)S(1)}, u32[]{:S(2)}, u32[]{:S(2)}) collective-permute-start(bf16[256,2048]{1,0:T(8,128)(2,1)S(1)} %get-tuple-element.20), channel_id=1, source_target_pairs={{0,1},{1,0},{2,3},{3,2},{4,5},{5,4},{6,7},{7,6},{8,9},{9,8},{10,11... | collective-permute-start | bytes 3145736 | tf_op jit(solution)/shard_map/ppermute | solution.py:259
  91.7 14.0 %all_to_all.16 = bf16[16,32,512]{2,1,0:T(8,128)(2,1)S(1)} all-to-all(bf16[16,32,512]{2,1,0:T(8,128)(2,1)S(1)} %broadcast_in_dim.8), channel_id=1, replica_groups=mesh['y'=4,'z'=8,'x'=4,'c'=2] {'y','x'}, dimensions={0} | all-to-all | bytes 1048576 | tf_op jit(solution)/shard_map/all_to_all | solution.py:224
  105.7 0.0 copy-start.5
  105.7 1.1 collective-permute-start.1
  106.8 0.7 shard_map.66.first
  107.5 0.0 collective-permute-done.7.got
  107.5 0.0 copy-done.5
  107.5 1.1 shard_map.71.base
  108.6 0.0 collective-permute-done.1.ct
  108.6 1.8 %shard_map.72 = bf16[256,4,512]{2,1,0:T(4,128)(2,1)} custom-call(s32[1]{0:T(128)S(6)} %sub.3.half, bf16[256,4,1024]{2,1,0:T(4,128)(2,1)S(1)} %copy-done.1, bf16[512,512]{1,0:T(8,128)(2,1)S(1)} %collective-permute-done.1.ct, f32[1024,512]{1,0:T(8,128)S(1)} %shard_map.66.first, f32[1024,512]{1,0:T(8,128)S(1)} %shard_map.71.base), custom_call_target="tpu_custom_call" | custom-call | bytes 5100000 | tf_op jit(solution)/shard_map/pallas_call | solution.py:267
  (3 shorter events, 0.1 us)
Async XLA Ops:
  0.0 11.2 %copy-start.7 = (s32[32,128]{1,0:T(8,128)S(1)}, s32[32,128]{1,0:T(8,128)}, u32[]{:S(2)}) copy-start(s32[32,128]{1,0:T(8,128)} %mask.7) | copy-start | bytes 49156
  0.1 1.6 %copy-start = (bf16[256,4,1024]{2,1,0:T(4,128)(2,1)S(1)}, bf16[256,4,1024]{2,1,0:T(4,128)(2,1)}, u32[]{:S(2)}) copy-start(bf16[256,4,1024]{2,1,0:T(4,128)(2,1)} %chol.7) | copy-start | bytes 6291460
  1.7 0.7 copy-start.6
  2.4 8.8 %copy-start.1 = (bf16[256,4,1024]{2,1,0:T(4,128)(2,1)S(1)}, bf16[256,4,1024]{2,1,0:T(4,128)(2,1)}, u32[]{:S(2)}) copy-start(bf16[256,4,1024]{2,1,0:T(4,128)(2,1)} %chol.7) | copy-start | bytes 6291460
  5.2 8.9 %collective-permute-start = (bf16[512,512]{1,0:T(8,128)(2,1)S(1)}, bf16[512,512]{1,0:T(8,128)(2,1)S(1)}, u32[]{:S(2)}, u32[]{:S(2)}) collective-permute-start(bf16[512,512]{1,0:T(8,128)(2,1)S(1)} %shard_map.65), channel_id=1, source_target_pairs={{0,1},{1,0},{2,3},{3,2},{4,5},{5,4},{6,7},{7,6},{8,9},{9,8},{10,11... | collective-permute-start | bytes 1572872 | tf_op jit(solution)/shard_map/ppermute | solution.py:212
  8.5 34.4 %collective-permute-start.3 = (bf16[256,4,512]{2,1,0:T(4,128)(2,1)}, bf16[256,4,512]{2,1,0:T(4,128)(2,1)S(1)}, u32[]{:S(2)}, u32[]{:S(2)}) collective-permute-start(bf16[256,4,512]{2,1,0:T(4,128)(2,1)} %refs_0_.1), channel_id=1, source_target_pairs={{0,2},{2,4},{4,6},{6,0},{1,3},{3,5},{5,7},{7,1},{8,10},{10,12},{12... | collective-permute-start | bytes 3145736 | tf_op jit(solution)/shard_map/ppermute | solution.py:196
  8.5 34.4 %collective-permute-start.4 = (bf16[256,4,512]{2,1,0:T(4,128)(2,1)}, bf16[256,4,512]{2,1,0:T(4,128)(2,1)}, u32[]{:S(2)}, u32[]{:S(2)}) collective-permute-start(bf16[256,4,512]{2,1,0:T(4,128)(2,1)} %refs_0_.1), channel_id=1, source_target_pairs={{0,6},{2,0},{4,2},{6,4},{1,7},{3,1},{5,3},{7,5},{8,14},{10,8},{12,... | collective-permute-start | bytes 3145736 | tf_op jit(solution)/shard_map/ppermute | solution.py:197
  14.1 5.2 %copy-start.8 = (s32[32,32]{1,0:T(8,128)S(1)}, s32[32,32]{1,0:T(8,128)}, u32[]{:S(2)}) copy-start(s32[32,32]{1,0:T(8,128)} %tiles.1) | copy-start | bytes 12292
  15.0 26.8 %all-to-all-start = ((bf16[16,32,512]{2,1,0:T(8,128)(2,1)}), bf16[16,32,512]{2,1,0:T(8,128)(2,1)}, u32[]{:S(2)}, u32[]{:S(2)}) async-start(bf16[16,32,512]{2,1,0:T(8,128)(2,1)} %bitcast.4), calls=%async_computation | async-start | bytes 1048576 | tf_op jit(solution)/shard_map/all_to_all | solution.py:218
  19.3 1.2 %copy-start.4 = (bf16[256,2048]{1,0:T(8,128)(2,1)S(1)}, bf16[256,2048]{1,0:T(8,128)(2,1)}, u32[]{:S(2)}) copy-start(bf16[256,2048]{1,0:T(8,128)(2,1)} %w.1) | copy-start | bytes 3145732
  22.5 0.8 copy-start.2
  23.3 56.7 %collective-permute-start.2 = (bf16[256,1024]{1,0:T(8,128)(2,1)}, bf16[256,1024]{1,0:T(8,128)(2,1)}, u32[]{:S(2)}, u32[]{:S(2)}) collective-permute-start(bf16[256,1024]{1,0:T(8,128)(2,1)} %get-tuple-element.14), channel_id=1, source_target_pairs={{0,1},{1,0},{2,3},{3,2},{4,5},{5,4},{6,7},{7,6},{8,9},{9,8},{10,11... | collective-permute-start | bytes 1572872 | tf_op jit(solution)/shard_map/ppermute | solution.py:233
  60.0 25.4 %collective-permute-start.5 = (bf16[128,4,512]{2,1,0:T(4,128)(2,1)}, bf16[128,4,512]{2,1,0:T(4,128)(2,1)}, u32[]{:S(2)}, u32[]{:S(2)}) collective-permute-start(bf16[128,4,512]{2,1,0:T(4,128)(2,1)} %get-tuple-element.15), channel_id=1, source_target_pairs={{0,2},{2,4},{4,6},{6,0},{1,3},{3,5},{5,7},{7,1},{8,10},{10,12},{12... | collective-permute-start | bytes 1572872 | tf_op jit(solution)/shard_map/ppermute | solution.py:244
  60.6 24.8 %collective-permute-start.6 = (bf16[128,4,512]{2,1,0:T(4,128)(2,1)}, bf16[128,4,512]{2,1,0:T(4,128)(2,1)}, u32[]{:S(2)}, u32[]{:S(2)}) collective-permute-start(bf16[128,4,512]{2,1,0:T(4,128)(2,1)} %get-tuple-element.16), channel_id=1, source_target_pairs={{0,6},{2,0},{4,2},{6,4},{1,7},{3,1},{5,3},{7,5},{8,14},{10,8},{12,... | collective-permute-start | bytes 1572872 | tf_op jit(solution)/shard_map/ppermute | solution.py:245
  80.0 1.0 copy-start.3
  87.9 19.6 %collective-permute-start.7 = (bf16[256,2048]{1,0:T(8,128)(2,1)S(1)}, bf16[256,2048]{1,0:T(8,128)(2,1)S(1)}, u32[]{:S(2)}, u32[]{:S(2)}) collective-permute-start(bf16[256,2048]{1,0:T(8,128)(2,1)S(1)} %get-tuple-element.20), channel_id=1, source_target_pairs={{0,1},{1,0},{2,3},{3,2},{4,5},{5,4},{6,7},{7,6},{8,9},{9,8},{10,11... | collective-permute-start | bytes 3145736 | tf_op jit(solution)/shard_map/ppermute | solution.py:259
  105.7 1.8 %copy-start.5 = (bf16[256,4,512]{2,1,0:T(4,128)(2,1)S(1)}, bf16[256,4,512]{2,1,0:T(4,128)(2,1)}, u32[]{:S(2)}) copy-start(bf16[256,4,512]{2,1,0:T(4,128)(2,1)} %source.1) | copy-start | bytes 3145732
  105.7 2.9 %collective-permute-start.1 = (bf16[512,512]{1,0:T(8,128)(2,1)S(1)}, bf16[512,512]{1,0:T(8,128)(2,1)S(1)}, u32[]{:S(2)}, u32[]{:S(2)}) collective-permute-start(bf16[512,512]{1,0:T(8,128)(2,1)S(1)} %bitcast.6), channel_id=1, source_target_pairs={{0,1},{1,0},{2,3},{3,2},{4,5},{5,4},{6,7},{7,6},{8,9},{9,8},{10,11... | collective-permute-start | bytes 1572872 | tf_op jit(solution)/shard_map/ppermute | solution.py:228

commit v4 on v3

v4 whole, which is shorter than its diff:
```python
import functools

import jax
import jax.numpy as jnp
from jax import lax
from jax.experimental import pallas as pl
from jax.experimental.pallas import tpu as pltpu
from jax.sharding import Mesh, PartitionSpec as P

TILE = 64
FULL = 58
SWAP = [(0, 1), (1, 0)]
F32, BF16 = jnp.float32, jnp.bfloat16
VMEM = pl.BlockSpec(memory_space=pltpu.VMEM)
SMEM = pl.BlockSpec(memory_space=pltpu.SMEM)
ANY = pl.BlockSpec(memory_space=pl.ANY)
shape = jax.ShapeDtypeStruct


def shift(n, d):
    return [(i, (i + d) % n) for i in range(n)]


def call(kernel, outs, specs, micros, limit, scratch=(), spaces=None, grid=()):
    return pl.pallas_call(
        kernel,
        out_shape=outs,
        grid=grid,
        in_specs=specs,
        out_specs=spaces or jax.tree.map(lambda _: VMEM, outs),
        scratch_shapes=scratch,
        compiler_params=pltpu.CompilerParams(vmem_limit_bytes=limit * 2**20),
        cost_estimate=pl.CostEstimate(
            flops=0, bytes_accessed=int(micros * 3.4e6), transcendentals=0
        ),
    )


def dot(a, b, over=1):
    return lax.dot_general(a, b, (((over,), (0,)), ((), ())), preferred_element_type=F32)


def column_kernel(vir, tile, half, tiles, t, chol, *refs):
    out, pieces = refs[0], refs[1:-6]
    t_buf, chol_buf, mask, sems, piece_sems, mask_sem = refs[-6:]
    rows, occ, cols = t.shape
    width = out.shape[0]
    steps = rows // TILE
    start = pl.multiple_of(half[0] * width, width)
    mask_copy = pltpu.make_async_copy(tiles, mask, mask_sem)
    mask_copy.start()
    copies = []
    for v in range(steps):
        at = pl.ds(v * TILE, TILE)
        copies.append((
            pltpu.make_async_copy(t.at[at], t_buf.at[v], sems.at[0, v]),
            pltpu.make_async_copy(
                chol.at[at, :, pl.ds(start, width)], chol_buf.at[v], sems.at[1, v]
            ),
        ))
    for pair in copies:
        for copy in pair:
            copy.start()
    k_id = lax.broadcasted_iota(jnp.int32, (occ, cols), 0)
    total = None
    outgoing = []
    mask_copy.wait()
    for v in range(steps):
        keep = jnp.zeros((occ, cols), F32)
        for k in range(occ):
            kept = mask[vir[0] * steps + v, tile[0] * occ + k]
            keep = jnp.where(k_id == k, kept.astype(F32), keep)
        for copy in copies[v]:
            copy.wait()
        for piece in pieces[v * 2 // steps:][:1]:
            here = pl.ds((v % (steps // 2)) * TILE, TILE)
            outgoing.append(pltpu.make_async_copy(t_buf.at[v], piece.at[here], piece_sems.at[v]))
            outgoing[-1].start()
        masked = (t_buf[v] * keep.astype(BF16)[None]).reshape(TILE * occ, cols)
        term = dot(chol_buf[v].reshape(TILE * occ, width), masked, 0)
        total = term if total is None else total + term
    out[...] = total.astype(out.dtype)
    for copy in outgoing:
        copy.wait()


def add_kernel(kept, got, out):
    out[...] = (kept[...] + got[...].astype(F32)).astype(BF16)


def w_kernel(places, vir, x, core, tiles, w, after, mine, other):
    rows = w.shape[0]
    steps = rows // TILE
    ring = len(places)
    lane = lax.broadcasted_iota(jnp.int32, (TILE, 2 * TILE), 1)
    for i, d in enumerate(places):
        for out, which in ((mine, core[0]), (other, 1 - core[0])):
            block = ((x[0] + d) % ring) * 2 + which
            for j in range(rows // (2 * TILE)):
                at = pl.ds(pl.multiple_of(block * rows + j * 2 * TILE, 2 * TILE), 2 * TILE)
                col = block * steps + 2 * j
                for v in range(steps):
                    row = vir[0] * steps + v
                    keep = jnp.where(
                        lane < TILE, tiles[row, col].astype(F32), tiles[row, col + 1].astype(F32)
                    )
                    here = slice(v * TILE, (v + 1) * TILE)
                    to = slice(i * rows + j * 2 * TILE, i * rows + (j + 1) * 2 * TILE)
                    out[here, to] = w[here, at] * keep.astype(BF16)


def pieces_kernel(t, left, right, after, *refs):
    outs, token, held, sems = refs[:4], refs[4], refs[5], refs[6]
    token[...] = jnp.zeros_like(token)
    half = left.shape[0]
    sources = (t.at[pl.ds(0, half)], t.at[pl.ds(half, half)], left, right)
    inward = [
        pltpu.make_async_copy(source, held.at[i], sems.at[0, i])
        for i, source in enumerate(sources)
    ]
    outward = [
        pltpu.make_async_copy(held.at[i], out, sems.at[1, i]) for i, out in enumerate(outs)
    ]
    for copy in inward:
        copy.start()
    for copy, then in zip(inward, outward):
        copy.wait()
        then.start()
    for copy in outward:
        copy.wait()


def pass_kernel(value, after, out):
    out[...] = value[...]


def sum_kernel(parts, *refs):
    out = refs[-1]
    total = parts[0].astype(F32)
    for i in range(1, parts.shape[0]):
        total = total + parts[i].astype(F32)
    total = total.astype(BF16)
    for i in range(out.shape[0]):
        out[i] = total


def permutation(n, occ):
    row = lax.broadcasted_iota(jnp.int32, (n, n), 0)
    col = lax.broadcasted_iota(jnp.int32, (n, n), 1)
    per = n // occ
    return jnp.where(col == (row % per) * occ + row // per, 1.0, 0.0), row // per


def lay_block(block, mask, row, col, right, start):
    rows, occ, cols = block.shape
    perm, k_id = permutation(TILE * occ, occ)
    for v in range(rows // TILE):
        scale = jnp.zeros(perm.shape, F32)
        for k in range(occ):
            scale = jnp.where(k_id == k, mask[row + v, col + k].astype(F32), scale)
        tile = block[v * TILE:(v + 1) * TILE].reshape(TILE * occ, cols)
        laid = dot((perm * scale).astype(BF16), tile).astype(BF16)
        at = slice(start + v * TILE, start + (v + 1) * TILE)
        for k in range(occ):
            right[k, at] = laid[k * TILE:(k + 1) * TILE]


def lay_kernel(ring, x, tile, core, mask, *refs):
    n = len(ring)
    blocks, (out, token), (held, right, in_sems, out_sems) = refs[:n], refs[n:n + 2], refs[n + 2:]
    token[...] = jnp.zeros_like(token)
    occ = blocks[0].shape[1]
    spots = []
    start = 0
    for block in blocks:
        spots.append(pl.ds(start, block.shape[0]))
        start += block.shape[0]
    inward = [
        pltpu.make_async_copy(block, held.at[spot], in_sems.at[i])
        for i, (block, spot) in enumerate(zip(blocks, spots))
    ]
    outward = [
        pltpu.make_async_copy(right.at[:, spot], out.at[:, spot], out_sems.at[i])
        for i, spot in enumerate(spots)
    ]
    for copy in inward:
        copy.start()
    for (v0, d, chips, steps), spot, copy, then in zip(ring, spots, inward, outward):
        copy.wait()
        row = ((x[0] + d) % chips * 2 + core[0]) * steps + v0
        lay_block(held.at[spot], mask, row, tile[0] * occ, right, spot.start)
        then.start()
    for copy in outward:
        copy.wait()


def ladder_kernel(ring, x, tile, core, mask, w_mine, w_other, laid, source, after, *refs):
    n = len(ring)
    blocks, (base, low_sent, high_sent, token) = refs[:n], refs[n:n + 4]
    held, right, w_held, source_held, base_held, sent_held, in_sems, out_sems = refs[n + 4:]
    token[...] = jnp.zeros_like(token)
    rows, occ, cols = source.shape
    steps = rows // TILE
    group = TILE * occ
    near = laid.shape[1]
    spots = []
    start = 0
    for block in blocks:
        spots.append(pl.ds(start, block.shape[0]))
        start += block.shape[0]
    copies = [
        pltpu.make_async_copy(block, held.at[spot], in_sems.at[i])
        for i, (block, spot) in enumerate(zip(blocks, spots))
    ]
    copies += [
        pltpu.make_async_copy(w_other, w_held.at[pl.ds(0, rows)], in_sems.at[n]),
        pltpu.make_async_copy(w_mine, w_held.at[pl.ds(rows, rows)], in_sems.at[n + 1]),
        pltpu.make_async_copy(laid, right.at[:, pl.ds(0, near)], in_sems.at[n + 2]),
        pltpu.make_async_copy(source, source_held, in_sems.at[n + 3]),
    ]
    for copy in copies:
        copy.start()
    for (v0, d, chips, _), spot, copy in zip(ring, spots, copies):
        copy.wait()
        row = ((x[0] + d) % chips * 2 + core[0]) * steps + v0
        lay_block(held.at[spot], mask, row, tile[0] * occ, right, near + spot.start)
    for copy in copies[n:]:
        copy.wait()
    w = w_held[...]
    sums = [dot(w, right[k]).astype(BF16) for k in range(occ)]
    back = permutation(group, occ)[0].astype(BF16)
    outward = []
    for v in range(2 * steps):
        here = slice(v * TILE, (v + 1) * TILE)
        own = dot(back, jnp.concatenate([part[here] for part in sums], 0), 0)
        if v < steps:
            sent_held[v] = own.astype(BF16)
            from_, to = sent_held.at[v], (low_sent, high_sent)[v * 2 // steps]
            at = pl.ds((v % (steps // 2)) * group, group)
        else:
            mine = v - steps
            block = source_held[mine * TILE:(mine + 1) * TILE].reshape(group, cols)
            base_held[mine] = own + block.astype(F32)
            from_, to, at = base_held.at[mine], base, pl.ds(mine * group, group)
        outward.append(pltpu.make_async_copy(from_, to.at[at], out_sems.at[v]))
        outward[-1].start()
    for copy in outward:
        copy.wait()


def first_kernel(half, chol, ct, base, got_low, got_high, out, base_held, got_held, sems):
    rows, occ, _ = chol.shape
    width = ct.shape[0]
    copies = [
        pltpu.make_async_copy(base, base_held, sems.at[0]),
        pltpu.make_async_copy(got_low, got_held.at[0], sems.at[1]),
        pltpu.make_async_copy(got_high, got_held.at[1], sems.at[2]),
    ]
    for copy in copies:
        copy.start()
    start = pl.multiple_of(half[0] * width, width)
    total = dot(chol[:, :, pl.ds(start, width)].reshape(rows * occ, width), ct[...])
    for copy in copies:
        copy.wait()
    size = got_low.shape[0]
    for i in range(2):
        at = slice(i * size, (i + 1) * size)
        out[at] = total[at] + base_held[at] + got_held[i].astype(F32)


def last_kernel(half, chol, ct, first, out):
    rows, occ, _ = chol.shape
    width = ct.shape[0]
    start = pl.multiple_of(half[0] * width, width)
    total = dot(chol[:, :, pl.ds(start, width)].reshape(rows * occ, width), ct[...])
    out[...] = (total + first[...]).astype(BF16).reshape(out.shape)


def shards(
    amplitudes, source_block, ladder_integrals, cholesky_vectors, integral_tiles, amplitude_tiles
):
    rows, occ, columns = amplitudes.shape
    vectors = cholesky_vectors.shape[2]
    wide = vectors // 2
    steps = rows // TILE
    ny, nz, nx = lax.axis_size("y"), lax.axis_size("z"), lax.axis_size("x")
    core, x = lax.axis_index("c"), lax.axis_index("x")
    tile = lax.axis_index("y") * nz + lax.axis_index("z")
    vir = (x * 2 + core)[None]
    tile, x, mine, other = tile[None], x[None], core[None], 1 - core[None]

    row_half = rows // 2
    piece = shape((row_half, occ, columns), BF16)
    token = shape((8, 128), F32)

    def column(half, outs, spaces, micros, limit):
        return call(
            column_kernel,
            outs,
            [SMEM] * 3 + [ANY] * 3,
            micros,
            limit,
            [
                pltpu.VMEM((steps, TILE, occ, columns), BF16),
                pltpu.VMEM((steps, TILE, occ, wide), BF16),
                pltpu.SMEM(amplitude_tiles.shape, jnp.int32),
                pltpu.SemaphoreType.DMA((2, steps)),
                pltpu.SemaphoreType.DMA((steps,)),
                pltpu.SemaphoreType.DMA(()),
            ],
            spaces,
        )(vir, tile, half, amplitude_tiles, amplitudes, cholesky_vectors)

    sent, low, high = column(
        other, (shape((wide, columns), BF16), piece, piece), (VMEM, ANY, ANY), 3.0, FULL
    )
    got = lax.ppermute(sent, "c", SWAP)
    left_low = lax.ppermute(low, "x", shift(nx, 1))
    right_high = lax.ppermute(high, "x", shift(nx, -1))
    (kept,) = column(mine, (shape((wide, columns), F32),), (VMEM,), 2.0, 16)

    group = ny * nx
    chunk = wide // group
    added = call(add_kernel, shape((wide, columns), BF16), [VMEM] * 2, 0.7, 8)(kept, got)
    s1 = lax.all_to_all(added.reshape(group, chunk, columns), ("y", "x"), 0, 0, tiled=True)

    places = (0, nx - 1, 1, 2)
    w_mine, w_swap = call(
        functools.partial(w_kernel, places),
        (shape((rows, nx * rows), BF16),) * 2,
        [SMEM] * 4 + [VMEM, ANY],
        1.9,
        FULL,
    )(vir, x, mine, integral_tiles, ladder_integrals, added)
    w_other = lax.ppermute(w_swap, "c", SWAP)

    low, high, go_right, go_left, after_pieces = call(
        pieces_kernel,
        (piece,) * 4 + (token,),
        [ANY] * 4,
        1.5,
        FULL,
        [pltpu.VMEM((4,) + piece.shape, BF16), pltpu.SemaphoreType.DMA((2, 4))],
        (ANY,) * 4 + (VMEM,),
    )(amplitudes, left_low, right_high, w_swap)
    left_high = lax.ppermute(high, "x", shift(nx, 1))
    right_low = lax.ppermute(low, "x", shift(nx, -1))
    far_low = lax.ppermute(go_right, "x", shift(nx, 1))
    far_high = lax.ppermute(go_left, "x", shift(nx, -1))

    def summed(receivers, *parts):
        return call(
            sum_kernel,
            shape((receivers, chunk, columns), BF16),
            [VMEM] * len(parts),
            1.0,
            8,
        )(*parts)

    s2 = lax.all_to_all(summed(nz, s1, after_pieces), "z", 0, 0, tiled=True)
    mid = steps // 2
    near_ring = tuple(
        (v0, d, nx, steps) for v0, d in ((0, 0), (0, nx - 1), (mid, nx - 1), (0, 1), (mid, 1))
    )
    near_blocks = (amplitudes, left_low, left_high, right_low, right_high)
    near = 3 * rows
    laid, after_lay = call(
        functools.partial(lay_kernel, near_ring),
        (shape((occ, near, columns), BF16), token),
        [SMEM] * 4 + [ANY] * len(near_blocks),
        3.0,
        FULL,
        [
            pltpu.VMEM((near, occ, columns), BF16),
            pltpu.VMEM((occ, near, columns), BF16),
            pltpu.SemaphoreType.DMA((len(near_blocks),)),
            pltpu.SemaphoreType.DMA((len(near_blocks),)),
        ],
        (ANY, VMEM),
    )(x, tile, mine, amplitude_tiles, *near_blocks)

    third = summed(group, s2, after_lay)
    s3 = lax.all_to_all(third, ("y", "x"), 0, 0, tiled=True)

    half_out = shape((rows * occ // 2, columns), BF16)
    base, low_sent, high_sent, after_ladder = call(
        functools.partial(ladder_kernel, ((0, 2, nx, steps), (mid, 2, nx, steps))),
        (shape((rows * occ, columns), F32), half_out, half_out, token),
        [SMEM] * 4 + [ANY] * 7,
        5.0,
        56,
        [
            pltpu.VMEM((rows, occ, columns), BF16),
            pltpu.VMEM((occ, nx * rows, columns), BF16),
            pltpu.VMEM((2 * rows, nx * rows), BF16),
            pltpu.VMEM((rows, occ, columns), BF16),
            pltpu.VMEM((steps, TILE * occ, columns), F32),
            pltpu.VMEM((steps, TILE * occ, columns), BF16),
            pltpu.SemaphoreType.DMA((6,)),
            pltpu.SemaphoreType.DMA((2 * steps,)),
        ],
        (ANY, ANY, ANY, VMEM),
    )(
        x, tile, mine, amplitude_tiles, w_mine, w_other, laid, source_block, third, far_low,
        far_high,
    )
    low_got = lax.ppermute(low_sent, "c", SWAP)
    high_got = lax.ppermute(high_sent, "c", SWAP)
    ct_mine = call(pass_kernel, shape((wide, columns), BF16), [VMEM] * 2, 0.4, 8)(
        s3.reshape(wide, columns), after_ladder
    )
    ct_other = lax.ppermute(ct_mine, "c", SWAP)
    first = call(
        first_kernel,
        shape((rows * occ, columns), F32),
        [SMEM] + [VMEM] * 2 + [ANY] * 3,
        1.2,
        16,
        [
            pltpu.VMEM((rows * occ, columns), F32),
            pltpu.VMEM((2,) + half_out.shape, BF16),
            pltpu.SemaphoreType.DMA((3,)),
        ],
    )(mine, cholesky_vectors, ct_mine, base, low_got, high_got)
    return call(
        last_kernel, shape((rows, occ, columns), BF16), [SMEM] + [VMEM] * 3, 1.5, 16
    )(other, cholesky_vectors, ct_other, first)


def solution(mesh):
    split = Mesh(mesh.devices.reshape(4, 8, 4, 2), ("y", "z", "x", "c"))
    rows, cols = ("x", "c"), ("y", "z")
    return jax.shard_map(
        shards,
        mesh=split,
        in_specs=(
            P(rows, cols, None),
            P(rows, cols, None),
            P(rows, None),
            P(rows, cols, None),
            P(),
            P(),
        ),
        out_specs=P(rows, cols, None),
        check_vma=False,
    )
```

time: 111 us -> 75.4 us (0.68)
  blocking collectives: 31.2 us -> 0 us
  starting transfers between devices: 18.5 us -> 32.9 us
  waiting for transfers between devices: 17.9 us -> 6.84 us
  Pallas kernels: 34.9 us -> 31.2 us
  other arithmetic: 2.2 us -> 0 us
  local copies, waits for them, and re-layouts: 5.46 us -> 3.65 us
    all_to_all x2 -> x0, blocking collectives: 31.2 us -> none  [the longest x1 17.2 us: shards(): lax.all_to_all(jnp.broadcast_to(s2[None], (nz, chunk, columns)), 'z', 0,...]
    all_to_all x1 -> x3, waiting for transfers between devices: 17.9 us -> 0.53 us  [the longest x1 0.52 us: shards(): s2 = lax.all_to_all(summed(nz, s1, after_pieces), 'z', 0, 0, tiled=True)]
    all_to_all x1 -> x3, starting transfers between devices: 4.24 us -> 15.3 us  [the longest x1 7.49 us: shards(): s2 = lax.all_to_all(summed(nz, s1, after_pieces), 'z', 0, 0, tiled=True)]
    ppermute x6 -> x9, waiting for transfers between devices: 0.02 us -> 6.31 us  [the longest x1 4.99 us: shards(): left_low = lax.ppermute(low, 'x', shift(nx, 1))]
    pallas_call x9 -> x12, Pallas kernels: 34.9 us -> 31.2 us  [the longest x1 8.55 us: shards(): call(functools.partial(ladder_kernel, ((0, 2, nx, steps), (mid, 2, nx, st...]
    ppermute x6 -> x9, starting transfers between devices: 12.5 us -> 14.6 us  [the longest x1 3.31 us: shards(): got = lax.ppermute(sent, 'c', SWAP)]
    unnamed x18 -> x16, local copies, waits for them, and re-layouts: 5.4 us -> 3.65 us
    reduce_sum x2 -> x0, other arithmetic: 1.16 us -> none  [the longest x1 1.12 us: shards(): s2 = s.astype(F32).sum(0).astype(BF16)]
  transfers between devices with their start and end apart: 9 -> 14, of which waited for: 1 -> 4; matrix products, arithmetic and copies ran while one was open for 2% -> 0% of each run, Pallas kernels for 25% -> 35%
where the time goes in v4:
time: 75.4 us; the launch traced here: 74.7 us
  starting transfers between devices  32.9 us (44%)
  Pallas kernels  31.2 us (41%)
  waiting for transfers between devices  6.84 us (9%)
  local copies, waits for them, and re-layouts  3.65 us (5%)
    pallas_call x1, Pallas kernels, shards(): call(functools.partial(ladder_kernel, ((0, 2, nx, steps), (mid, 2, nx, st...  8.55 us
    all_to_all x1, starting transfers between devices, shards(): s2 = lax.all_to_all(summed(nz, s1, after_pieces), 'z', 0, 0, tiled=True)  7.49 us
    pallas_call x2, Pallas kernels, column(): call(column_kernel, outs, [SMEM] * 3 + [ANY] * 3, micros, limit, [pltpu.V...  5.43 us
    pallas_call x1, Pallas kernels, shards(): call(functools.partial(lay_kernel, near_ring), (shape((occ, near, columns...  5.33 us
    ppermute x1, waiting for transfers between devices, shards(): left_low = lax.ppermute(low, 'x', shift(nx, 1))  4.99 us
    all_to_all x1, starting transfers between devices, shards(): s3 = lax.all_to_all(third, ('y', 'x'), 0, 0, tiled=True)  3.95 us
    all_to_all x1, starting transfers between devices, shards(): lax.all_to_all(added.reshape(group, chunk, columns), ('y', 'x'), 0, 0, ti...  3.82 us
    unnamed x16, local copies, waits for them, and re-layouts  3.65 us
  transfers between devices with their start and end apart: 14, of which 4 were waited for; matrix products, arithmetic and copies ran while one was open for 0% of the time, Pallas kernels for 35%

profile of v4, /device:TPU:1, one launch (start us, length us, event | category | flops | bytes accessed | tf_op | source)
XLA Modules:
  0.0 74.7 jit_solution(12593470212172400026)
XLA Ops:
  0.0 0.0 copy-start.3
  0.0 0.0 copy-start
  0.0 0.0 copy-start.1
  0.0 3.5 %shard_map.65 = (bf16[512,512]{1,0:T(8,128)(2,1)}, bf16[128,4,512]{2,1,0:T(4,128)(2,1)}, bf16[128,4,512]{2,1,0:T(4,128)(2,1)}) custom-call(s32[1]{0:T(128)} %bitcast.1.vir, s32[1]{0:T(128)} %bitcast.2.tile, s32[1]{0:T(128)S(6)} %sub.3.half, s32[32,128]{1,0:T(8,128)} %mask.3, bf16[256,4,512]{2,1,0:T(4,128)(2,1)} %refs_0_.1, bf16[256,4,1024]{2,1,0:T(4,128)(2,1)} %chol.7), custom_call_target="tpu_custom_call" | custom-call | bytes 10200000 | tf_op jit(solution)/shard_map/pallas_call | solution.py:297
  3.6 3.3 %collective-permute-start = (bf16[512,512]{1,0:T(8,128)(2,1)}, bf16[512,512]{1,0:T(8,128)(2,1)S(1)}, u32[]{:S(2)}, u32[]{:S(2)}) collective-permute-start(bf16[512,512]{1,0:T(8,128)(2,1)} %get-tuple-element.21), channel_id=1, source_target_pairs={{0,1},{1,0},{2,3},{3,2},{4,5},{5,4},{6,7},{7,6},{8,9},{9,8},{10,11... | collective-permute-start | bytes 1572872 | tf_op jit(solution)/shard_map/ppermute | solution.py:317
  6.9 0.0 collective-permute-start.1
  6.9 2.7 %collective-permute-start.2 = (bf16[128,4,512]{2,1,0:T(4,128)(2,1)}, bf16[128,4,512]{2,1,0:T(4,128)(2,1)}, u32[]{:S(2)}, u32[]{:S(2)}) collective-permute-start(bf16[128,4,512]{2,1,0:T(4,128)(2,1)} %get-tuple-element.23), channel_id=1, source_target_pairs={{0,6},{2,0},{4,2},{6,4},{1,7},{3,1},{5,3},{7,5},{8,14},{10,8},{12,... | collective-permute-start | bytes 1572872 | tf_op jit(solution)/shard_map/ppermute | solution.py:319
  9.6 0.0 copy-done.3
  9.6 0.0 copy-done
  9.6 0.0 copy-done.1
  9.6 1.9 %shard_map.64.kept = f32[512,512]{1,0:T(8,128)S(1)} custom-call(s32[1]{0:T(128)} %bitcast.1.vir, s32[1]{0:T(128)} %bitcast.2.tile, s32[1]{0:T(128)} %bitcast.half.core, s32[32,128]{1,0:T(8,128)S(1)} %copy-done.3, bf16[256,4,512]{2,1,0:T(4,128)(2,1)S(1)} %copy-done.1, bf16[256,4,1024]{2,1,0:T(4,128)(2,1)S(1)} %copy-done), custom_call_target="tpu_custom_call" | custom-call | bytes 6800000 | tf_op jit(solution)/shard_map/pallas_call | solution.py:297
  11.5 0.0 collective-permute-done.got
  11.5 0.9 %shard_map.66.after = bf16[512,512]{1,0:T(8,128)(2,1)} custom-call(f32[512,512]{1,0:T(8,128)S(1)} %shard_map.64.kept, bf16[512,512]{1,0:T(8,128)(2,1)S(1)} %collective-permute-done.got), custom_call_target="tpu_custom_call" | custom-call | bytes 2380000 | tf_op jit(solution)/shard_map/pallas_call | solution.py:324
  12.4 3.8 %all-to-all-start = ((bf16[16,32,512]{2,1,0:T(8,128)(2,1)}), bf16[16,32,512]{2,1,0:T(8,128)(2,1)S(1)}, u32[]{:S(2)}, u32[]{:S(2)}) async-start(bf16[16,32,512]{2,1,0:T(8,128)(2,1)} %bitcast.3), calls=%async_computation | async-start | bytes 1048576 | tf_op jit(solution)/shard_map/all_to_all | solution.py:325
  16.2 2.6 %shard_map.67 = (bf16[256,1024]{1,0:T(8,128)(2,1)}, bf16[256,1024]{1,0:T(8,128)(2,1)}) custom-call(s32[1]{0:T(128)} %bitcast.1.vir, s32[1]{0:T(128)} %bitcast.4.x, s32[1]{0:T(128)} %bitcast.half.core, s32[32,32]{1,0:T(8,128)} %tiles.5, bf16[256,2048]{1,0:T(8,128)(2,1)} %w.1, bf16[512,512]{1,0:T(8,128)(2,1)} %shard_map.66.after), custom_call_target="tpu_custom_call" | custom-call | bytes 6460000 | tf_op jit(solution)/shard_map/pallas_call | solution.py:328
  18.8 0.0 copy-start.7
  18.8 5.0 %collective-permute-done.1.left.refs_1_ = bf16[128,4,512]{2,1,0:T(4,128)(2,1)} collective-permute-done((bf16[128,4,512]{2,1,0:T(4,128)(2,1)}, bf16[128,4,512]{2,1,0:T(4,128)(2,1)}, u32[]{:S(2)}, u32[]{:S(2)}) %collective-permute-start.1) | collective-permute-done | bytes 524320 | tf_op jit(solution)/shard_map/ppermute | solution.py:318
  23.7 0.0 collective-permute-done.2.right.refs_4_
  23.7 3.0 %shard_map.68 = (bf16[128,4,512]{2,1,0:T(4,128)(2,1)}, bf16[128,4,512]{2,1,0:T(4,128)(2,1)}, bf16[128,4,512]{2,1,0:T(4,128)(2,1)}, bf16[128,4,512]{2,1,0:T(4,128)(2,1)}, f32[8,128]{1,0:T(8,128)}) custom-call(bf16[256,4,512]{2,1,0:T(4,128)(2,1)} %refs_0_.1, bf16[128,4,512]{2,1,0:T(4,128)(2,1)} %collective-permute-done.1.left.refs_1_, ...), custom_call_target="tpu_custom_call" | custom-call | bytes 5100000 | tf_op jit(solution)/shard_map/pallas_call | solution.py:337
  26.8 0.1 collective-permute-start.3
  26.9 2.7 %collective-permute-start.4 = (bf16[128,4,512]{2,1,0:T(4,128)(2,1)}, bf16[128,4,512]{2,1,0:T(4,128)(2,1)}, u32[]{:S(2)}, u32[]{:S(2)}) collective-permute-start(bf16[128,4,512]{2,1,0:T(4,128)(2,1)} %get-tuple-element.27), channel_id=1, source_target_pairs={{0,6},{2,0},{4,2},{6,4},{1,7},{3,1},{5,3},{7,5},{8,14},{10,8},{12,... | collective-permute-start | bytes 1572872 | tf_op jit(solution)/shard_map/ppermute | solution.py:347
  29.6 0.0 all-to-all-done.parts
  29.6 0.0 copy-start.5
  29.6 0.7 copy-done.5
  30.3 0.8 %shard_map.69 = bf16[8,32,512]{2,1,0:T(8,128)(2,1)} custom-call(bf16[16,32,512]{2,1,0:T(8,128)(2,1)S(1)} %all-to-all-done.parts, f32[8,128]{1,0:T(8,128)S(1)} %copy-done.5), custom_call_target="tpu_custom_call" | custom-call | bytes 3400000 | tf_op jit(solution)/shard_map/pallas_call | solution.py:352
  31.0 7.5 %all-to-all-start.1 = ((bf16[8,32,512]{2,1,0:T(8,128)(2,1)}), bf16[8,32,512]{2,1,0:T(8,128)(2,1)S(1)}, u32[]{:S(2)}, u32[]{:S(2)}) async-start(bf16[8,32,512]{2,1,0:T(8,128)(2,1)} %shard_map.69), calls=%async_computation.1 | async-start | bytes 524288 | tf_op jit(solution)/shard_map/all_to_all | solution.py:360
  38.5 0.0 copy-done.7
  38.5 1.6 %collective-permute-start.5 = (bf16[256,1024]{1,0:T(8,128)(2,1)S(1)}, bf16[256,1024]{1,0:T(8,128)(2,1)}, u32[]{:S(2)}, u32[]{:S(2)}) collective-permute-start(bf16[256,1024]{1,0:T(8,128)(2,1)S(1)} %copy-done.7), channel_id=1, source_target_pairs={{0,1},{1,0},{2,3},{3,2},{4,5},{5,4},{6,7},{7,6},{8,9},{9,8},{10,11... | collective-permute-start | bytes 1572872 | tf_op jit(solution)/shard_map/ppermute | solution.py:335
  40.1 0.8 %collective-permute-start.6 = (bf16[128,4,512]{2,1,0:T(4,128)(2,1)}, bf16[128,4,512]{2,1,0:T(4,128)(2,1)}, u32[]{:S(2)}, u32[]{:S(2)}) collective-permute-start(bf16[128,4,512]{2,1,0:T(4,128)(2,1)} %get-tuple-element.31), channel_id=1, source_target_pairs={{0,2},{2,4},{4,6},{6,0},{1,3},{3,5},{5,7},{7,1},{8,10},{10,12},{12... | collective-permute-start | bytes 1572872 | tf_op jit(solution)/shard_map/ppermute | solution.py:348
  40.9 1.9 %collective-permute-start.7 = (bf16[128,4,512]{2,1,0:T(4,128)(2,1)}, bf16[128,4,512]{2,1,0:T(4,128)(2,1)}, u32[]{:S(2)}, u32[]{:S(2)}) collective-permute-start(bf16[128,4,512]{2,1,0:T(4,128)(2,1)} %get-tuple-element.32), channel_id=1, source_target_pairs={{0,6},{2,0},{4,2},{6,4},{1,7},{3,1},{5,3},{7,5},{8,14},{10,8},{12,... | collective-permute-start | bytes 1572872 | tf_op jit(solution)/shard_map/ppermute | solution.py:349
  42.8 0.0 collective-permute-done.3.refs_2_
  42.8 0.0 collective-permute-done.4.refs_3_
  42.8 5.3 %shard_map.70 = (bf16[4,768,512]{2,1,0:T(8,128)(2,1)}, f32[8,128]{1,0:T(8,128)}) custom-call(s32[1]{0:T(128)} %bitcast.4.x, s32[1]{0:T(128)} %bitcast.2.tile, s32[1]{0:T(128)} %bitcast.half.core, s32[32,128]{1,0:T(8,128)} %mask.3, bf16[256,4,512]{2,1,0:T(4,128)(2,1)} %refs_0_.1, bf16[128,4,512]{2,1,0:T(4,128)(2,1)} %collective-permute-done.1.left.refs_1_, ...), custom_call_target="tpu_custom_call" | custom-call | bytes 10200000 | tf_op jit(solution)/shard_map/pallas_call | solution.py:367
  48.2 0.5 all-to-all-done.1.parts
  48.7 0.0 copy-start.6
  48.7 0.7 copy-done.6
  49.4 0.9 %shard_map.71.after = bf16[16,32,512]{2,1,0:T(8,128)(2,1)} custom-call(bf16[8,32,512]{2,1,0:T(8,128)(2,1)S(1)} %all-to-all-done.1.parts, f32[8,128]{1,0:T(8,128)S(1)} %copy-done.6), custom_call_target="tpu_custom_call" | custom-call | bytes 3400000 | tf_op jit(solution)/shard_map/pallas_call | solution.py:352
  50.2 4.0 %all-to-all-start.2 = ((bf16[16,32,512]{2,1,0:T(8,128)(2,1)}), bf16[16,32,512]{2,1,0:T(8,128)(2,1)S(1)}, u32[]{:S(2)}, u32[]{:S(2)}) async-start(bf16[16,32,512]{2,1,0:T(8,128)(2,1)} %shard_map.71.after), calls=%async_computation.2 | async-start | bytes 1048576 | tf_op jit(solution)/shard_map/all_to_all | solution.py:383
  54.2 0.0 collective-permute-done.5.w_other
  54.2 0.9 %collective-permute-done.6.refs_0_ = bf16[128,4,512]{2,1,0:T(4,128)(2,1)} collective-permute-done((bf16[128,4,512]{2,1,0:T(4,128)(2,1)}, bf16[128,4,512]{2,1,0:T(4,128)(2,1)}, u32[]{:S(2)}, u32[]{:S(2)}) %collective-permute-start.6) | collective-permute-done | bytes 524320 | tf_op jit(solution)/shard_map/ppermute | solution.py:348
  55.1 0.0 collective-permute-done.7.refs_1_
  55.1 8.6 %shard_map.72 = (f32[1024,512]{1,0:T(8,128)}, bf16[512,512]{1,0:T(8,128)(2,1)}, bf16[512,512]{1,0:T(8,128)(2,1)}, f32[8,128]{1,0:T(8,128)}) custom-call(s32[1]{0:T(128)} %bitcast.4.x, s32[1]{0:T(128)} %bitcast.2.tile, s32[1]{0:T(128)} %bitcast.half.core, s32[32,128]{1,0:T(8,128)} %mask.3, bf16[256,1024]{1,0:T(8,128)(2,1)} %get-tuple-element.29.w_mine, ...), custom_call_target="tpu_custom_call" | custom-call | bytes 17000000 | tf_op jit(solution)/shard_map/pallas_call | solution.py:386
  63.7 3.0 %collective-permute-start.9 = (bf16[512,512]{1,0:T(8,128)(2,1)}, bf16[512,512]{1,0:T(8,128)(2,1)S(1)}, u32[]{:S(2)}, u32[]{:S(2)}) collective-permute-start(bf16[512,512]{1,0:T(8,128)(2,1)} %get-tuple-element.35), channel_id=1, source_target_pairs={{0,1},{1,0},{2,3},{3,2},{4,5},{5,4},{6,7},{7,6},{8,9},{9,8},{10,11... | collective-permute-start | bytes 1572872 | tf_op jit(solution)/shard_map/ppermute | solution.py:407
  66.7 0.1 collective-permute-start.10
  66.8 0.0 all-to-all-done.2
  66.8 0.0 copy-start.4
  66.8 0.7 copy-done.4
  67.5 1.4 %collective-permute-start.8 = (bf16[512,512]{1,0:T(8,128)(2,1)S(1)}, bf16[512,512]{1,0:T(8,128)(2,1)S(1)}, u32[]{:S(2)}, u32[]{:S(2)}) collective-permute-start(bf16[512,512]{1,0:T(8,128)(2,1)S(1)} %shard_map.73.ct), channel_id=1, source_target_pairs={{0,1},{1,0},{2,3},{3,2},{4,5},{5,4},{6,7},{7,6},{8,9},{9,8},{10,11... | collective-permute-start | bytes 1572872 | tf_op jit(solution)/shard_map/ppermute | solution.py:412
  69.0 0.0 collective-permute-done.9.got_low
  69.0 0.4 collective-permute-done.10.got_high
  69.3 0.0 copy-start.2
  69.3 1.6 %copy-done.2 = f32[1024,512]{1,0:T(8,128)S(1)} copy-done((f32[1024,512]{1,0:T(8,128)S(1)}, f32[1024,512]{1,0:T(8,128)}, u32[]{:S(2)}) %copy-start.2) | copy-done | bytes 2097176
  70.9 2.1 %shard_map.74.first = f32[1024,512]{1,0:T(8,128)S(1)} custom-call(s32[1]{0:T(128)} %bitcast.half.core, bf16[256,4,1024]{2,1,0:T(4,128)(2,1)S(1)} %copy-done, bf16[512,512]{1,0:T(8,128)(2,1)S(1)} %shard_map.73.ct, f32[1024,512]{1,0:T(8,128)S(1)} %copy-done.2, bf16[512,512]{1,0:T(8,128)(2,1)S(1)} %collective-permute-done.9.got_low, ...), custom_call_target="tpu_custom_call" | custom-call | bytes 4080000 | tf_op jit(solution)/shard_map/pallas_call | solution.py:413
  73.0 0.0 collective-permute-done.8.ct
  73.0 1.7 %shard_map.75 = bf16[256,4,512]{2,1,0:T(4,128)(2,1)} custom-call(s32[1]{0:T(128)S(6)} %sub.3.half, bf16[256,4,1024]{2,1,0:T(4,128)(2,1)S(1)} %copy-done, bf16[512,512]{1,0:T(8,128)(2,1)S(1)} %collective-permute-done.8.ct, f32[1024,512]{1,0:T(8,128)S(1)} %shard_map.74.first), custom_call_target="tpu_custom_call" | custom-call | bytes 5100000 | tf_op jit(solution)/shard_map/pallas_call | solution.py:425
  (1 shorter events, 0.0 us)
Async XLA Ops:
  0.0 9.6 %copy-start.3 = (s32[32,128]{1,0:T(8,128)S(1)}, s32[32,128]{1,0:T(8,128)}, u32[]{:S(2)}) copy-start(s32[32,128]{1,0:T(8,128)} %mask.3) | copy-start | bytes 49156
  0.0 9.6 %copy-start = (bf16[256,4,1024]{2,1,0:T(4,128)(2,1)S(1)}, bf16[256,4,1024]{2,1,0:T(4,128)(2,1)}, u32[]{:S(2)}) copy-start(bf16[256,4,1024]{2,1,0:T(4,128)(2,1)} %chol.7) | copy-start | bytes 6291460
  0.0 9.6 %copy-start.1 = (bf16[256,4,512]{2,1,0:T(4,128)(2,1)S(1)}, bf16[256,4,512]{2,1,0:T(4,128)(2,1)}, u32[]{:S(2)}) copy-start(bf16[256,4,512]{2,1,0:T(4,128)(2,1)} %refs_0_.1) | copy-start | bytes 3145732
  3.6 7.9 %collective-permute-start = (bf16[512,512]{1,0:T(8,128)(2,1)}, bf16[512,512]{1,0:T(8,128)(2,1)S(1)}, u32[]{:S(2)}, u32[]{:S(2)}) collective-permute-start(bf16[512,512]{1,0:T(8,128)(2,1)} %get-tuple-element.21), channel_id=1, source_target_pairs={{0,1},{1,0},{2,3},{3,2},{4,5},{5,4},{6,7},{7,6},{8,9},{9,8},{10,11... | collective-permute-start | bytes 1572872 | tf_op jit(solution)/shard_map/ppermute | solution.py:317
  6.9 16.9 %collective-permute-start.1 = (bf16[128,4,512]{2,1,0:T(4,128)(2,1)}, bf16[128,4,512]{2,1,0:T(4,128)(2,1)}, u32[]{:S(2)}, u32[]{:S(2)}) collective-permute-start(bf16[128,4,512]{2,1,0:T(4,128)(2,1)} %get-tuple-element.22), channel_id=1, source_target_pairs={{0,2},{2,4},{4,6},{6,0},{1,3},{3,5},{5,7},{7,1},{8,10},{10,12},{12... | collective-permute-start | bytes 1572872 | tf_op jit(solution)/shard_map/ppermute | solution.py:318
  6.9 16.9 %collective-permute-start.2 = (bf16[128,4,512]{2,1,0:T(4,128)(2,1)}, bf16[128,4,512]{2,1,0:T(4,128)(2,1)}, u32[]{:S(2)}, u32[]{:S(2)}) collective-permute-start(bf16[128,4,512]{2,1,0:T(4,128)(2,1)} %get-tuple-element.23), channel_id=1, source_target_pairs={{0,6},{2,0},{4,2},{6,4},{1,7},{3,1},{5,3},{7,5},{8,14},{10,8},{12,... | collective-permute-start | bytes 1572872 | tf_op jit(solution)/shard_map/ppermute | solution.py:319
  12.4 17.2 %all-to-all-start = ((bf16[16,32,512]{2,1,0:T(8,128)(2,1)}), bf16[16,32,512]{2,1,0:T(8,128)(2,1)S(1)}, u32[]{:S(2)}, u32[]{:S(2)}) async-start(bf16[16,32,512]{2,1,0:T(8,128)(2,1)} %bitcast.3), calls=%async_computation | async-start | bytes 1048576 | tf_op jit(solution)/shard_map/all_to_all | solution.py:325
  18.8 19.8 %copy-start.7 = (bf16[256,1024]{1,0:T(8,128)(2,1)S(1)}, bf16[256,1024]{1,0:T(8,128)(2,1)}, u32[]{:S(2)}) copy-start(bf16[256,1024]{1,0:T(8,128)(2,1)} %get-tuple-element.24.after) | copy-start | bytes 1572868
  26.8 16.0 %collective-permute-start.3 = (bf16[128,4,512]{2,1,0:T(4,128)(2,1)}, bf16[128,4,512]{2,1,0:T(4,128)(2,1)}, u32[]{:S(2)}, u32[]{:S(2)}) collective-permute-start(bf16[128,4,512]{2,1,0:T(4,128)(2,1)} %get-tuple-element.26), channel_id=1, source_target_pairs={{0,2},{2,4},{4,6},{6,0},{1,3},{3,5},{5,7},{7,1},{8,10},{10,12},{12... | collective-permute-start | bytes 1572872 | tf_op jit(solution)/shard_map/ppermute | solution.py:346
  26.9 15.9 %collective-permute-start.4 = (bf16[128,4,512]{2,1,0:T(4,128)(2,1)}, bf16[128,4,512]{2,1,0:T(4,128)(2,1)}, u32[]{:S(2)}, u32[]{:S(2)}) collective-permute-start(bf16[128,4,512]{2,1,0:T(4,128)(2,1)} %get-tuple-element.27), channel_id=1, source_target_pairs={{0,6},{2,0},{4,2},{6,4},{1,7},{3,1},{5,3},{7,5},{8,14},{10,8},{12,... | collective-permute-start | bytes 1572872 | tf_op jit(solution)/shard_map/ppermute | solution.py:347
  29.6 0.7 copy-start.5
  31.0 17.6 %all-to-all-start.1 = ((bf16[8,32,512]{2,1,0:T(8,128)(2,1)}), bf16[8,32,512]{2,1,0:T(8,128)(2,1)S(1)}, u32[]{:S(2)}, u32[]{:S(2)}) async-start(bf16[8,32,512]{2,1,0:T(8,128)(2,1)} %shard_map.69), calls=%async_computation.1 | async-start | bytes 524288 | tf_op jit(solution)/shard_map/all_to_all | solution.py:360
  38.5 15.7 %collective-permute-start.5 = (bf16[256,1024]{1,0:T(8,128)(2,1)S(1)}, bf16[256,1024]{1,0:T(8,128)(2,1)}, u32[]{:S(2)}, u32[]{:S(2)}) collective-permute-start(bf16[256,1024]{1,0:T(8,128)(2,1)S(1)} %copy-done.7), channel_id=1, source_target_pairs={{0,1},{1,0},{2,3},{3,2},{4,5},{5,4},{6,7},{7,6},{8,9},{9,8},{10,11... | collective-permute-start | bytes 1572872 | tf_op jit(solution)/shard_map/ppermute | solution.py:335
  40.1 15.0 %collective-permute-start.6 = (bf16[128,4,512]{2,1,0:T(4,128)(2,1)}, bf16[128,4,512]{2,1,0:T(4,128)(2,1)}, u32[]{:S(2)}, u32[]{:S(2)}) collective-permute-start(bf16[128,4,512]{2,1,0:T(4,128)(2,1)} %get-tuple-element.31), channel_id=1, source_target_pairs={{0,2},{2,4},{4,6},{6,0},{1,3},{3,5},{5,7},{7,1},{8,10},{10,12},{12... | collective-permute-start | bytes 1572872 | tf_op jit(solution)/shard_map/ppermute | solution.py:348
  40.9 14.3 %collective-permute-start.7 = (bf16[128,4,512]{2,1,0:T(4,128)(2,1)}, bf16[128,4,512]{2,1,0:T(4,128)(2,1)}, u32[]{:S(2)}, u32[]{:S(2)}) collective-permute-start(bf16[128,4,512]{2,1,0:T(4,128)(2,1)} %get-tuple-element.32), channel_id=1, source_target_pairs={{0,6},{2,0},{4,2},{6,4},{1,7},{3,1},{5,3},{7,5},{8,14},{10,8},{12,... | collective-permute-start | bytes 1572872 | tf_op jit(solution)/shard_map/ppermute | solution.py:349
  48.7 0.7 copy-start.6
  50.2 16.6 %all-to-all-start.2 = ((bf16[16,32,512]{2,1,0:T(8,128)(2,1)}), bf16[16,32,512]{2,1,0:T(8,128)(2,1)S(1)}, u32[]{:S(2)}, u32[]{:S(2)}) async-start(bf16[16,32,512]{2,1,0:T(8,128)(2,1)} %shard_map.71.after), calls=%async_computation.2 | async-start | bytes 1048576 | tf_op jit(solution)/shard_map/all_to_all | solution.py:383
  63.7 5.3 %collective-permute-start.9 = (bf16[512,512]{1,0:T(8,128)(2,1)}, bf16[512,512]{1,0:T(8,128)(2,1)S(1)}, u32[]{:S(2)}, u32[]{:S(2)}) collective-permute-start(bf16[512,512]{1,0:T(8,128)(2,1)} %get-tuple-element.35), channel_id=1, source_target_pairs={{0,1},{1,0},{2,3},{3,2},{4,5},{5,4},{6,7},{7,6},{8,9},{9,8},{10,11... | collective-permute-start | bytes 1572872 | tf_op jit(solution)/shard_map/ppermute | solution.py:407
  66.7 2.6 %collective-permute-start.10 = (bf16[512,512]{1,0:T(8,128)(2,1)}, bf16[512,512]{1,0:T(8,128)(2,1)}, u32[]{:S(2)}, u32[]{:S(2)}) collective-permute-start(bf16[512,512]{1,0:T(8,128)(2,1)} %get-tuple-element.36), channel_id=1, source_target_pairs={{0,1},{1,0},{2,3},{3,2},{4,5},{5,4},{6,7},{7,6},{8,9},{9,8},{10,11... | collective-permute-start | bytes 1572872 | tf_op jit(solution)/shard_map/ppermute | solution.py:408
  66.8 0.7 copy-start.4
  67.5 5.5 %collective-permute-start.8 = (bf16[512,512]{1,0:T(8,128)(2,1)S(1)}, bf16[512,512]{1,0:T(8,128)(2,1)S(1)}, u32[]{:S(2)}, u32[]{:S(2)}) collective-permute-start(bf16[512,512]{1,0:T(8,128)(2,1)S(1)} %shard_map.73.ct), channel_id=1, source_target_pairs={{0,1},{1,0},{2,3},{3,2},{4,5},{5,4},{6,7},{7,6},{8,9},{9,8},{10,11... | collective-permute-start | bytes 1572872 | tf_op jit(solution)/shard_map/ppermute | solution.py:412
  69.3 1.6 %copy-start.2 = (f32[1024,512]{1,0:T(8,128)S(1)}, f32[1024,512]{1,0:T(8,128)}, u32[]{:S(2)}) copy-start(f32[1024,512]{1,0:T(8,128)} %get-tuple-element.34.base) | copy-start | bytes 6291460

commit v5 on v4

v5 whole, which is shorter than its diff:
```python
import functools

import jax
import jax.numpy as jnp
from jax import lax
from jax.experimental import pallas as pl
from jax.experimental.pallas import tpu as pltpu
from jax.sharding import Mesh, PartitionSpec as P

TILE = 64
FULL = 58
SWAP = [(0, 1), (1, 0)]
F32, BF16 = jnp.float32, jnp.bfloat16
VMEM = pl.BlockSpec(memory_space=pltpu.VMEM)
SMEM = pl.BlockSpec(memory_space=pltpu.SMEM)
ANY = pl.BlockSpec(memory_space=pl.ANY)
shape = jax.ShapeDtypeStruct


def shift(n, d):
    return [(i, (i + d) % n) for i in range(n)]


def call(kernel, outs, specs, micros, limit, scratch=(), spaces=None, grid=()):
    return pl.pallas_call(
        kernel,
        out_shape=outs,
        grid=grid,
        in_specs=specs,
        out_specs=spaces or jax.tree.map(lambda _: VMEM, outs),
        scratch_shapes=scratch,
        compiler_params=pltpu.CompilerParams(vmem_limit_bytes=limit * 2**20),
        cost_estimate=pl.CostEstimate(
            flops=0, bytes_accessed=int(micros * 3.4e6), transcendentals=0
        ),
    )


def dot(a, b, over=1):
    return lax.dot_general(a, b, (((over,), (0,)), ((), ())), preferred_element_type=F32)


def permutation(n, occ):
    row = lax.broadcasted_iota(jnp.int32, (n, n), 0)
    col = lax.broadcasted_iota(jnp.int32, (n, n), 1)
    per = n // occ
    return jnp.where(col == (row % per) * occ + row // per, 1.0, 0.0).astype(BF16)


def column_kernel(vir, tile, half, tiles, t, chol, *refs):
    out, pieces = refs[0], refs[1:-7]
    t_buf, chol_buf, laid, mask, sems, piece_sems, mask_sem = refs[-7:]
    rows, occ, cols = t.shape
    width = out.shape[0]
    steps = rows // TILE
    start = pl.multiple_of(half[0] * width, width)
    mask_copy = pltpu.make_async_copy(tiles, mask, mask_sem)
    mask_copy.start()
    copies = []
    for v in range(steps):
        at = pl.ds(v * TILE, TILE)
        copies.append((
            pltpu.make_async_copy(t.at[at], t_buf.at[v], sems.at[0, v]),
            pltpu.make_async_copy(
                chol.at[at, :, pl.ds(start, width)], chol_buf.at[v], sems.at[1, v]
            ),
        ))
    for pair in copies:
        for copy in pair:
            copy.start()
    k_id = lax.broadcasted_iota(jnp.int32, (occ, cols), 0)
    perm = permutation(TILE * occ, occ)
    total = None
    outgoing = []
    mask_copy.wait()
    for v in range(steps):
        keep = jnp.zeros((occ, cols), F32)
        for k in range(occ):
            kept = mask[vir[0] * steps + v, tile[0] * occ + k]
            keep = jnp.where(k_id == k, kept.astype(F32), keep)
        for copy in copies[v]:
            copy.wait()
        masked = (t_buf[v] * keep.astype(BF16)[None]).reshape(TILE * occ, cols)
        if pieces:
            moved = dot(perm, masked).astype(BF16)
            which, place = divmod(v, steps // 2)
            for k in range(occ):
                laid[which, k, place * TILE:(place + 1) * TILE] = moved[k * TILE:(k + 1) * TILE]
            if place == steps // 2 - 1:
                outgoing.append(
                    pltpu.make_async_copy(laid.at[which], pieces[which], piece_sems.at[which])
                )
                outgoing[-1].start()
        term = dot(chol_buf[v].reshape(TILE * occ, width), masked, 0)
        total = term if total is None else total + term
    out[...] = total.astype(out.dtype)
    for copy in outgoing:
        copy.wait()


def add_kernel(kept, got, out):
    out[...] = (kept[...] + got[...].astype(F32)).astype(BF16)


def w_kernel(places, vir, x, core, tiles, w, after, mine, other):
    rows = w.shape[0]
    steps = rows // TILE
    ring = len(places)
    lane = lax.broadcasted_iota(jnp.int32, (TILE, 2 * TILE), 1)
    for i, d in enumerate(places):
        for out, which in ((mine, core[0]), (other, 1 - core[0])):
            block = ((x[0] + d) % ring) * 2 + which
            for j in range(rows // (2 * TILE)):
                at = pl.ds(pl.multiple_of(block * rows + j * 2 * TILE, 2 * TILE), 2 * TILE)
                col = block * steps + 2 * j
                for v in range(steps):
                    row = vir[0] * steps + v
                    keep = jnp.where(
                        lane < TILE, tiles[row, col].astype(F32), tiles[row, col + 1].astype(F32)
                    )
                    here = slice(v * TILE, (v + 1) * TILE)
                    to = slice(i * rows + j * 2 * TILE, i * rows + (j + 1) * 2 * TILE)
                    out[here, to] = w[here, at] * keep.astype(BF16)


def pieces_kernel(low, high, left, right, after, to_right, to_left, held, sems):
    pairs = (
        (high, to_right.at[0]), (low, to_left.at[0]), (left, to_right.at[1]), (right, to_left.at[1])
    )
    inward = [
        pltpu.make_async_copy(source, held.at[i], sems.at[0, i])
        for i, (source, _) in enumerate(pairs)
    ]
    outward = [
        pltpu.make_async_copy(held.at[i], out, sems.at[1, i]) for i, (_, out) in enumerate(pairs)
    ]
    for copy in inward:
        copy.start()
    for copy, then in zip(inward, outward):
        copy.wait()
        then.start()
    for copy in outward:
        copy.wait()


def sum_kernel(parts, *refs):
    out = refs[-1]
    total = parts[0].astype(F32)
    for i in range(1, parts.shape[0]):
        total = total + parts[i].astype(F32)
    total = total.astype(BF16)
    for i in range(out.shape[0]):
        out[i] = total


def ladder_kernel(
    w_mine, w_other, source, low, high, left_low, right_high, from_left, from_right, after,
    base, low_sent, high_sent, right, w_held, source_held, base_held, sent_held, in_sems, out_sems,
):
    rows, occ, cols = source.shape
    pieces = (
        low, high, left_low, from_left.at[0], from_right.at[0], right_high, from_left.at[1],
        from_right.at[1],
    )
    steps = rows // TILE
    group = TILE * occ
    size = pieces[0].shape[1]
    w_copies = [
        pltpu.make_async_copy(w_other, w_held.at[pl.ds(0, rows)], in_sems.at[len(pieces), 0]),
        pltpu.make_async_copy(w_mine, w_held.at[pl.ds(rows, rows)], in_sems.at[len(pieces), 1]),
    ]
    source_copy = pltpu.make_async_copy(source, source_held, in_sems.at[len(pieces), 2])
    copies = [
        [
            pltpu.make_async_copy(
                piece.at[k], right.at[k, pl.ds(i * size, size)], in_sems.at[i, k]
            )
            for i, piece in enumerate(pieces)
        ]
        for k in range(occ)
    ]
    for copy in w_copies + sum(copies, []) + [source_copy]:
        copy.start()
    back = permutation(group, occ)
    for copy in w_copies:
        copy.wait()
    w = w_held[...]
    sums = []
    for k in range(occ):
        for copy in copies[k]:
            copy.wait()
        sums.append(dot(w, right[k]).astype(BF16))
    source_copy.wait()
    outward = []
    for v in range(2 * steps):
        here = slice(v * TILE, (v + 1) * TILE)
        own = dot(back, jnp.concatenate([part[here] for part in sums], 0), 0)
        if v < steps:
            sent_held[v] = own.astype(BF16)
            from_, to = sent_held.at[v], (low_sent, high_sent)[v * 2 // steps]
            at = pl.ds((v % (steps // 2)) * group, group)
        else:
            mine = v - steps
            block = source_held[mine * TILE:(mine + 1) * TILE].reshape(group, cols)
            base_held[mine] = (own + block.astype(F32)).astype(BF16)
            from_, to, at = base_held.at[mine], base, pl.ds(mine * group, group)
        outward.append(pltpu.make_async_copy(from_, to.at[at], out_sems.at[v]))
        outward[-1].start()
    for copy in outward:
        copy.wait()


def first_kernel(half, chol, ct, base, out):
    rows, occ, _ = chol.shape
    width = ct.shape[0]
    start = pl.multiple_of(half[0] * width, width)
    total = dot(chol[:, :, pl.ds(start, width)].reshape(rows * occ, width), ct[...])
    out[...] = total + base[...].astype(F32)


def last_kernel(half, chol, ct, first, got_low, got_high, out):
    rows, occ, _ = chol.shape
    width = ct.shape[0]
    start = pl.multiple_of(half[0] * width, width)
    total = dot(chol[:, :, pl.ds(start, width)].reshape(rows * occ, width), ct[...])
    size = got_low.shape[0]
    for i, got in enumerate((got_low, got_high)):
        at = slice(i * size, (i + 1) * size)
        part = total[at] + (first[at] + got[...].astype(F32))
        here = slice(i * rows // 2, (i + 1) * rows // 2)
        out[here] = part.astype(BF16).reshape(rows // 2, occ, out.shape[2])


def shards(
    amplitudes, source_block, ladder_integrals, cholesky_vectors, integral_tiles, amplitude_tiles
):
    rows, occ, columns = amplitudes.shape
    vectors = cholesky_vectors.shape[2]
    wide = vectors // 2
    steps = rows // TILE
    ny, nz, nx = lax.axis_size("y"), lax.axis_size("z"), lax.axis_size("x")
    core, x = lax.axis_index("c"), lax.axis_index("x")
    tile = lax.axis_index("y") * nz + lax.axis_index("z")
    vir = (x * 2 + core)[None]
    tile, x, mine, other = tile[None], x[None], core[None], 1 - core[None]

    row_half = rows // 2
    piece = shape((occ, row_half, columns), BF16)

    def column(half, outs, spaces, micros, limit):
        return call(
            column_kernel,
            outs,
            [SMEM] * 3 + [ANY] * 3,
            micros,
            limit,
            [
                pltpu.VMEM((steps, TILE, occ, columns), BF16),
                pltpu.VMEM((steps, TILE, occ, wide), BF16),
                pltpu.VMEM((2,) + piece.shape, BF16),
                pltpu.SMEM(amplitude_tiles.shape, jnp.int32),
                pltpu.SemaphoreType.DMA((2, steps)),
                pltpu.SemaphoreType.DMA((2,)),
                pltpu.SemaphoreType.DMA(()),
            ],
            spaces,
        )(vir, tile, half, amplitude_tiles, amplitudes, cholesky_vectors)

    sent, low, high = column(
        other, (shape((wide, columns), BF16), piece, piece), (VMEM, ANY, ANY), 3.0, FULL
    )
    got = lax.ppermute(sent, "c", SWAP)
    left_low = lax.ppermute(low, "x", shift(nx, 1))
    right_high = lax.ppermute(high, "x", shift(nx, -1))
    (kept,) = column(mine, (shape((wide, columns), F32),), (VMEM,), 2.0, 16)

    group = ny * nx
    chunk = wide // group
    added = call(add_kernel, shape((wide, columns), BF16), [VMEM] * 2, 0.7, 8)(kept, got)
    plane = [[(i + group // 2 + nx // 2) % group for i in range(group)]]
    line = [[(i + nz // 2) % nz for i in range(nz)]]

    def exchange(parts, axes, members):
        return lax.all_to_all(parts, axes, 0, 0, axis_index_groups=members, tiled=True)

    s1 = exchange(added.reshape(group, chunk, columns), ("y", "x"), plane)

    places = (0, nx - 1, 1, 2)
    w_mine, w_swap = call(
        functools.partial(w_kernel, places),
        (shape((rows, nx * rows), BF16),) * 2,
        [SMEM] * 4 + [VMEM, ANY],
        1.9,
        FULL,
    )(vir, x, mine, integral_tiles, ladder_integrals, added)
    w_other = lax.ppermute(w_swap, "c", SWAP)

    pair = shape((2,) + piece.shape, BF16)
    to_right, to_left = call(
        pieces_kernel,
        (pair, pair),
        [ANY] * 5,
        1.5,
        FULL,
        [pltpu.VMEM((4,) + piece.shape, BF16), pltpu.SemaphoreType.DMA((2, 4))],
        (ANY,) * 2,
    )(low, high, left_low, right_high, w_swap)
    from_left = lax.ppermute(to_right, "x", shift(nx, 1))
    from_right = lax.ppermute(to_left, "x", shift(nx, -1))

    def summed(receivers, *parts):
        return call(
            sum_kernel,
            shape((receivers, chunk, columns), BF16),
            [VMEM] * len(parts),
            1.0,
            8,
        )(*parts)

    s2 = exchange(summed(nz, s1), "z", line)
    third = summed(group, s2)
    s3 = exchange(third, ("y", "x"), plane)

    half_out = shape((rows * occ // 2, columns), BF16)
    base, low_sent, high_sent = call(
        ladder_kernel,
        (shape((rows * occ, columns), BF16), half_out, half_out),
        [ANY] * 10,
        5.0,
        FULL,
        [
            pltpu.VMEM((occ, nx * rows, columns), BF16),
            pltpu.VMEM((2 * rows, nx * rows), BF16),
            pltpu.VMEM((rows, occ, columns), BF16),
            pltpu.VMEM((steps, TILE * occ, columns), BF16),
            pltpu.VMEM((steps, TILE * occ, columns), BF16),
            pltpu.SemaphoreType.DMA((9, occ)),
            pltpu.SemaphoreType.DMA((2 * steps,)),
        ],
        (ANY, ANY, ANY),
    )(
        w_mine, w_other, source_block, low, high, left_low, right_high, from_left, from_right, third
    )
    low_got = lax.ppermute(low_sent, "c", SWAP)
    high_got = lax.ppermute(high_sent, "c", SWAP)
    ct_mine = s3.reshape(wide, columns)
    ct_other = lax.ppermute(ct_mine, "c", SWAP)
    first = call(
        first_kernel, shape((rows * occ, columns), F32), [SMEM] + [VMEM] * 3, 0.9, 12
    )(mine, cholesky_vectors, ct_mine, base)
    return call(
        last_kernel, shape((rows, occ, columns), BF16), [SMEM] + [VMEM] * 5, 2.0, 16
    )(other, cholesky_vectors, ct_other, first, low_got, high_got)


def solution(mesh):
    split = Mesh(mesh.devices.reshape(4, 8, 4, 2), ("y", "z", "x", "c"))
    rows, cols = ("x", "c"), ("y", "z")
    return jax.shard_map(
        shards,
        mesh=split,
        in_specs=(
            P(rows, cols, None),
            P(rows, cols, None),
            P(rows, None),
            P(rows, cols, None),
            P(),
            P(),
        ),
        out_specs=P(rows, cols, None),
        check_vma=False,
    )
```

time: 75.4 us -> 69.4 us (0.920)
  Pallas kernels: 31.2 us -> 23.2 us
  starting transfers between devices: 32.9 us -> 36.9 us
  local copies, waits for them, and re-layouts: 3.65 us -> 1.24 us
    pallas_call x6 -> x4, Pallas kernels: 20.7 us -> 12.2 us  [the longest x1 6.32 us: shards(): call(ladder_kernel, (shape((rows * occ, columns), BF16), half_out, half_o...]
    all_to_all x3, starting transfers between devices: 15.3 us -> 23.5 us  [exchange(): lax.all_to_all(parts, axes, 0, 0, axis_index_groups=members, tiled=True)]
    all_to_all x3, waiting for transfers between devices: 0.53 us -> 4.4 us  [exchange(): lax.all_to_all(parts, axes, 0, 0, axis_index_groups=members, tiled=True)]
    ppermute x1, waiting for transfers between devices: 4.99 us -> 1.99 us  [shards(): left_low = lax.ppermute(low, 'x', shift(nx, 1))]
    ppermute x4 -> x2, starting transfers between devices: 5.46 us -> 2.97 us  [the longest x1 2.88 us: shards(): from_right = lax.ppermute(to_left, 'x', shift(nx, -1))]
    unnamed x16 -> x10, local copies, waits for them, and re-layouts: 3.65 us -> 1.24 us
    ppermute x1, starting transfers between devices: 1.43 us -> 0.41 us  [shards(): ct_other = lax.ppermute(ct_mine, 'c', SWAP)]
    ppermute x4 -> x2, waiting for transfers between devices: 0.95 us -> 0.01 us  [the longest x1 0.01 us: shards(): from_right = lax.ppermute(to_left, 'x', shift(nx, -1))]
  transfers between devices with their start and end apart: 14 -> 12, of which waited for: 4 -> 3; matrix products, arithmetic and copies ran while one was open for 0% -> 0% of each run, Pallas kernels for 35% -> 24%
where the time goes in v5:
time: 69.4 us; the launch traced here: 68.8 us
  starting transfers between devices  36.9 us (53%)
  Pallas kernels  23.2 us (33%)
  waiting for transfers between devices  7.33 us (11%)
  local copies, waits for them, and re-layouts  1.24 us (2%)
    all_to_all x3, starting transfers between devices, exchange(): lax.all_to_all(parts, axes, 0, 0, axis_index_groups=members, tiled=True)  23.5 us
    pallas_call x1, Pallas kernels, shards(): call(ladder_kernel, (shape((rows * occ, columns), BF16), half_out, half_o...  6.32 us
    pallas_call x2, Pallas kernels, column(): call(column_kernel, outs, [SMEM] * 3 + [ANY] * 3, micros, limit, [pltpu.V...  5.94 us
    all_to_all x3, waiting for transfers between devices, exchange(): lax.all_to_all(parts, axes, 0, 0, axis_index_groups=members, tiled=True)  4.4 us
    ppermute x1, starting transfers between devices, shards(): got = lax.ppermute(sent, 'c', SWAP)  3.31 us
    ppermute x1, starting transfers between devices, shards(): from_right = lax.ppermute(to_left, 'x', shift(nx, -1))  2.88 us
    pallas_call x1, Pallas kernels, shards(): call(last_kernel, shape((rows, occ, columns), BF16), [SMEM] + [VMEM] * 5,...  2.75 us
    ppermute x1, starting transfers between devices, shards(): right_high = lax.ppermute(high, 'x', shift(nx, -1))  2.69 us
  transfers between devices with their start and end apart: 12, of which 3 were waited for; matrix products, arithmetic and copies ran while one was open for 0% of the time, Pallas kernels for 24%

profile of v5, /device:TPU:1, one launch (start us, length us, event | category | flops | bytes accessed | tf_op | source)
XLA Modules:
  0.0 68.8 jit_solution(5397355954083845274)
XLA Ops:
  0.0 0.0 copy-start.3
  0.0 0.0 copy-start.1
  0.0 0.0 copy-start
  0.0 4.1 %shard_map.65 = (bf16[512,512]{1,0:T(8,128)(2,1)}, bf16[4,128,512]{2,1,0:T(8,128)(2,1)}, bf16[4,128,512]{2,1,0:T(8,128)(2,1)}) custom-call(s32[1]{0:T(128)} %bitcast.1.vir, s32[1]{0:T(128)} %bitcast.2.tile, s32[1]{0:T(128)S(6)} %sub.3.half, s32[32,128]{1,0:T(8,128)} %tiles.4, bf16[256,4,512]{2,1,0:T(4,128)(2,1)} %t.3, bf16[256,4,1024]{2,1,0:T(4,128)(2,1)} %chol.7), custom_call_target="tpu_custom_call" | custom-call | bytes 10200000 | tf_op jit(solution)/shard_map/pallas_call | solution.py:251
  4.1 3.3 %collective-permute-start = (bf16[512,512]{1,0:T(8,128)(2,1)}, bf16[512,512]{1,0:T(8,128)(2,1)S(1)}, u32[]{:S(2)}, u32[]{:S(2)}) collective-permute-start(bf16[512,512]{1,0:T(8,128)(2,1)} %get-tuple-element.15), channel_id=1, source_target_pairs={{0,1},{1,0},{2,3},{3,2},{4,5},{5,4},{6,7},{7,6},{8,9},{9,8},{10,11... | collective-permute-start | bytes 1572872 | tf_op jit(solution)/shard_map/ppermute | solution.py:272
  7.4 0.0 collective-permute-start.3
  7.4 2.7 %collective-permute-start.4 = (bf16[4,128,512]{2,1,0:T(8,128)(2,1)}, bf16[4,128,512]{2,1,0:T(8,128)(2,1)}, u32[]{:S(2)}, u32[]{:S(2)}) collective-permute-start(bf16[4,128,512]{2,1,0:T(8,128)(2,1)} %get-tuple-element.19.high), channel_id=1, source_target_pairs={{0,6},{2,0},{4,2},{6,4},{1,7},{3,1},{5,3},{7,5},{8,14},{10,8},{12,... | collective-permute-start | bytes 1572872 | tf_op jit(solution)/shard_map/ppermute | solution.py:274
  10.1 0.0 copy-done.3
  10.1 0.0 copy-done.1
  10.1 0.0 copy-done
  10.1 1.9 %shard_map.64.kept = f32[512,512]{1,0:T(8,128)S(1)} custom-call(s32[1]{0:T(128)} %bitcast.1.vir, s32[1]{0:T(128)} %bitcast.2.tile, s32[1]{0:T(128)} %bitcast.half.core, s32[32,128]{1,0:T(8,128)S(1)} %copy-done.3, bf16[256,4,512]{2,1,0:T(4,128)(2,1)S(1)} %copy-done.1, bf16[256,4,1024]{2,1,0:T(4,128)(2,1)S(1)} %copy-done), custom_call_target="tpu_custom_call" | custom-call | bytes 6800000 | tf_op jit(solution)/shard_map/pallas_call | solution.py:251
  12.0 0.0 collective-permute-done.got
  12.0 0.9 %shard_map.66.after = bf16[512,512]{1,0:T(8,128)(2,1)} custom-call(f32[512,512]{1,0:T(8,128)S(1)} %shard_map.64.kept, bf16[512,512]{1,0:T(8,128)(2,1)S(1)} %collective-permute-done.got), custom_call_target="tpu_custom_call" | custom-call | bytes 2380000 | tf_op jit(solution)/shard_map/pallas_call | solution.py:279
  12.9 6.7 %all-to-all-start = ((bf16[16,32,512]{2,1,0:T(8,128)(2,1)}), bf16[16,32,512]{2,1,0:T(8,128)(2,1)S(1)}, u32[]{:S(2)}, u32[]{:S(2)}) async-start(bf16[16,32,512]{2,1,0:T(8,128)(2,1)} %bitcast.3), calls=%async_computation | async-start | bytes 1048576 | tf_op jit(solution)/shard_map/all_to_all | solution.py:284
  19.5 2.5 %shard_map.69 = (bf16[256,1024]{1,0:T(8,128)(2,1)}, bf16[256,1024]{1,0:T(8,128)(2,1)}) custom-call(s32[1]{0:T(128)} %bitcast.1.vir, s32[1]{0:T(128)} %bitcast.5.x, s32[1]{0:T(128)} %bitcast.half.core, s32[32,32]{1,0:T(8,128)} %tiles.5, bf16[256,2048]{1,0:T(8,128)(2,1)} %w.1, bf16[512,512]{1,0:T(8,128)(2,1)} %shard_map.66.after), custom_call_target="tpu_custom_call" | custom-call | bytes 6460000 | tf_op jit(solution)/shard_map/pallas_call | solution.py:289
  22.1 0.0 copy-start.4
  22.1 2.0 %collective-permute-done.3.left.left_low = bf16[4,128,512]{2,1,0:T(8,128)(2,1)} collective-permute-done((bf16[4,128,512]{2,1,0:T(8,128)(2,1)}, bf16[4,128,512]{2,1,0:T(8,128)(2,1)}, u32[]{:S(2)}, u32[]{:S(2)}) %collective-permute-start.3) | collective-permute-done | bytes 524320 | tf_op jit(solution)/shard_map/ppermute | solution.py:273
  24.1 0.0 collective-permute-done.4.right.right_high
  24.1 2.4 %shard_map.70 = (bf16[2,4,128,512]{3,2,1,0:T(8,128)(2,1)}, bf16[2,4,128,512]{3,2,1,0:T(8,128)(2,1)}) custom-call(bf16[4,128,512]{2,1,0:T(8,128)(2,1)} %get-tuple-element.18.low, bf16[4,128,512]{2,1,0:T(8,128)(2,1)} %get-tuple-element.19.high, bf16[4,128,512]{2,1,0:T(8,128)(2,1)} %collective-permute-done.3.left.left_low, ...), custom_call_target="tpu_custom_call" | custom-call | bytes 5100000 | tf_op jit(solution)/shard_map/pallas_call | solution.py:299
  26.5 0.1 collective-permute-start.5
  26.6 2.9 %collective-permute-start.6 = (bf16[2,4,128,512]{3,2,1,0:T(8,128)(2,1)}, bf16[2,4,128,512]{3,2,1,0:T(8,128)(2,1)}, u32[]{:S(2)}, u32[]{:S(2)}) collective-permute-start(bf16[2,4,128,512]{3,2,1,0:T(8,128)(2,1)} %get-tuple-element.21), channel_id=1, source_target_pairs={{0,6},{2,0},{4,2},{6,4},{1,7},{3,1},{5,3},{7,5},{8,14},{10,8},{12,... | collective-permute-start | bytes 3145736 | tf_op jit(solution)/shard_map/ppermute | solution.py:309
  29.5 0.0 all-to-all-done.parts
  29.5 0.8 %shard_map.67 = bf16[8,32,512]{2,1,0:T(8,128)(2,1)} custom-call(bf16[16,32,512]{2,1,0:T(8,128)(2,1)S(1)} %all-to-all-done.parts), custom_call_target="tpu_custom_call" | custom-call | bytes 3400000 | tf_op jit(solution)/shard_map/pallas_call | solution.py:312
  30.3 10.2 %all-to-all-start.1 = ((bf16[8,32,512]{2,1,0:T(8,128)(2,1)}), bf16[8,32,512]{2,1,0:T(8,128)(2,1)S(1)}, u32[]{:S(2)}, u32[]{:S(2)}) async-start(bf16[8,32,512]{2,1,0:T(8,128)(2,1)} %shard_map.67), calls=%async_computation.1 | async-start | bytes 524288 | tf_op jit(solution)/shard_map/all_to_all | solution.py:284
  40.4 0.0 copy-done.4
  40.4 1.5 %collective-permute-start.2 = (bf16[256,1024]{1,0:T(8,128)(2,1)S(1)}, bf16[256,1024]{1,0:T(8,128)(2,1)}, u32[]{:S(2)}, u32[]{:S(2)}) collective-permute-start(bf16[256,1024]{1,0:T(8,128)(2,1)S(1)} %copy-done.4), channel_id=1, source_target_pairs={{0,1},{1,0},{2,3},{3,2},{4,5},{5,4},{6,7},{7,6},{8,9},{9,8},{10,11... | collective-permute-start | bytes 1572872 | tf_op jit(solution)/shard_map/ppermute | solution.py:296
  42.0 4.4 %all-to-all-done.1.parts = bf16[8,32,512]{2,1,0:T(8,128)(2,1)S(1)} async-done(((bf16[8,32,512]{2,1,0:T(8,128)(2,1)}), bf16[8,32,512]{2,1,0:T(8,128)(2,1)S(1)}, u32[]{:S(2)}, u32[]{:S(2)}) %all-to-all-start.1) | async-done | bytes 262176 | tf_op jit(solution)/shard_map/all_to_all | solution.py:284
  46.4 0.9 %shard_map.68.after = bf16[16,32,512]{2,1,0:T(8,128)(2,1)} custom-call(bf16[8,32,512]{2,1,0:T(8,128)(2,1)S(1)} %all-to-all-done.1.parts), custom_call_target="tpu_custom_call" | custom-call | bytes 3400000 | tf_op jit(solution)/shard_map/pallas_call | solution.py:312
  47.3 6.7 %all-to-all-start.2 = ((bf16[16,32,512]{2,1,0:T(8,128)(2,1)}), bf16[16,32,512]{2,1,0:T(8,128)(2,1)S(1)}, u32[]{:S(2)}, u32[]{:S(2)}) async-start(bf16[16,32,512]{2,1,0:T(8,128)(2,1)} %shard_map.68.after), calls=%async_computation.2 | async-start | bytes 1048576 | tf_op jit(solution)/shard_map/all_to_all | solution.py:284
  53.9 0.0 collective-permute-done.2.w_other
  53.9 0.0 collective-permute-done.5.from_left
  53.9 0.0 collective-permute-done.6.from_right
  53.9 6.3 %shard_map.71 = (bf16[1024,512]{1,0:T(8,128)(2,1)}, bf16[512,512]{1,0:T(8,128)(2,1)}, bf16[512,512]{1,0:T(8,128)(2,1)}) custom-call(bf16[256,1024]{1,0:T(8,128)(2,1)} %get-tuple-element.16.w_mine, bf16[256,1024]{1,0:T(8,128)(2,1)} %collective-permute-done.2.w_other, bf16[256,4,512]{2,1,0:T(4,128)(2,1)} %source.1, ...), custom_call_target="tpu_custom_call" | custom-call | bytes 17000000 | tf_op jit(solution)/shard_map/pallas_call | solution.py:325
  60.3 2.4 %collective-permute-start.7 = (bf16[512,512]{1,0:T(8,128)(2,1)}, bf16[512,512]{1,0:T(8,128)(2,1)S(1)}, u32[]{:S(2)}, u32[]{:S(2)}) collective-permute-start(bf16[512,512]{1,0:T(8,128)(2,1)} %get-tuple-element.23), channel_id=1, source_target_pairs={{0,1},{1,0},{2,3},{3,2},{4,5},{5,4},{6,7},{7,6},{8,9},{9,8},{10,11... | collective-permute-start | bytes 1572872 | tf_op jit(solution)/shard_map/ppermute | solution.py:344
  62.7 0.1 collective-permute-start.8
  62.8 0.0 all-to-all-done.2
  62.8 0.4 collective-permute-start.1
  63.2 0.0 copy-start.2
  63.2 1.2 %copy-done.2 = bf16[1024,512]{1,0:T(8,128)(2,1)S(1)} copy-done((bf16[1024,512]{1,0:T(8,128)(2,1)S(1)}, bf16[1024,512]{1,0:T(8,128)(2,1)}, u32[]{:S(2)}) %copy-start.2) | copy-done | bytes 1048600
  64.4 0.7 %shard_map.72.first = f32[1024,512]{1,0:T(8,128)S(1)} custom-call(s32[1]{0:T(128)} %bitcast.half.core, bf16[256,4,1024]{2,1,0:T(4,128)(2,1)S(1)} %copy-done, bf16[512,512]{1,0:T(8,128)(2,1)S(1)} %bitcast.7, bf16[1024,512]{1,0:T(8,128)(2,1)S(1)} %copy-done.2), custom_call_target="tpu_custom_call" | custom-call | bytes 3060000 | tf_op jit(solution)/shard_map/pallas_call | solution.py:348
  65.2 0.0 collective-permute-done.7.got_low
  65.2 0.9 %collective-permute-done.8.got_high = bf16[512,512]{1,0:T(8,128)(2,1)} collective-permute-done((bf16[512,512]{1,0:T(8,128)(2,1)}, bf16[512,512]{1,0:T(8,128)(2,1)}, u32[]{:S(2)}, u32[]{:S(2)}) %collective-permute-start.8) | collective-permute-done | bytes 524320 | tf_op jit(solution)/shard_map/ppermute | solution.py:345
  66.1 0.0 collective-permute-done.1.ct
  66.1 2.7 %shard_map.73 = bf16[256,4,512]{2,1,0:T(4,128)(2,1)} custom-call(s32[1]{0:T(128)S(6)} %sub.3.half, bf16[256,4,1024]{2,1,0:T(4,128)(2,1)S(1)} %copy-done, bf16[512,512]{1,0:T(8,128)(2,1)S(1)} %collective-permute-done.1.ct, f32[1024,512]{1,0:T(8,128)S(1)} %shard_map.72.first, bf16[512,512]{1,0:T(8,128)(2,1)S(1)} %collective-permute-done.7.got_low, ...), custom_call_target="tpu_custom_call" | custom-call | bytes 6800000 | tf_op jit(solution)/shard_map/pallas_call | solution.py:351
Async XLA Ops:
  0.0 10.1 %copy-start.3 = (s32[32,128]{1,0:T(8,128)S(1)}, s32[32,128]{1,0:T(8,128)}, u32[]{:S(2)}) copy-start(s32[32,128]{1,0:T(8,128)} %tiles.4) | copy-start | bytes 49156
  0.0 10.1 %copy-start.1 = (bf16[256,4,512]{2,1,0:T(4,128)(2,1)S(1)}, bf16[256,4,512]{2,1,0:T(4,128)(2,1)}, u32[]{:S(2)}) copy-start(bf16[256,4,512]{2,1,0:T(4,128)(2,1)} %t.3) | copy-start | bytes 3145732
  0.0 10.1 %copy-start = (bf16[256,4,1024]{2,1,0:T(4,128)(2,1)S(1)}, bf16[256,4,1024]{2,1,0:T(4,128)(2,1)}, u32[]{:S(2)}) copy-start(bf16[256,4,1024]{2,1,0:T(4,128)(2,1)} %chol.7) | copy-start | bytes 6291460
  4.1 7.9 %collective-permute-start = (bf16[512,512]{1,0:T(8,128)(2,1)}, bf16[512,512]{1,0:T(8,128)(2,1)S(1)}, u32[]{:S(2)}, u32[]{:S(2)}) collective-permute-start(bf16[512,512]{1,0:T(8,128)(2,1)} %get-tuple-element.15), channel_id=1, source_target_pairs={{0,1},{1,0},{2,3},{3,2},{4,5},{5,4},{6,7},{7,6},{8,9},{9,8},{10,11... | collective-permute-start | bytes 1572872 | tf_op jit(solution)/shard_map/ppermute | solution.py:272
  7.4 16.7 %collective-permute-start.3 = (bf16[4,128,512]{2,1,0:T(8,128)(2,1)}, bf16[4,128,512]{2,1,0:T(8,128)(2,1)}, u32[]{:S(2)}, u32[]{:S(2)}) collective-permute-start(bf16[4,128,512]{2,1,0:T(8,128)(2,1)} %get-tuple-element.18.low), channel_id=1, source_target_pairs={{0,2},{2,4},{4,6},{6,0},{1,3},{3,5},{5,7},{7,1},{8,10},{10,12},{12... | collective-permute-start | bytes 1572872 | tf_op jit(solution)/shard_map/ppermute | solution.py:273
  7.4 16.7 %collective-permute-start.4 = (bf16[4,128,512]{2,1,0:T(8,128)(2,1)}, bf16[4,128,512]{2,1,0:T(8,128)(2,1)}, u32[]{:S(2)}, u32[]{:S(2)}) collective-permute-start(bf16[4,128,512]{2,1,0:T(8,128)(2,1)} %get-tuple-element.19.high), channel_id=1, source_target_pairs={{0,6},{2,0},{4,2},{6,4},{1,7},{3,1},{5,3},{7,5},{8,14},{10,8},{12,... | collective-permute-start | bytes 1572872 | tf_op jit(solution)/shard_map/ppermute | solution.py:274
  12.9 16.6 %all-to-all-start = ((bf16[16,32,512]{2,1,0:T(8,128)(2,1)}), bf16[16,32,512]{2,1,0:T(8,128)(2,1)S(1)}, u32[]{:S(2)}, u32[]{:S(2)}) async-start(bf16[16,32,512]{2,1,0:T(8,128)(2,1)} %bitcast.3), calls=%async_computation | async-start | bytes 1048576 | tf_op jit(solution)/shard_map/all_to_all | solution.py:284
  22.1 18.3 %copy-start.4 = (bf16[256,1024]{1,0:T(8,128)(2,1)S(1)}, bf16[256,1024]{1,0:T(8,128)(2,1)}, u32[]{:S(2)}) copy-start(bf16[256,1024]{1,0:T(8,128)(2,1)} %get-tuple-element.17.after) | copy-start | bytes 1572868
  26.5 27.4 %collective-permute-start.5 = (bf16[2,4,128,512]{3,2,1,0:T(8,128)(2,1)}, bf16[2,4,128,512]{3,2,1,0:T(8,128)(2,1)}, u32[]{:S(2)}, u32[]{:S(2)}) collective-permute-start(bf16[2,4,128,512]{3,2,1,0:T(8,128)(2,1)} %get-tuple-element.20), channel_id=1, source_target_pairs={{0,2},{2,4},{4,6},{6,0},{1,3},{3,5},{5,7},{7,1},{8,10},{10,12},{12... | collective-permute-start | bytes 3145736 | tf_op jit(solution)/shard_map/ppermute | solution.py:308
  26.6 27.3 %collective-permute-start.6 = (bf16[2,4,128,512]{3,2,1,0:T(8,128)(2,1)}, bf16[2,4,128,512]{3,2,1,0:T(8,128)(2,1)}, u32[]{:S(2)}, u32[]{:S(2)}) collective-permute-start(bf16[2,4,128,512]{3,2,1,0:T(8,128)(2,1)} %get-tuple-element.21), channel_id=1, source_target_pairs={{0,6},{2,0},{4,2},{6,4},{1,7},{3,1},{5,3},{7,5},{8,14},{10,8},{12,... | collective-permute-start | bytes 3145736 | tf_op jit(solution)/shard_map/ppermute | solution.py:309
  30.3 16.1 %all-to-all-start.1 = ((bf16[8,32,512]{2,1,0:T(8,128)(2,1)}), bf16[8,32,512]{2,1,0:T(8,128)(2,1)S(1)}, u32[]{:S(2)}, u32[]{:S(2)}) async-start(bf16[8,32,512]{2,1,0:T(8,128)(2,1)} %shard_map.67), calls=%async_computation.1 | async-start | bytes 524288 | tf_op jit(solution)/shard_map/all_to_all | solution.py:284
  40.4 13.5 %collective-permute-start.2 = (bf16[256,1024]{1,0:T(8,128)(2,1)S(1)}, bf16[256,1024]{1,0:T(8,128)(2,1)}, u32[]{:S(2)}, u32[]{:S(2)}) collective-permute-start(bf16[256,1024]{1,0:T(8,128)(2,1)S(1)} %copy-done.4), channel_id=1, source_target_pairs={{0,1},{1,0},{2,3},{3,2},{4,5},{5,4},{6,7},{7,6},{8,9},{9,8},{10,11... | collective-permute-start | bytes 1572872 | tf_op jit(solution)/shard_map/ppermute | solution.py:296
  47.3 15.6 %all-to-all-start.2 = ((bf16[16,32,512]{2,1,0:T(8,128)(2,1)}), bf16[16,32,512]{2,1,0:T(8,128)(2,1)S(1)}, u32[]{:S(2)}, u32[]{:S(2)}) async-start(bf16[16,32,512]{2,1,0:T(8,128)(2,1)} %shard_map.68.after), calls=%async_computation.2 | async-start | bytes 1048576 | tf_op jit(solution)/shard_map/all_to_all | solution.py:284
  60.3 4.9 %collective-permute-start.7 = (bf16[512,512]{1,0:T(8,128)(2,1)}, bf16[512,512]{1,0:T(8,128)(2,1)S(1)}, u32[]{:S(2)}, u32[]{:S(2)}) collective-permute-start(bf16[512,512]{1,0:T(8,128)(2,1)} %get-tuple-element.23), channel_id=1, source_target_pairs={{0,1},{1,0},{2,3},{3,2},{4,5},{5,4},{6,7},{7,6},{8,9},{9,8},{10,11... | collective-permute-start | bytes 1572872 | tf_op jit(solution)/shard_map/ppermute | solution.py:344
  62.7 3.4 %collective-permute-start.8 = (bf16[512,512]{1,0:T(8,128)(2,1)}, bf16[512,512]{1,0:T(8,128)(2,1)}, u32[]{:S(2)}, u32[]{:S(2)}) collective-permute-start(bf16[512,512]{1,0:T(8,128)(2,1)} %get-tuple-element.24), channel_id=1, source_target_pairs={{0,1},{1,0},{2,3},{3,2},{4,5},{5,4},{6,7},{7,6},{8,9},{9,8},{10,11... | collective-permute-start | bytes 1572872 | tf_op jit(solution)/shard_map/ppermute | solution.py:345
  62.8 3.3 %collective-permute-start.1 = (bf16[512,512]{1,0:T(8,128)(2,1)S(1)}, bf16[512,512]{1,0:T(8,128)(2,1)S(1)}, u32[]{:S(2)}, u32[]{:S(2)}) collective-permute-start(bf16[512,512]{1,0:T(8,128)(2,1)S(1)} %bitcast.6), channel_id=1, source_target_pairs={{0,1},{1,0},{2,3},{3,2},{4,5},{5,4},{6,7},{7,6},{8,9},{9,8},{10,11... | collective-permute-start | bytes 1572872 | tf_op jit(solution)/shard_map/ppermute | solution.py:347
  63.2 1.2 %copy-start.2 = (bf16[1024,512]{1,0:T(8,128)(2,1)S(1)}, bf16[1024,512]{1,0:T(8,128)(2,1)}, u32[]{:S(2)}) copy-start(bf16[1024,512]{1,0:T(8,128)(2,1)} %get-tuple-element.22.base) | copy-start | bytes 3145732

commit v6 on v5

--- a/solution.py
+++ b/solution.py
@@ -47,30 +47,29 @@
     return jnp.where(col == (row % per) * occ + row // per, 1.0, 0.0).astype(BF16)
 
 
-def column_kernel(vir, tile, half, tiles, t, chol, *refs):
-    out, pieces = refs[0], refs[1:-7]
-    t_buf, chol_buf, laid, mask, sems, piece_sems, mask_sem = refs[-7:]
+def column_kernel(vir, tile, half, tiles, t, chol, out, *refs):
+    pieces = refs[:-10]
+    t_buf, masked, chol_buf, out_buf, laid, mask, t_sems, sems, piece_sems, mask_sem = refs[-10:]
     rows, occ, cols = t.shape
-    width = out.shape[0]
+    parts, width = out_buf.shape[:2]
     steps = rows // TILE
-    start = pl.multiple_of(half[0] * width, width)
+    group = TILE * occ
+    start = pl.multiple_of(half[0] * parts * width, parts * width)
     mask_copy = pltpu.make_async_copy(tiles, mask, mask_sem)
-    mask_copy.start()
-    copies = []
-    for v in range(steps):
-        at = pl.ds(v * TILE, TILE)
-        copies.append((
-            pltpu.make_async_copy(t.at[at], t_buf.at[v], sems.at[0, v]),
-            pltpu.make_async_copy(
-                chol.at[at, :, pl.ds(start, width)], chol_buf.at[v], sems.at[1, v]
-            ),
-        ))
-    for pair in copies:
-        for copy in pair:
-            copy.start()
+    t_copies = [
+        pltpu.make_async_copy(t.at[pl.ds(v * TILE, TILE)], t_buf.at[v], t_sems.at[v])
+        for v in range(steps)
+    ]
+    chol_copies = [
+        pltpu.make_async_copy(
+            chol.at[:, :, pl.ds(start + i * width, width)], chol_buf.at[i], sems.at[0, i]
+        )
+        for i in range(parts)
+    ]
+    for copy in [mask_copy] + t_copies + chol_copies:
+        copy.start()
     k_id = lax.broadcasted_iota(jnp.int32, (occ, cols), 0)
-    perm = permutation(TILE * occ, occ)
-    total = None
+    perm = permutation(group, occ)
     outgoing = []
     mask_copy.wait()
     for v in range(steps):
@@ -78,11 +77,11 @@
         for k in range(occ):
             kept = mask[vir[0] * steps + v, tile[0] * occ + k]
             keep = jnp.where(k_id == k, kept.astype(F32), keep)
-        for copy in copies[v]:
-            copy.wait()
-        masked = (t_buf[v] * keep.astype(BF16)[None]).reshape(TILE * occ, cols)
+        t_copies[v].wait()
+        here = (t_buf[v] * keep.astype(BF16)[None]).reshape(group, cols)
+        masked[v * group:(v + 1) * group] = here
         if pieces:
-            moved = dot(perm, masked).astype(BF16)
+            moved = dot(perm, here).astype(BF16)
             which, place = divmod(v, steps // 2)
             for k in range(occ):
                 laid[which, k, place * TILE:(place + 1) * TILE] = moved[k * TILE:(k + 1) * TILE]
@@ -91,9 +90,14 @@
                     pltpu.make_async_copy(laid.at[which], pieces[which], piece_sems.at[which])
                 )
                 outgoing[-1].start()
-        term = dot(chol_buf[v].reshape(TILE * occ, width), masked, 0)
-        total = term if total is None else total + term
-    out[...] = total.astype(out.dtype)
+    for i in range(parts):
+        chol_copies[i].wait()
+        left = chol_buf[i].reshape(rows * occ, width)
+        out_buf[i] = dot(left, masked[...], 0).astype(out_buf.dtype)
+        outgoing.append(
+            pltpu.make_async_copy(out_buf.at[i], out.at[pl.ds(i * width, width)], sems.at[1, i])
+        )
+        outgoing[-1].start()
     for copy in outgoing:
         copy.wait()
 
@@ -218,17 +222,27 @@
     out[...] = total + base[...].astype(F32)
 
 
-def last_kernel(half, chol, ct, first, got_low, got_high, out):
+def last_kernel(half, chol, ct, first, got_low, got_high, out, held, sems):
     rows, occ, _ = chol.shape
     width = ct.shape[0]
+    steps = held.shape[0]
+    each = rows // steps
+    group = each * occ
     start = pl.multiple_of(half[0] * width, width)
-    total = dot(chol[:, :, pl.ds(start, width)].reshape(rows * occ, width), ct[...])
-    size = got_low.shape[0]
-    for i, got in enumerate((got_low, got_high)):
-        at = slice(i * size, (i + 1) * size)
-        part = total[at] + (first[at] + got[...].astype(F32))
-        here = slice(i * rows // 2, (i + 1) * rows // 2)
-        out[here] = part.astype(BF16).reshape(rows // 2, occ, out.shape[2])
+    copies = []
+    for v in range(steps):
+        here = slice(v * each, (v + 1) * each)
+        total = dot(chol[here, :, pl.ds(start, width)].reshape(group, width), ct[...])
+        got = (got_low, got_high)[v * 2 // steps]
+        at = (v % (steps // 2)) * group
+        part = first[v * group:(v + 1) * group] + got[at:at + group].astype(F32)
+        held[v] = (total + part).astype(BF16).reshape(held.shape[1:])
+        copies.append(
+            pltpu.make_async_copy(held.at[v], out.at[pl.ds(v * each, each)], sems.at[v])
+        )
+        copies[-1].start()
+    for copy in copies:
+        copy.wait()
 
 
 def shards(
@@ -256,10 +270,13 @@
             limit,
             [
                 pltpu.VMEM((steps, TILE, occ, columns), BF16),
-                pltpu.VMEM((steps, TILE, occ, wide), BF16),
+                pltpu.VMEM((rows * occ, columns), BF16),
+                pltpu.VMEM((2, rows, occ, wide // 2), BF16),
+                pltpu.VMEM((2, wide // 2, columns), outs[0].dtype),
                 pltpu.VMEM((2,) + piece.shape, BF16),
                 pltpu.SMEM(amplitude_tiles.shape, jnp.int32),
-                pltpu.SemaphoreType.DMA((2, steps)),
+                pltpu.SemaphoreType.DMA((steps,)),
+                pltpu.SemaphoreType.DMA((2, 2)),
                 pltpu.SemaphoreType.DMA((2,)),
                 pltpu.SemaphoreType.DMA(()),
             ],
@@ -267,7 +284,7 @@
         )(vir, tile, half, amplitude_tiles, amplitudes, cholesky_vectors)
 
     sent, low, high = column(
-        other, (shape((wide, columns), BF16), piece, piece), (VMEM, ANY, ANY), 3.0, FULL
+        other, (shape((wide, columns), BF16), piece, piece), (ANY,) * 3, 3.0, FULL
     )
     got = lax.ppermute(sent, "c", SWAP)
     left_low = lax.ppermute(low, "x", shift(nx, 1))
@@ -277,7 +294,7 @@
     group = ny * nx
     chunk = wide // group
     added = call(add_kernel, shape((wide, columns), BF16), [VMEM] * 2, 0.7, 8)(kept, got)
-    plane = [[(i + group // 2 + nx // 2) % group for i in range(group)]]
+    plane = [[group - 1 - i for i in range(group)]]
     line = [[(i + nz // 2) % nz for i in range(nz)]]
 
     def exchange(parts, axes, members):
@@ -349,7 +366,16 @@
         first_kernel, shape((rows * occ, columns), F32), [SMEM] + [VMEM] * 3, 0.9, 12
     )(mine, cholesky_vectors, ct_mine, base)
     return call(
-        last_kernel, shape((rows, occ, columns), BF16), [SMEM] + [VMEM] * 5, 2.0, 16
+        last_kernel,
+        shape((rows, occ, columns), BF16),
+        [SMEM] + [VMEM] * 5,
+        2.0,
+        16,
+        [
+            pltpu.VMEM((steps, TILE, occ, columns), BF16),
+            pltpu.SemaphoreType.DMA((steps,)),
+        ],
+        ANY,
     )(other, cholesky_vectors, ct_other, first, low_got, high_got)
 
 

time: 69.4 us -> 67.8 us (0.977)
  waiting for transfers between devices: 7.33 us -> 4.91 us
  starting transfers between devices: 36.9 us -> 38.1 us
    all_to_all x3, waiting for transfers between devices: 4.4 us -> 1.97 us  [exchange(): lax.all_to_all(parts, axes, 0, 0, axis_index_groups=members, tiled=True)]
    ppermute x1, starting transfers between devices: 2.44 us -> 3.3 us  [shards(): low_got = lax.ppermute(low_sent, 'c', SWAP)]
    ppermute x1, starting transfers between devices: 1.55 us -> 2.32 us  [shards(): w_other = lax.ppermute(w_swap, 'c', SWAP)]
  transfers between devices with their start and end apart: 12 -> 12, of which waited for: 3 -> 3; matrix products, arithmetic and copies ran while one was open for 0% -> 0% of each run, Pallas kernels for 24% -> 25%
where the time goes in v6:
time: 67.8 us; the launch traced here: 67.2 us
  starting transfers between devices  38.1 us (56%)
  Pallas kernels  22.9 us (34%)
  waiting for transfers between devices  4.91 us (7%)
  local copies, waits for them, and re-layouts  1.24 us (2%)
    all_to_all x3, starting transfers between devices, exchange(): lax.all_to_all(parts, axes, 0, 0, axis_index_groups=members, tiled=True)  22.9 us
    pallas_call x1, Pallas kernels, shards(): call(ladder_kernel, (shape((rows * occ, columns), BF16), half_out, half_o...  6.32 us
    pallas_call x2, Pallas kernels, column(): call(column_kernel, outs, [SMEM] * 3 + [ANY] * 3, micros, limit, [pltpu.V...  5.84 us
    ppermute x1, starting transfers between devices, shards(): low_got = lax.ppermute(low_sent, 'c', SWAP)  3.3 us
    ppermute x1, starting transfers between devices, shards(): got = lax.ppermute(sent, 'c', SWAP)  3.29 us
    ppermute x1, starting transfers between devices, shards(): from_right = lax.ppermute(to_left, 'x', shift(nx, -1))  3 us
    ppermute x1, starting transfers between devices, shards(): right_high = lax.ppermute(high, 'x', shift(nx, -1))  2.69 us
    pallas_call x1, Pallas kernels, shards(): call(last_kernel, shape((rows, occ, columns), BF16), [SMEM] + [VMEM] * 5,...  2.54 us
  transfers between devices with their start and end apart: 12, of which 3 were waited for; matrix products, arithmetic and copies ran while one was open for 0% of the time, Pallas kernels for 25%

profile of v6, /device:TPU:1, one launch (start us, length us, event | category | flops | bytes accessed | tf_op | source)
XLA Modules:
  0.0 67.2 jit_solution(14558588365994835726)
XLA Ops:
  0.0 0.0 copy-start.3
  0.0 0.0 copy-start.1
  0.0 0.0 copy-start
  0.0 3.8 %shard_map.65 = (bf16[512,512]{1,0:T(8,128)(2,1)}, bf16[4,128,512]{2,1,0:T(8,128)(2,1)}, bf16[4,128,512]{2,1,0:T(8,128)(2,1)}) custom-call(s32[1]{0:T(128)} %bitcast.1.vir, s32[1]{0:T(128)} %bitcast.2.tile, s32[1]{0:T(128)S(6)} %sub.3.half, s32[32,128]{1,0:T(8,128)} %tiles.4, bf16[256,4,512]{2,1,0:T(4,128)(2,1)} %t.3, bf16[256,4,1024]{2,1,0:T(4,128)(2,1)} %chol.7), custom_call_target="tpu_custom_call" | custom-call | bytes 10200000 | tf_op jit(solution)/shard_map/pallas_call | solution.py:265
  3.8 3.3 %collective-permute-start = (bf16[512,512]{1,0:T(8,128)(2,1)}, bf16[512,512]{1,0:T(8,128)(2,1)S(1)}, u32[]{:S(2)}, u32[]{:S(2)}) collective-permute-start(bf16[512,512]{1,0:T(8,128)(2,1)} %get-tuple-element.15), channel_id=1, source_target_pairs={{0,1},{1,0},{2,3},{3,2},{4,5},{5,4},{6,7},{7,6},{8,9},{9,8},{10,11... | collective-permute-start | bytes 1572872 | tf_op jit(solution)/shard_map/ppermute | solution.py:289
  7.1 0.0 collective-permute-start.3
  7.1 2.7 %collective-permute-start.4 = (bf16[4,128,512]{2,1,0:T(8,128)(2,1)}, bf16[4,128,512]{2,1,0:T(8,128)(2,1)}, u32[]{:S(2)}, u32[]{:S(2)}) collective-permute-start(bf16[4,128,512]{2,1,0:T(8,128)(2,1)} %get-tuple-element.19.high), channel_id=1, source_target_pairs={{0,6},{2,0},{4,2},{6,4},{1,7},{3,1},{5,3},{7,5},{8,14},{10,8},{12,... | collective-permute-start | bytes 1572872 | tf_op jit(solution)/shard_map/ppermute | solution.py:291
  9.8 0.0 copy-done.3
  9.8 0.0 copy-done.1
  9.8 0.0 copy-done
  9.8 2.0 %shard_map.64.kept = f32[512,512]{1,0:T(8,128)S(1)} custom-call(s32[1]{0:T(128)} %bitcast.1.vir, s32[1]{0:T(128)} %bitcast.2.tile, s32[1]{0:T(128)} %bitcast.half.core, s32[32,128]{1,0:T(8,128)S(1)} %copy-done.3, bf16[256,4,512]{2,1,0:T(4,128)(2,1)S(1)} %copy-done.1, bf16[256,4,1024]{2,1,0:T(4,128)(2,1)S(1)} %copy-done), custom_call_target="tpu_custom_call" | custom-call | bytes 6800000 | tf_op jit(solution)/shard_map/pallas_call | solution.py:265
  11.9 0.0 collective-permute-done.got
  11.9 0.9 %shard_map.66.after = bf16[512,512]{1,0:T(8,128)(2,1)} custom-call(f32[512,512]{1,0:T(8,128)S(1)} %shard_map.64.kept, bf16[512,512]{1,0:T(8,128)(2,1)S(1)} %collective-permute-done.got), custom_call_target="tpu_custom_call" | custom-call | bytes 2380000 | tf_op jit(solution)/shard_map/pallas_call | solution.py:296
  12.8 6.1 %all-to-all-start = ((bf16[16,32,512]{2,1,0:T(8,128)(2,1)}), bf16[16,32,512]{2,1,0:T(8,128)(2,1)S(1)}, u32[]{:S(2)}, u32[]{:S(2)}) async-start(bf16[16,32,512]{2,1,0:T(8,128)(2,1)} %bitcast.3), calls=%async_computation | async-start | bytes 1048576 | tf_op jit(solution)/shard_map/all_to_all | solution.py:301
  18.9 2.5 %shard_map.69 = (bf16[256,1024]{1,0:T(8,128)(2,1)}, bf16[256,1024]{1,0:T(8,128)(2,1)}) custom-call(s32[1]{0:T(128)} %bitcast.1.vir, s32[1]{0:T(128)} %bitcast.5.x, s32[1]{0:T(128)} %bitcast.half.core, s32[32,32]{1,0:T(8,128)} %tiles.5, bf16[256,2048]{1,0:T(8,128)(2,1)} %w.1, bf16[512,512]{1,0:T(8,128)(2,1)} %shard_map.66.after), custom_call_target="tpu_custom_call" | custom-call | bytes 6460000 | tf_op jit(solution)/shard_map/pallas_call | solution.py:306
  21.4 0.0 copy-start.4
  21.4 2.0 %collective-permute-done.3.left.left_low = bf16[4,128,512]{2,1,0:T(8,128)(2,1)} collective-permute-done((bf16[4,128,512]{2,1,0:T(8,128)(2,1)}, bf16[4,128,512]{2,1,0:T(8,128)(2,1)}, u32[]{:S(2)}, u32[]{:S(2)}) %collective-permute-start.3) | collective-permute-done | bytes 524320 | tf_op jit(solution)/shard_map/ppermute | solution.py:290
  23.4 0.0 collective-permute-done.4.right.right_high
  23.4 2.4 %shard_map.70 = (bf16[2,4,128,512]{3,2,1,0:T(8,128)(2,1)}, bf16[2,4,128,512]{3,2,1,0:T(8,128)(2,1)}) custom-call(bf16[4,128,512]{2,1,0:T(8,128)(2,1)} %get-tuple-element.18.low, bf16[4,128,512]{2,1,0:T(8,128)(2,1)} %get-tuple-element.19.high, bf16[4,128,512]{2,1,0:T(8,128)(2,1)} %collective-permute-done.3.left.left_low, ...), custom_call_target="tpu_custom_call" | custom-call | bytes 5100000 | tf_op jit(solution)/shard_map/pallas_call | solution.py:316
  25.8 0.1 collective-permute-start.5
  25.9 3.0 %collective-permute-start.6 = (bf16[2,4,128,512]{3,2,1,0:T(8,128)(2,1)}, bf16[2,4,128,512]{3,2,1,0:T(8,128)(2,1)}, u32[]{:S(2)}, u32[]{:S(2)}) collective-permute-start(bf16[2,4,128,512]{3,2,1,0:T(8,128)(2,1)} %get-tuple-element.21), channel_id=1, source_target_pairs={{0,6},{2,0},{4,2},{6,4},{1,7},{3,1},{5,3},{7,5},{8,14},{10,8},{12,... | collective-permute-start | bytes 3145736 | tf_op jit(solution)/shard_map/ppermute | solution.py:326
  28.9 0.0 all-to-all-done.parts
  28.9 0.8 %shard_map.67 = bf16[8,32,512]{2,1,0:T(8,128)(2,1)} custom-call(bf16[16,32,512]{2,1,0:T(8,128)(2,1)S(1)} %all-to-all-done.parts), custom_call_target="tpu_custom_call" | custom-call | bytes 3400000 | tf_op jit(solution)/shard_map/pallas_call | solution.py:329
  29.7 9.0 %all-to-all-start.1 = ((bf16[8,32,512]{2,1,0:T(8,128)(2,1)}), bf16[8,32,512]{2,1,0:T(8,128)(2,1)S(1)}, u32[]{:S(2)}, u32[]{:S(2)}) async-start(bf16[8,32,512]{2,1,0:T(8,128)(2,1)} %shard_map.67), calls=%async_computation.1 | async-start | bytes 524288 | tf_op jit(solution)/shard_map/all_to_all | solution.py:301
  38.8 0.0 copy-done.4
  38.8 2.3 %collective-permute-start.2 = (bf16[256,1024]{1,0:T(8,128)(2,1)S(1)}, bf16[256,1024]{1,0:T(8,128)(2,1)}, u32[]{:S(2)}, u32[]{:S(2)}) collective-permute-start(bf16[256,1024]{1,0:T(8,128)(2,1)S(1)} %copy-done.4), channel_id=1, source_target_pairs={{0,1},{1,0},{2,3},{3,2},{4,5},{5,4},{6,7},{7,6},{8,9},{9,8},{10,11... | collective-permute-start | bytes 1572872 | tf_op jit(solution)/shard_map/ppermute | solution.py:313
  41.1 2.0 %all-to-all-done.1.parts = bf16[8,32,512]{2,1,0:T(8,128)(2,1)S(1)} async-done(((bf16[8,32,512]{2,1,0:T(8,128)(2,1)}), bf16[8,32,512]{2,1,0:T(8,128)(2,1)S(1)}, u32[]{:S(2)}, u32[]{:S(2)}) %all-to-all-start.1) | async-done | bytes 262176 | tf_op jit(solution)/shard_map/all_to_all | solution.py:301
  43.0 0.9 %shard_map.68.after = bf16[16,32,512]{2,1,0:T(8,128)(2,1)} custom-call(bf16[8,32,512]{2,1,0:T(8,128)(2,1)S(1)} %all-to-all-done.1.parts), custom_call_target="tpu_custom_call" | custom-call | bytes 3400000 | tf_op jit(solution)/shard_map/pallas_call | solution.py:329
  43.9 7.7 %all-to-all-start.2 = ((bf16[16,32,512]{2,1,0:T(8,128)(2,1)}), bf16[16,32,512]{2,1,0:T(8,128)(2,1)S(1)}, u32[]{:S(2)}, u32[]{:S(2)}) async-start(bf16[16,32,512]{2,1,0:T(8,128)(2,1)} %shard_map.68.after), calls=%async_computation.2 | async-start | bytes 1048576 | tf_op jit(solution)/shard_map/all_to_all | solution.py:301
  51.7 0.0 collective-permute-done.2.w_other
  51.7 0.0 collective-permute-done.5.from_left
  51.7 0.0 collective-permute-done.6.from_right
  51.7 6.3 %shard_map.71 = (bf16[1024,512]{1,0:T(8,128)(2,1)}, bf16[512,512]{1,0:T(8,128)(2,1)}, bf16[512,512]{1,0:T(8,128)(2,1)}) custom-call(bf16[256,1024]{1,0:T(8,128)(2,1)} %get-tuple-element.16.w_mine, bf16[256,1024]{1,0:T(8,128)(2,1)} %collective-permute-done.2.w_other, bf16[256,4,512]{2,1,0:T(4,128)(2,1)} %source.1, ...), custom_call_target="tpu_custom_call" | custom-call | bytes 17000000 | tf_op jit(solution)/shard_map/pallas_call | solution.py:342
  58.0 3.3 %collective-permute-start.7 = (bf16[512,512]{1,0:T(8,128)(2,1)}, bf16[512,512]{1,0:T(8,128)(2,1)S(1)}, u32[]{:S(2)}, u32[]{:S(2)}) collective-permute-start(bf16[512,512]{1,0:T(8,128)(2,1)} %get-tuple-element.23), channel_id=1, source_target_pairs={{0,1},{1,0},{2,3},{3,2},{4,5},{5,4},{6,7},{7,6},{8,9},{9,8},{10,11... | collective-permute-start | bytes 1572872 | tf_op jit(solution)/shard_map/ppermute | solution.py:361
  61.3 0.1 collective-permute-start.8
  61.4 0.0 all-to-all-done.2
  61.4 0.4 collective-permute-start.1
  61.8 0.0 copy-start.2
  61.8 1.2 %copy-done.2 = bf16[1024,512]{1,0:T(8,128)(2,1)S(1)} copy-done((bf16[1024,512]{1,0:T(8,128)(2,1)S(1)}, bf16[1024,512]{1,0:T(8,128)(2,1)}, u32[]{:S(2)}) %copy-start.2) | copy-done | bytes 1048600
  63.1 0.7 %shard_map.72.first = f32[1024,512]{1,0:T(8,128)S(1)} custom-call(s32[1]{0:T(128)} %bitcast.half.core, bf16[256,4,1024]{2,1,0:T(4,128)(2,1)S(1)} %copy-done, bf16[512,512]{1,0:T(8,128)(2,1)S(1)} %bitcast.7, bf16[1024,512]{1,0:T(8,128)(2,1)S(1)} %copy-done.2), custom_call_target="tpu_custom_call" | custom-call | bytes 3060000 | tf_op jit(solution)/shard_map/pallas_call | solution.py:365
  63.8 0.0 collective-permute-done.7.got_low
  63.8 0.9 %collective-permute-done.8.got_high = bf16[512,512]{1,0:T(8,128)(2,1)} collective-permute-done((bf16[512,512]{1,0:T(8,128)(2,1)}, bf16[512,512]{1,0:T(8,128)(2,1)}, u32[]{:S(2)}, u32[]{:S(2)}) %collective-permute-start.8) | collective-permute-done | bytes 524320 | tf_op jit(solution)/shard_map/ppermute | solution.py:362
  64.7 0.0 collective-permute-done.1.ct
  64.7 2.5 %shard_map.73 = bf16[256,4,512]{2,1,0:T(4,128)(2,1)} custom-call(s32[1]{0:T(128)S(6)} %sub.3.half, bf16[256,4,1024]{2,1,0:T(4,128)(2,1)S(1)} %copy-done, bf16[512,512]{1,0:T(8,128)(2,1)S(1)} %collective-permute-done.1.ct, f32[1024,512]{1,0:T(8,128)S(1)} %shard_map.72.first, bf16[512,512]{1,0:T(8,128)(2,1)S(1)} %collective-permute-done.7.got_low, ...), custom_call_target="tpu_custom_call" | custom-call | bytes 6800000 | tf_op jit(solution)/shard_map/pallas_call | solution.py:368
Async XLA Ops:
  0.0 9.8 %copy-start.3 = (s32[32,128]{1,0:T(8,128)S(1)}, s32[32,128]{1,0:T(8,128)}, u32[]{:S(2)}) copy-start(s32[32,128]{1,0:T(8,128)} %tiles.4) | copy-start | bytes 49156
  0.0 9.8 %copy-start.1 = (bf16[256,4,512]{2,1,0:T(4,128)(2,1)S(1)}, bf16[256,4,512]{2,1,0:T(4,128)(2,1)}, u32[]{:S(2)}) copy-start(bf16[256,4,512]{2,1,0:T(4,128)(2,1)} %t.3) | copy-start | bytes 3145732
  0.0 9.8 %copy-start = (bf16[256,4,1024]{2,1,0:T(4,128)(2,1)S(1)}, bf16[256,4,1024]{2,1,0:T(4,128)(2,1)}, u32[]{:S(2)}) copy-start(bf16[256,4,1024]{2,1,0:T(4,128)(2,1)} %chol.7) | copy-start | bytes 6291460
  3.8 8.0 %collective-permute-start = (bf16[512,512]{1,0:T(8,128)(2,1)}, bf16[512,512]{1,0:T(8,128)(2,1)S(1)}, u32[]{:S(2)}, u32[]{:S(2)}) collective-permute-start(bf16[512,512]{1,0:T(8,128)(2,1)} %get-tuple-element.15), channel_id=1, source_target_pairs={{0,1},{1,0},{2,3},{3,2},{4,5},{5,4},{6,7},{7,6},{8,9},{9,8},{10,11... | collective-permute-start | bytes 1572872 | tf_op jit(solution)/shard_map/ppermute | solution.py:289
  7.1 16.3 %collective-permute-start.3 = (bf16[4,128,512]{2,1,0:T(8,128)(2,1)}, bf16[4,128,512]{2,1,0:T(8,128)(2,1)}, u32[]{:S(2)}, u32[]{:S(2)}) collective-permute-start(bf16[4,128,512]{2,1,0:T(8,128)(2,1)} %get-tuple-element.18.low), channel_id=1, source_target_pairs={{0,2},{2,4},{4,6},{6,0},{1,3},{3,5},{5,7},{7,1},{8,10},{10,12},{12... | collective-permute-start | bytes 1572872 | tf_op jit(solution)/shard_map/ppermute | solution.py:290
  7.1 16.3 %collective-permute-start.4 = (bf16[4,128,512]{2,1,0:T(8,128)(2,1)}, bf16[4,128,512]{2,1,0:T(8,128)(2,1)}, u32[]{:S(2)}, u32[]{:S(2)}) collective-permute-start(bf16[4,128,512]{2,1,0:T(8,128)(2,1)} %get-tuple-element.19.high), channel_id=1, source_target_pairs={{0,6},{2,0},{4,2},{6,4},{1,7},{3,1},{5,3},{7,5},{8,14},{10,8},{12,... | collective-permute-start | bytes 1572872 | tf_op jit(solution)/shard_map/ppermute | solution.py:291
  12.8 16.1 %all-to-all-start = ((bf16[16,32,512]{2,1,0:T(8,128)(2,1)}), bf16[16,32,512]{2,1,0:T(8,128)(2,1)S(1)}, u32[]{:S(2)}, u32[]{:S(2)}) async-start(bf16[16,32,512]{2,1,0:T(8,128)(2,1)} %bitcast.3), calls=%async_computation | async-start | bytes 1048576 | tf_op jit(solution)/shard_map/all_to_all | solution.py:301
  21.4 17.4 %copy-start.4 = (bf16[256,1024]{1,0:T(8,128)(2,1)S(1)}, bf16[256,1024]{1,0:T(8,128)(2,1)}, u32[]{:S(2)}) copy-start(bf16[256,1024]{1,0:T(8,128)(2,1)} %get-tuple-element.17.after) | copy-start | bytes 1572868
  25.8 25.9 %collective-permute-start.5 = (bf16[2,4,128,512]{3,2,1,0:T(8,128)(2,1)}, bf16[2,4,128,512]{3,2,1,0:T(8,128)(2,1)}, u32[]{:S(2)}, u32[]{:S(2)}) collective-permute-start(bf16[2,4,128,512]{3,2,1,0:T(8,128)(2,1)} %get-tuple-element.20), channel_id=1, source_target_pairs={{0,2},{2,4},{4,6},{6,0},{1,3},{3,5},{5,7},{7,1},{8,10},{10,12},{12... | collective-permute-start | bytes 3145736 | tf_op jit(solution)/shard_map/ppermute | solution.py:325
  25.9 25.8 %collective-permute-start.6 = (bf16[2,4,128,512]{3,2,1,0:T(8,128)(2,1)}, bf16[2,4,128,512]{3,2,1,0:T(8,128)(2,1)}, u32[]{:S(2)}, u32[]{:S(2)}) collective-permute-start(bf16[2,4,128,512]{3,2,1,0:T(8,128)(2,1)} %get-tuple-element.21), channel_id=1, source_target_pairs={{0,6},{2,0},{4,2},{6,4},{1,7},{3,1},{5,3},{7,5},{8,14},{10,8},{12,... | collective-permute-start | bytes 3145736 | tf_op jit(solution)/shard_map/ppermute | solution.py:326
  29.7 13.3 %all-to-all-start.1 = ((bf16[8,32,512]{2,1,0:T(8,128)(2,1)}), bf16[8,32,512]{2,1,0:T(8,128)(2,1)S(1)}, u32[]{:S(2)}, u32[]{:S(2)}) async-start(bf16[8,32,512]{2,1,0:T(8,128)(2,1)} %shard_map.67), calls=%async_computation.1 | async-start | bytes 524288 | tf_op jit(solution)/shard_map/all_to_all | solution.py:301
  38.8 12.9 %collective-permute-start.2 = (bf16[256,1024]{1,0:T(8,128)(2,1)S(1)}, bf16[256,1024]{1,0:T(8,128)(2,1)}, u32[]{:S(2)}, u32[]{:S(2)}) collective-permute-start(bf16[256,1024]{1,0:T(8,128)(2,1)S(1)} %copy-done.4), channel_id=1, source_target_pairs={{0,1},{1,0},{2,3},{3,2},{4,5},{5,4},{6,7},{7,6},{8,9},{9,8},{10,11... | collective-permute-start | bytes 1572872 | tf_op jit(solution)/shard_map/ppermute | solution.py:313
  43.9 17.5 %all-to-all-start.2 = ((bf16[16,32,512]{2,1,0:T(8,128)(2,1)}), bf16[16,32,512]{2,1,0:T(8,128)(2,1)S(1)}, u32[]{:S(2)}, u32[]{:S(2)}) async-start(bf16[16,32,512]{2,1,0:T(8,128)(2,1)} %shard_map.68.after), calls=%async_computation.2 | async-start | bytes 1048576 | tf_op jit(solution)/shard_map/all_to_all | solution.py:301
  58.0 5.8 %collective-permute-start.7 = (bf16[512,512]{1,0:T(8,128)(2,1)}, bf16[512,512]{1,0:T(8,128)(2,1)S(1)}, u32[]{:S(2)}, u32[]{:S(2)}) collective-permute-start(bf16[512,512]{1,0:T(8,128)(2,1)} %get-tuple-element.23), channel_id=1, source_target_pairs={{0,1},{1,0},{2,3},{3,2},{4,5},{5,4},{6,7},{7,6},{8,9},{9,8},{10,11... | collective-permute-start | bytes 1572872 | tf_op jit(solution)/shard_map/ppermute | solution.py:361
  61.3 3.4 %collective-permute-start.8 = (bf16[512,512]{1,0:T(8,128)(2,1)}, bf16[512,512]{1,0:T(8,128)(2,1)}, u32[]{:S(2)}, u32[]{:S(2)}) collective-permute-start(bf16[512,512]{1,0:T(8,128)(2,1)} %get-tuple-element.24), channel_id=1, source_target_pairs={{0,1},{1,0},{2,3},{3,2},{4,5},{5,4},{6,7},{7,6},{8,9},{9,8},{10,11... | collective-permute-start | bytes 1572872 | tf_op jit(solution)/shard_map/ppermute | solution.py:362
  61.4 3.3 %collective-permute-start.1 = (bf16[512,512]{1,0:T(8,128)(2,1)S(1)}, bf16[512,512]{1,0:T(8,128)(2,1)S(1)}, u32[]{:S(2)}, u32[]{:S(2)}) collective-permute-start(bf16[512,512]{1,0:T(8,128)(2,1)S(1)} %bitcast.6), channel_id=1, source_target_pairs={{0,1},{1,0},{2,3},{3,2},{4,5},{5,4},{6,7},{7,6},{8,9},{9,8},{10,11... | collective-permute-start | bytes 1572872 | tf_op jit(solution)/shard_map/ppermute | solution.py:364
  61.8 1.2 %copy-start.2 = (bf16[1024,512]{1,0:T(8,128)(2,1)S(1)}, bf16[1024,512]{1,0:T(8,128)(2,1)}, u32[]{:S(2)}) copy-start(bf16[1024,512]{1,0:T(8,128)(2,1)} %get-tuple-element.22.base) | copy-start | bytes 3145732

commit v7 on v6

--- a/solution.py
+++ b/solution.py
@@ -294,7 +294,7 @@
     group = ny * nx
     chunk = wide // group
     added = call(add_kernel, shape((wide, columns), BF16), [VMEM] * 2, 0.7, 8)(kept, got)
-    plane = [[group - 1 - i for i in range(group)]]
+    plane = [[row * nx + col for row in range(ny) for col in reversed(range(nx))]]
     line = [[(i + nz // 2) % nz for i in range(nz)]]
 
     def exchange(parts, axes, members):

time: 67.8 us -> 66.9 us (0.987)
  starting transfers between devices: 38.1 us -> 36.6 us
    all_to_all x3, starting transfers between devices: 22.9 us -> 21 us  [exchange(): lax.all_to_all(parts, axes, 0, 0, axis_index_groups=members, tiled=True)]
    ppermute x1, waiting for transfers between devices: 2 us -> 3.81 us  [shards(): left_low = lax.ppermute(low, 'x', shift(nx, 1))]
    ppermute x1, waiting for transfers between devices: 0.92 us -> 0.01 us  [shards(): high_got = lax.ppermute(high_sent, 'c', SWAP)]
    ppermute x1, starting transfers between devices: 0.41 us -> 1.15 us  [shards(): ct_other = lax.ppermute(ct_mine, 'c', SWAP)]
    ppermute x1, starting transfers between devices: 3.3 us -> 2.6 us  [shards(): low_got = lax.ppermute(low_sent, 'c', SWAP)]
  transfers between devices with their start and end apart: 12 -> 12, of which waited for: 3 -> 2; matrix products, arithmetic and copies ran while one was open for 0% -> 0% of each run, Pallas kernels for 25% -> 25%
where the time goes in v7:
time: 66.9 us; the launch traced here: 66.4 us
  starting transfers between devices  36.6 us (55%)
  Pallas kernels  22.9 us (34%)
  waiting for transfers between devices  5.55 us (8%)
  local copies, waits for them, and re-layouts  1.24 us (2%)
    all_to_all x3, starting transfers between devices, exchange(): lax.all_to_all(parts, axes, 0, 0, axis_index_groups=members, tiled=True)  21 us
    pallas_call x1, Pallas kernels, shards(): call(ladder_kernel, (shape((rows * occ, columns), BF16), half_out, half_o...  6.31 us
    pallas_call x2, Pallas kernels, column(): call(column_kernel, outs, [SMEM] * 3 + [ANY] * 3, micros, limit, [pltpu.V...  5.84 us
    ppermute x1, waiting for transfers between devices, shards(): left_low = lax.ppermute(low, 'x', shift(nx, 1))  3.81 us
    ppermute x1, starting transfers between devices, shards(): got = lax.ppermute(sent, 'c', SWAP)  3.29 us
    ppermute x1, starting transfers between devices, shards(): w_other = lax.ppermute(w_swap, 'c', SWAP)  2.92 us
    ppermute x1, starting transfers between devices, shards(): from_right = lax.ppermute(to_left, 'x', shift(nx, -1))  2.69 us
    ppermute x1, starting transfers between devices, shards(): right_high = lax.ppermute(high, 'x', shift(nx, -1))  2.69 us
  transfers between devices with their start and end apart: 12, of which 2 were waited for; matrix products, arithmetic and copies ran while one was open for 0% of the time, Pallas kernels for 25%

profile of v7, /device:TPU:1, one launch (start us, length us, event | category | flops | bytes accessed | tf_op | source)
XLA Modules:
  0.0 66.4 jit_solution(15633636156703141829)
XLA Ops:
  0.0 0.0 copy-start.3
  0.0 0.0 copy-start.1
  0.0 0.0 copy-start
  0.0 3.8 %shard_map.65 = (bf16[512,512]{1,0:T(8,128)(2,1)}, bf16[4,128,512]{2,1,0:T(8,128)(2,1)}, bf16[4,128,512]{2,1,0:T(8,128)(2,1)}) custom-call(s32[1]{0:T(128)} %bitcast.1.vir, s32[1]{0:T(128)} %bitcast.2.tile, s32[1]{0:T(128)S(6)} %sub.3.half, s32[32,128]{1,0:T(8,128)} %tiles.4, bf16[256,4,512]{2,1,0:T(4,128)(2,1)} %t.3, bf16[256,4,1024]{2,1,0:T(4,128)(2,1)} %chol.7), custom_call_target="tpu_custom_call" | custom-call | bytes 10200000 | tf_op jit(solution)/shard_map/pallas_call | solution.py:265
  3.8 3.3 %collective-permute-start = (bf16[512,512]{1,0:T(8,128)(2,1)}, bf16[512,512]{1,0:T(8,128)(2,1)S(1)}, u32[]{:S(2)}, u32[]{:S(2)}) collective-permute-start(bf16[512,512]{1,0:T(8,128)(2,1)} %get-tuple-element.15), channel_id=1, source_target_pairs={{0,1},{1,0},{2,3},{3,2},{4,5},{5,4},{6,7},{7,6},{8,9},{9,8},{10,11... | collective-permute-start | bytes 1572872 | tf_op jit(solution)/shard_map/ppermute | solution.py:289
  7.1 0.0 collective-permute-start.3
  7.1 2.7 %collective-permute-start.4 = (bf16[4,128,512]{2,1,0:T(8,128)(2,1)}, bf16[4,128,512]{2,1,0:T(8,128)(2,1)}, u32[]{:S(2)}, u32[]{:S(2)}) collective-permute-start(bf16[4,128,512]{2,1,0:T(8,128)(2,1)} %get-tuple-element.19.high), channel_id=1, source_target_pairs={{0,6},{2,0},{4,2},{6,4},{1,7},{3,1},{5,3},{7,5},{8,14},{10,8},{12,... | collective-permute-start | bytes 1572872 | tf_op jit(solution)/shard_map/ppermute | solution.py:291
  9.8 0.0 copy-done.3
  9.8 0.0 copy-done.1
  9.8 0.0 copy-done
  9.8 2.0 %shard_map.64.kept = f32[512,512]{1,0:T(8,128)S(1)} custom-call(s32[1]{0:T(128)} %bitcast.1.vir, s32[1]{0:T(128)} %bitcast.2.tile, s32[1]{0:T(128)} %bitcast.half.core, s32[32,128]{1,0:T(8,128)S(1)} %copy-done.3, bf16[256,4,512]{2,1,0:T(4,128)(2,1)S(1)} %copy-done.1, bf16[256,4,1024]{2,1,0:T(4,128)(2,1)S(1)} %copy-done), custom_call_target="tpu_custom_call" | custom-call | bytes 6800000 | tf_op jit(solution)/shard_map/pallas_call | solution.py:265
  11.9 0.0 collective-permute-done.got
  11.9 0.9 %shard_map.66.after = bf16[512,512]{1,0:T(8,128)(2,1)} custom-call(f32[512,512]{1,0:T(8,128)S(1)} %shard_map.64.kept, bf16[512,512]{1,0:T(8,128)(2,1)S(1)} %collective-permute-done.got), custom_call_target="tpu_custom_call" | custom-call | bytes 2380000 | tf_op jit(solution)/shard_map/pallas_call | solution.py:296
  12.8 4.9 %all-to-all-start = ((bf16[16,32,512]{2,1,0:T(8,128)(2,1)}), bf16[16,32,512]{2,1,0:T(8,128)(2,1)S(1)}, u32[]{:S(2)}, u32[]{:S(2)}) async-start(bf16[16,32,512]{2,1,0:T(8,128)(2,1)} %bitcast.3), calls=%async_computation | async-start | bytes 1048576 | tf_op jit(solution)/shard_map/all_to_all | solution.py:301
  17.7 2.5 %shard_map.69 = (bf16[256,1024]{1,0:T(8,128)(2,1)}, bf16[256,1024]{1,0:T(8,128)(2,1)}) custom-call(s32[1]{0:T(128)} %bitcast.1.vir, s32[1]{0:T(128)} %bitcast.5.x, s32[1]{0:T(128)} %bitcast.half.core, s32[32,32]{1,0:T(8,128)} %tiles.5, bf16[256,2048]{1,0:T(8,128)(2,1)} %w.1, bf16[512,512]{1,0:T(8,128)(2,1)} %shard_map.66.after), custom_call_target="tpu_custom_call" | custom-call | bytes 6460000 | tf_op jit(solution)/shard_map/pallas_call | solution.py:306
  20.2 0.0 copy-start.4
  20.2 3.8 %collective-permute-done.3.left.left_low = bf16[4,128,512]{2,1,0:T(8,128)(2,1)} collective-permute-done((bf16[4,128,512]{2,1,0:T(8,128)(2,1)}, bf16[4,128,512]{2,1,0:T(8,128)(2,1)}, u32[]{:S(2)}, u32[]{:S(2)}) %collective-permute-start.3) | collective-permute-done | bytes 524320 | tf_op jit(solution)/shard_map/ppermute | solution.py:290
  24.0 0.0 collective-permute-done.4.right.right_high
  24.0 2.4 %shard_map.70 = (bf16[2,4,128,512]{3,2,1,0:T(8,128)(2,1)}, bf16[2,4,128,512]{3,2,1,0:T(8,128)(2,1)}) custom-call(bf16[4,128,512]{2,1,0:T(8,128)(2,1)} %get-tuple-element.18.low, bf16[4,128,512]{2,1,0:T(8,128)(2,1)} %get-tuple-element.19.high, bf16[4,128,512]{2,1,0:T(8,128)(2,1)} %collective-permute-done.3.left.left_low, ...), custom_call_target="tpu_custom_call" | custom-call | bytes 5100000 | tf_op jit(solution)/shard_map/pallas_call | solution.py:316
  26.4 0.1 collective-permute-start.5
  26.5 2.7 %collective-permute-start.6 = (bf16[2,4,128,512]{3,2,1,0:T(8,128)(2,1)}, bf16[2,4,128,512]{3,2,1,0:T(8,128)(2,1)}, u32[]{:S(2)}, u32[]{:S(2)}) collective-permute-start(bf16[2,4,128,512]{3,2,1,0:T(8,128)(2,1)} %get-tuple-element.21), channel_id=1, source_target_pairs={{0,6},{2,0},{4,2},{6,4},{1,7},{3,1},{5,3},{7,5},{8,14},{10,8},{12,... | collective-permute-start | bytes 3145736 | tf_op jit(solution)/shard_map/ppermute | solution.py:326
  29.2 0.0 all-to-all-done.parts
  29.2 0.8 %shard_map.67 = bf16[8,32,512]{2,1,0:T(8,128)(2,1)} custom-call(bf16[16,32,512]{2,1,0:T(8,128)(2,1)S(1)} %all-to-all-done.parts), custom_call_target="tpu_custom_call" | custom-call | bytes 3400000 | tf_op jit(solution)/shard_map/pallas_call | solution.py:329
  30.0 8.1 %all-to-all-start.1 = ((bf16[8,32,512]{2,1,0:T(8,128)(2,1)}), bf16[8,32,512]{2,1,0:T(8,128)(2,1)S(1)}, u32[]{:S(2)}, u32[]{:S(2)}) async-start(bf16[8,32,512]{2,1,0:T(8,128)(2,1)} %shard_map.67), calls=%async_computation.1 | async-start | bytes 524288 | tf_op jit(solution)/shard_map/all_to_all | solution.py:301
  38.2 0.0 copy-done.4
  38.2 2.9 %collective-permute-start.2 = (bf16[256,1024]{1,0:T(8,128)(2,1)S(1)}, bf16[256,1024]{1,0:T(8,128)(2,1)}, u32[]{:S(2)}, u32[]{:S(2)}) collective-permute-start(bf16[256,1024]{1,0:T(8,128)(2,1)S(1)} %copy-done.4), channel_id=1, source_target_pairs={{0,1},{1,0},{2,3},{3,2},{4,5},{5,4},{6,7},{7,6},{8,9},{9,8},{10,11... | collective-permute-start | bytes 1572872 | tf_op jit(solution)/shard_map/ppermute | solution.py:313
  41.1 1.7 %all-to-all-done.1.parts = bf16[8,32,512]{2,1,0:T(8,128)(2,1)S(1)} async-done(((bf16[8,32,512]{2,1,0:T(8,128)(2,1)}), bf16[8,32,512]{2,1,0:T(8,128)(2,1)S(1)}, u32[]{:S(2)}, u32[]{:S(2)}) %all-to-all-start.1) | async-done | bytes 262176 | tf_op jit(solution)/shard_map/all_to_all | solution.py:301
  42.8 0.9 %shard_map.68.after = bf16[16,32,512]{2,1,0:T(8,128)(2,1)} custom-call(bf16[8,32,512]{2,1,0:T(8,128)(2,1)S(1)} %all-to-all-done.1.parts), custom_call_target="tpu_custom_call" | custom-call | bytes 3400000 | tf_op jit(solution)/shard_map/pallas_call | solution.py:329
  43.7 8.0 %all-to-all-start.2 = ((bf16[16,32,512]{2,1,0:T(8,128)(2,1)}), bf16[16,32,512]{2,1,0:T(8,128)(2,1)S(1)}, u32[]{:S(2)}, u32[]{:S(2)}) async-start(bf16[16,32,512]{2,1,0:T(8,128)(2,1)} %shard_map.68.after), calls=%async_computation.2 | async-start | bytes 1048576 | tf_op jit(solution)/shard_map/all_to_all | solution.py:301
  51.7 0.0 collective-permute-done.2.w_other
  51.7 0.0 collective-permute-done.5.from_left
  51.7 0.0 collective-permute-done.6.from_right
  51.7 6.3 %shard_map.71 = (bf16[1024,512]{1,0:T(8,128)(2,1)}, bf16[512,512]{1,0:T(8,128)(2,1)}, bf16[512,512]{1,0:T(8,128)(2,1)}) custom-call(bf16[256,1024]{1,0:T(8,128)(2,1)} %get-tuple-element.16.w_mine, bf16[256,1024]{1,0:T(8,128)(2,1)} %collective-permute-done.2.w_other, bf16[256,4,512]{2,1,0:T(4,128)(2,1)} %source.1, ...), custom_call_target="tpu_custom_call" | custom-call | bytes 17000000 | tf_op jit(solution)/shard_map/pallas_call | solution.py:342
  58.0 2.6 %collective-permute-start.7 = (bf16[512,512]{1,0:T(8,128)(2,1)}, bf16[512,512]{1,0:T(8,128)(2,1)S(1)}, u32[]{:S(2)}, u32[]{:S(2)}) collective-permute-start(bf16[512,512]{1,0:T(8,128)(2,1)} %get-tuple-element.23), channel_id=1, source_target_pairs={{0,1},{1,0},{2,3},{3,2},{4,5},{5,4},{6,7},{7,6},{8,9},{9,8},{10,11... | collective-permute-start | bytes 1572872 | tf_op jit(solution)/shard_map/ppermute | solution.py:361
  60.6 0.1 collective-permute-start.8
  60.7 0.0 all-to-all-done.2
  60.7 1.2 %collective-permute-start.1 = (bf16[512,512]{1,0:T(8,128)(2,1)S(1)}, bf16[512,512]{1,0:T(8,128)(2,1)S(1)}, u32[]{:S(2)}, u32[]{:S(2)}) collective-permute-start(bf16[512,512]{1,0:T(8,128)(2,1)S(1)} %bitcast.6), channel_id=1, source_target_pairs={{0,1},{1,0},{2,3},{3,2},{4,5},{5,4},{6,7},{7,6},{8,9},{9,8},{10,11... | collective-permute-start | bytes 1572872 | tf_op jit(solution)/shard_map/ppermute | solution.py:364
  61.9 0.0 copy-start.2
  61.9 1.2 %copy-done.2 = bf16[1024,512]{1,0:T(8,128)(2,1)S(1)} copy-done((bf16[1024,512]{1,0:T(8,128)(2,1)S(1)}, bf16[1024,512]{1,0:T(8,128)(2,1)}, u32[]{:S(2)}) %copy-start.2) | copy-done | bytes 1048600
  63.1 0.7 %shard_map.72.first = f32[1024,512]{1,0:T(8,128)S(1)} custom-call(s32[1]{0:T(128)} %bitcast.half.core, bf16[256,4,1024]{2,1,0:T(4,128)(2,1)S(1)} %copy-done, bf16[512,512]{1,0:T(8,128)(2,1)S(1)} %bitcast.7, bf16[1024,512]{1,0:T(8,128)(2,1)S(1)} %copy-done.2), custom_call_target="tpu_custom_call" | custom-call | bytes 3060000 | tf_op jit(solution)/shard_map/pallas_call | solution.py:365
  63.8 0.0 collective-permute-done.7.got_low
  63.9 0.0 collective-permute-done.8.got_high
  63.9 0.0 collective-permute-done.1.ct
  63.9 2.5 %shard_map.73 = bf16[256,4,512]{2,1,0:T(4,128)(2,1)} custom-call(s32[1]{0:T(128)S(6)} %sub.3.half, bf16[256,4,1024]{2,1,0:T(4,128)(2,1)S(1)} %copy-done, bf16[512,512]{1,0:T(8,128)(2,1)S(1)} %collective-permute-done.1.ct, f32[1024,512]{1,0:T(8,128)S(1)} %shard_map.72.first, bf16[512,512]{1,0:T(8,128)(2,1)S(1)} %collective-permute-done.7.got_low, ...), custom_call_target="tpu_custom_call" | custom-call | bytes 6800000 | tf_op jit(solution)/shard_map/pallas_call | solution.py:368
Async XLA Ops:
  0.0 9.8 %copy-start.3 = (s32[32,128]{1,0:T(8,128)S(1)}, s32[32,128]{1,0:T(8,128)}, u32[]{:S(2)}) copy-start(s32[32,128]{1,0:T(8,128)} %tiles.4) | copy-start | bytes 49156
  0.0 9.8 %copy-start.1 = (bf16[256,4,512]{2,1,0:T(4,128)(2,1)S(1)}, bf16[256,4,512]{2,1,0:T(4,128)(2,1)}, u32[]{:S(2)}) copy-start(bf16[256,4,512]{2,1,0:T(4,128)(2,1)} %t.3) | copy-start | bytes 3145732
  0.0 9.8 %copy-start = (bf16[256,4,1024]{2,1,0:T(4,128)(2,1)S(1)}, bf16[256,4,1024]{2,1,0:T(4,128)(2,1)}, u32[]{:S(2)}) copy-start(bf16[256,4,1024]{2,1,0:T(4,128)(2,1)} %chol.7) | copy-start | bytes 6291460
  3.8 8.0 %collective-permute-start = (bf16[512,512]{1,0:T(8,128)(2,1)}, bf16[512,512]{1,0:T(8,128)(2,1)S(1)}, u32[]{:S(2)}, u32[]{:S(2)}) collective-permute-start(bf16[512,512]{1,0:T(8,128)(2,1)} %get-tuple-element.15), channel_id=1, source_target_pairs={{0,1},{1,0},{2,3},{3,2},{4,5},{5,4},{6,7},{7,6},{8,9},{9,8},{10,11... | collective-permute-start | bytes 1572872 | tf_op jit(solution)/shard_map/ppermute | solution.py:289
  7.1 16.9 %collective-permute-start.3 = (bf16[4,128,512]{2,1,0:T(8,128)(2,1)}, bf16[4,128,512]{2,1,0:T(8,128)(2,1)}, u32[]{:S(2)}, u32[]{:S(2)}) collective-permute-start(bf16[4,128,512]{2,1,0:T(8,128)(2,1)} %get-tuple-element.18.low), channel_id=1, source_target_pairs={{0,2},{2,4},{4,6},{6,0},{1,3},{3,5},{5,7},{7,1},{8,10},{10,12},{12... | collective-permute-start | bytes 1572872 | tf_op jit(solution)/shard_map/ppermute | solution.py:290
  7.1 16.9 %collective-permute-start.4 = (bf16[4,128,512]{2,1,0:T(8,128)(2,1)}, bf16[4,128,512]{2,1,0:T(8,128)(2,1)}, u32[]{:S(2)}, u32[]{:S(2)}) collective-permute-start(bf16[4,128,512]{2,1,0:T(8,128)(2,1)} %get-tuple-element.19.high), channel_id=1, source_target_pairs={{0,6},{2,0},{4,2},{6,4},{1,7},{3,1},{5,3},{7,5},{8,14},{10,8},{12,... | collective-permute-start | bytes 1572872 | tf_op jit(solution)/shard_map/ppermute | solution.py:291
  12.8 16.4 %all-to-all-start = ((bf16[16,32,512]{2,1,0:T(8,128)(2,1)}), bf16[16,32,512]{2,1,0:T(8,128)(2,1)S(1)}, u32[]{:S(2)}, u32[]{:S(2)}) async-start(bf16[16,32,512]{2,1,0:T(8,128)(2,1)} %bitcast.3), calls=%async_computation | async-start | bytes 1048576 | tf_op jit(solution)/shard_map/all_to_all | solution.py:301
  20.2 18.0 %copy-start.4 = (bf16[256,1024]{1,0:T(8,128)(2,1)S(1)}, bf16[256,1024]{1,0:T(8,128)(2,1)}, u32[]{:S(2)}) copy-start(bf16[256,1024]{1,0:T(8,128)(2,1)} %get-tuple-element.17.after) | copy-start | bytes 1572868
  26.4 25.3 %collective-permute-start.5 = (bf16[2,4,128,512]{3,2,1,0:T(8,128)(2,1)}, bf16[2,4,128,512]{3,2,1,0:T(8,128)(2,1)}, u32[]{:S(2)}, u32[]{:S(2)}) collective-permute-start(bf16[2,4,128,512]{3,2,1,0:T(8,128)(2,1)} %get-tuple-element.20), channel_id=1, source_target_pairs={{0,2},{2,4},{4,6},{6,0},{1,3},{3,5},{5,7},{7,1},{8,10},{10,12},{12... | collective-permute-start | bytes 3145736 | tf_op jit(solution)/shard_map/ppermute | solution.py:325
  26.5 25.2 %collective-permute-start.6 = (bf16[2,4,128,512]{3,2,1,0:T(8,128)(2,1)}, bf16[2,4,128,512]{3,2,1,0:T(8,128)(2,1)}, u32[]{:S(2)}, u32[]{:S(2)}) collective-permute-start(bf16[2,4,128,512]{3,2,1,0:T(8,128)(2,1)} %get-tuple-element.21), channel_id=1, source_target_pairs={{0,6},{2,0},{4,2},{6,4},{1,7},{3,1},{5,3},{7,5},{8,14},{10,8},{12,... | collective-permute-start | bytes 3145736 | tf_op jit(solution)/shard_map/ppermute | solution.py:326
  30.0 12.8 %all-to-all-start.1 = ((bf16[8,32,512]{2,1,0:T(8,128)(2,1)}), bf16[8,32,512]{2,1,0:T(8,128)(2,1)S(1)}, u32[]{:S(2)}, u32[]{:S(2)}) async-start(bf16[8,32,512]{2,1,0:T(8,128)(2,1)} %shard_map.67), calls=%async_computation.1 | async-start | bytes 524288 | tf_op jit(solution)/shard_map/all_to_all | solution.py:301
  38.2 13.5 %collective-permute-start.2 = (bf16[256,1024]{1,0:T(8,128)(2,1)S(1)}, bf16[256,1024]{1,0:T(8,128)(2,1)}, u32[]{:S(2)}, u32[]{:S(2)}) collective-permute-start(bf16[256,1024]{1,0:T(8,128)(2,1)S(1)} %copy-done.4), channel_id=1, source_target_pairs={{0,1},{1,0},{2,3},{3,2},{4,5},{5,4},{6,7},{7,6},{8,9},{9,8},{10,11... | collective-permute-start | bytes 1572872 | tf_op jit(solution)/shard_map/ppermute | solution.py:313
  43.7 17.1 %all-to-all-start.2 = ((bf16[16,32,512]{2,1,0:T(8,128)(2,1)}), bf16[16,32,512]{2,1,0:T(8,128)(2,1)S(1)}, u32[]{:S(2)}, u32[]{:S(2)}) async-start(bf16[16,32,512]{2,1,0:T(8,128)(2,1)} %shard_map.68.after), calls=%async_computation.2 | async-start | bytes 1048576 | tf_op jit(solution)/shard_map/all_to_all | solution.py:301
  58.0 5.8 %collective-permute-start.7 = (bf16[512,512]{1,0:T(8,128)(2,1)}, bf16[512,512]{1,0:T(8,128)(2,1)S(1)}, u32[]{:S(2)}, u32[]{:S(2)}) collective-permute-start(bf16[512,512]{1,0:T(8,128)(2,1)} %get-tuple-element.23), channel_id=1, source_target_pairs={{0,1},{1,0},{2,3},{3,2},{4,5},{5,4},{6,7},{7,6},{8,9},{9,8},{10,11... | collective-permute-start | bytes 1572872 | tf_op jit(solution)/shard_map/ppermute | solution.py:361
  60.6 3.2 %collective-permute-start.8 = (bf16[512,512]{1,0:T(8,128)(2,1)}, bf16[512,512]{1,0:T(8,128)(2,1)}, u32[]{:S(2)}, u32[]{:S(2)}) collective-permute-start(bf16[512,512]{1,0:T(8,128)(2,1)} %get-tuple-element.24), channel_id=1, source_target_pairs={{0,1},{1,0},{2,3},{3,2},{4,5},{5,4},{6,7},{7,6},{8,9},{9,8},{10,11... | collective-permute-start | bytes 1572872 | tf_op jit(solution)/shard_map/ppermute | solution.py:362
  60.7 3.1 %collective-permute-start.1 = (bf16[512,512]{1,0:T(8,128)(2,1)S(1)}, bf16[512,512]{1,0:T(8,128)(2,1)S(1)}, u32[]{:S(2)}, u32[]{:S(2)}) collective-permute-start(bf16[512,512]{1,0:T(8,128)(2,1)S(1)} %bitcast.6), channel_id=1, source_target_pairs={{0,1},{1,0},{2,3},{3,2},{4,5},{5,4},{6,7},{7,6},{8,9},{9,8},{10,11... | collective-permute-start | bytes 1572872 | tf_op jit(solution)/shard_map/ppermute | solution.py:364
  61.9 1.2 %copy-start.2 = (bf16[1024,512]{1,0:T(8,128)(2,1)S(1)}, bf16[1024,512]{1,0:T(8,128)(2,1)}, u32[]{:S(2)}) copy-start(bf16[1024,512]{1,0:T(8,128)(2,1)} %get-tuple-element.22.base) | copy-start | bytes 3145732

commit v8 on v7

--- a/solution.py
+++ b/solution.py
@@ -102,8 +102,22 @@
         copy.wait()
 
 
-def add_kernel(kept, got, out):
-    out[...] = (kept[...] + got[...].astype(F32)).astype(BF16)
+def kept_kernel(vir, tile, half, mask, t, chol, got, out):
+    rows, occ, cols = t.shape
+    width = out.shape[0]
+    steps = rows // TILE
+    start = pl.multiple_of(half[0] * width, width)
+    k_id = lax.broadcasted_iota(jnp.int32, (occ, cols), 0)
+    parts = []
+    for v in range(steps):
+        keep = jnp.zeros((occ, cols), F32)
+        for k in range(occ):
+            kept = mask[vir[0] * steps + v, tile[0] * occ + k]
+            keep = jnp.where(k_id == k, kept.astype(F32), keep)
+        parts.append(t[v * TILE:(v + 1) * TILE] * keep.astype(BF16)[None])
+    masked = jnp.concatenate(parts, 0).reshape(rows * occ, cols)
+    left = chol[:, :, pl.ds(start, width)].reshape(rows * occ, width)
+    out[...] = (dot(left, masked, 0) + got[...].astype(F32)).astype(BF16)
 
 
 def w_kernel(places, vir, x, core, tiles, w, after, mine, other):
@@ -289,11 +303,11 @@
     got = lax.ppermute(sent, "c", SWAP)
     left_low = lax.ppermute(low, "x", shift(nx, 1))
     right_high = lax.ppermute(high, "x", shift(nx, -1))
-    (kept,) = column(mine, (shape((wide, columns), F32),), (VMEM,), 2.0, 16)
-
     group = ny * nx
     chunk = wide // group
-    added = call(add_kernel, shape((wide, columns), BF16), [VMEM] * 2, 0.7, 8)(kept, got)
+    added = call(
+        kept_kernel, shape((wide, columns), BF16), [SMEM] * 4 + [VMEM] * 3, 2.2, 16
+    )(vir, tile, mine, amplitude_tiles, amplitudes, cholesky_vectors, got)
     plane = [[row * nx + col for row in range(ny) for col in reversed(range(nx))]]
     line = [[(i + nz // 2) % nz for i in range(nz)]]
 

time: 66.9 us -> 67 us (level)
    pallas_call x2 -> x1, Pallas kernels: 5.84 us -> 3.82 us  [column(): call(column_kernel, outs, [SMEM] * 3 + [ANY] * 3, micros, limit, [pltpu.V...]
    pallas_call x1, Pallas kernels: 0.89 us -> 2.38 us  [shards(): call(kept_kernel, shape((wide, columns), BF16), [SMEM] * 4 + [VMEM] * 3,...]
  transfers between devices with their start and end apart: 12 -> 12, of which waited for: 2 -> 2; matrix products, arithmetic and copies ran while one was open for 0% -> 0% of each run, Pallas kernels for 25% -> 24%
where the time goes in v8:
time: 67 us; the launch traced here: 66.4 us
  starting transfers between devices  36.6 us (55%)
  Pallas kernels  22.4 us (33%)
  waiting for transfers between devices  6.09 us (9%)
  local copies, waits for them, and re-layouts  1.24 us (2%)
    all_to_all x3, starting transfers between devices, exchange(): lax.all_to_all(parts, axes, 0, 0, axis_index_groups=members, tiled=True)  21 us
    pallas_call x1, Pallas kernels, shards(): call(ladder_kernel, (shape((rows * occ, columns), BF16), half_out, half_o...  6.31 us
    ppermute x1, waiting for transfers between devices, shards(): left_low = lax.ppermute(low, 'x', shift(nx, 1))  4.35 us
    pallas_call x1, Pallas kernels, column(): call(column_kernel, outs, [SMEM] * 3 + [ANY] * 3, micros, limit, [pltpu.V...  3.82 us
    ppermute x1, starting transfers between devices, shards(): got = lax.ppermute(sent, 'c', SWAP)  3.29 us
    ppermute x1, starting transfers between devices, shards(): w_other = lax.ppermute(w_swap, 'c', SWAP)  2.92 us
    ppermute x1, starting transfers between devices, shards(): from_right = lax.ppermute(to_left, 'x', shift(nx, -1))  2.69 us
    ppermute x1, starting transfers between devices, shards(): right_high = lax.ppermute(high, 'x', shift(nx, -1))  2.69 us
  transfers between devices with their start and end apart: 12, of which 2 were waited for; matrix products, arithmetic and copies ran while one was open for 0% of the time, Pallas kernels for 24%

profile of v8, /device:TPU:1, one launch (start us, length us, event | category | flops | bytes accessed | tf_op | source)
XLA Modules:
  0.0 66.4 jit_solution(2272378092191579195)
XLA Ops:
  0.0 0.0 copy-start.3
  0.0 0.0 copy-start.1
  0.0 0.0 copy-start
  0.0 3.8 %shard_map.64 = (bf16[512,512]{1,0:T(8,128)(2,1)}, bf16[4,128,512]{2,1,0:T(8,128)(2,1)}, bf16[4,128,512]{2,1,0:T(8,128)(2,1)}) custom-call(s32[1]{0:T(128)} %bitcast.1.vir, s32[1]{0:T(128)} %bitcast.2.tile, s32[1]{0:T(128)S(6)} %sub.3.half, s32[32,128]{1,0:T(8,128)} %mask.1, bf16[256,4,512]{2,1,0:T(4,128)(2,1)} %t.3, bf16[256,4,1024]{2,1,0:T(4,128)(2,1)} %chol.7), custom_call_target="tpu_custom_call" | custom-call | bytes 10200000 | tf_op jit(solution)/shard_map/pallas_call | solution.py:279
  3.8 3.3 %collective-permute-start = (bf16[512,512]{1,0:T(8,128)(2,1)}, bf16[512,512]{1,0:T(8,128)(2,1)S(1)}, u32[]{:S(2)}, u32[]{:S(2)}) collective-permute-start(bf16[512,512]{1,0:T(8,128)(2,1)} %get-tuple-element.15), channel_id=1, source_target_pairs={{0,1},{1,0},{2,3},{3,2},{4,5},{5,4},{6,7},{7,6},{8,9},{9,8},{10,11... | collective-permute-start | bytes 1572872 | tf_op jit(solution)/shard_map/ppermute | solution.py:303
  7.1 0.0 collective-permute-start.3
  7.1 2.7 %collective-permute-start.4 = (bf16[4,128,512]{2,1,0:T(8,128)(2,1)}, bf16[4,128,512]{2,1,0:T(8,128)(2,1)}, u32[]{:S(2)}, u32[]{:S(2)}) collective-permute-start(bf16[4,128,512]{2,1,0:T(8,128)(2,1)} %get-tuple-element.19.high), channel_id=1, source_target_pairs={{0,6},{2,0},{4,2},{6,4},{1,7},{3,1},{5,3},{7,5},{8,14},{10,8},{12,... | collective-permute-start | bytes 1572872 | tf_op jit(solution)/shard_map/ppermute | solution.py:305
  9.8 0.0 collective-permute-done.got
  9.8 0.0 copy-done.3
  9.8 0.0 copy-done.1
  9.8 0.0 copy-done
  9.9 2.4 %shard_map.65.after = bf16[512,512]{1,0:T(8,128)(2,1)} custom-call(s32[1]{0:T(128)} %bitcast.1.vir, s32[1]{0:T(128)} %bitcast.2.tile, s32[1]{0:T(128)} %bitcast.half.core, s32[32,128]{1,0:T(8,128)S(1)} %copy-done.3, bf16[256,4,512]{2,1,0:T(4,128)(2,1)S(1)} %copy-done.1, bf16[256,4,1024]{2,1,0:T(4,128)(2,1)S(1)} %copy-done, ...), custom_call_target="tpu_custom_call" | custom-call | bytes 7480000 | tf_op jit(solution)/shard_map/pallas_call | solution.py:308
  12.2 4.9 %all-to-all-start = ((bf16[16,32,512]{2,1,0:T(8,128)(2,1)}), bf16[16,32,512]{2,1,0:T(8,128)(2,1)S(1)}, u32[]{:S(2)}, u32[]{:S(2)}) async-start(bf16[16,32,512]{2,1,0:T(8,128)(2,1)} %bitcast.3), calls=%async_computation | async-start | bytes 1048576 | tf_op jit(solution)/shard_map/all_to_all | solution.py:315
  17.1 2.5 %shard_map.68 = (bf16[256,1024]{1,0:T(8,128)(2,1)}, bf16[256,1024]{1,0:T(8,128)(2,1)}) custom-call(s32[1]{0:T(128)} %bitcast.1.vir, s32[1]{0:T(128)} %bitcast.5.x, s32[1]{0:T(128)} %bitcast.half.core, s32[32,32]{1,0:T(8,128)} %tiles.3, bf16[256,2048]{1,0:T(8,128)(2,1)} %w.1, bf16[512,512]{1,0:T(8,128)(2,1)} %shard_map.65.after), custom_call_target="tpu_custom_call" | custom-call | bytes 6460000 | tf_op jit(solution)/shard_map/pallas_call | solution.py:320
  19.7 0.0 copy-start.4
  19.7 4.3 %collective-permute-done.3.left.left_low = bf16[4,128,512]{2,1,0:T(8,128)(2,1)} collective-permute-done((bf16[4,128,512]{2,1,0:T(8,128)(2,1)}, bf16[4,128,512]{2,1,0:T(8,128)(2,1)}, u32[]{:S(2)}, u32[]{:S(2)}) %collective-permute-start.3) | collective-permute-done | bytes 524320 | tf_op jit(solution)/shard_map/ppermute | solution.py:304
  24.0 0.0 collective-permute-done.4.right.right_high
  24.0 2.4 %shard_map.69 = (bf16[2,4,128,512]{3,2,1,0:T(8,128)(2,1)}, bf16[2,4,128,512]{3,2,1,0:T(8,128)(2,1)}) custom-call(bf16[4,128,512]{2,1,0:T(8,128)(2,1)} %get-tuple-element.18.low, bf16[4,128,512]{2,1,0:T(8,128)(2,1)} %get-tuple-element.19.high, bf16[4,128,512]{2,1,0:T(8,128)(2,1)} %collective-permute-done.3.left.left_low, ...), custom_call_target="tpu_custom_call" | custom-call | bytes 5100000 | tf_op jit(solution)/shard_map/pallas_call | solution.py:330
  26.4 0.1 collective-permute-start.5
  26.5 2.7 %collective-permute-start.6 = (bf16[2,4,128,512]{3,2,1,0:T(8,128)(2,1)}, bf16[2,4,128,512]{3,2,1,0:T(8,128)(2,1)}, u32[]{:S(2)}, u32[]{:S(2)}) collective-permute-start(bf16[2,4,128,512]{3,2,1,0:T(8,128)(2,1)} %get-tuple-element.21), channel_id=1, source_target_pairs={{0,6},{2,0},{4,2},{6,4},{1,7},{3,1},{5,3},{7,5},{8,14},{10,8},{12,... | collective-permute-start | bytes 3145736 | tf_op jit(solution)/shard_map/ppermute | solution.py:340
  29.2 0.0 all-to-all-done.parts
  29.2 0.8 %shard_map.66 = bf16[8,32,512]{2,1,0:T(8,128)(2,1)} custom-call(bf16[16,32,512]{2,1,0:T(8,128)(2,1)S(1)} %all-to-all-done.parts), custom_call_target="tpu_custom_call" | custom-call | bytes 3400000 | tf_op jit(solution)/shard_map/pallas_call | solution.py:343
  30.0 8.1 %all-to-all-start.1 = ((bf16[8,32,512]{2,1,0:T(8,128)(2,1)}), bf16[8,32,512]{2,1,0:T(8,128)(2,1)S(1)}, u32[]{:S(2)}, u32[]{:S(2)}) async-start(bf16[8,32,512]{2,1,0:T(8,128)(2,1)} %shard_map.66), calls=%async_computation.1 | async-start | bytes 524288 | tf_op jit(solution)/shard_map/all_to_all | solution.py:315
  38.1 0.0 copy-done.4
  38.1 2.9 %collective-permute-start.2 = (bf16[256,1024]{1,0:T(8,128)(2,1)S(1)}, bf16[256,1024]{1,0:T(8,128)(2,1)}, u32[]{:S(2)}, u32[]{:S(2)}) collective-permute-start(bf16[256,1024]{1,0:T(8,128)(2,1)S(1)} %copy-done.4), channel_id=1, source_target_pairs={{0,1},{1,0},{2,3},{3,2},{4,5},{5,4},{6,7},{7,6},{8,9},{9,8},{10,11... | collective-permute-start | bytes 1572872 | tf_op jit(solution)/shard_map/ppermute | solution.py:327
  41.1 1.7 %all-to-all-done.1.parts = bf16[8,32,512]{2,1,0:T(8,128)(2,1)S(1)} async-done(((bf16[8,32,512]{2,1,0:T(8,128)(2,1)}), bf16[8,32,512]{2,1,0:T(8,128)(2,1)S(1)}, u32[]{:S(2)}, u32[]{:S(2)}) %all-to-all-start.1) | async-done | bytes 262176 | tf_op jit(solution)/shard_map/all_to_all | solution.py:315
  42.8 0.9 %shard_map.67.after = bf16[16,32,512]{2,1,0:T(8,128)(2,1)} custom-call(bf16[8,32,512]{2,1,0:T(8,128)(2,1)S(1)} %all-to-all-done.1.parts), custom_call_target="tpu_custom_call" | custom-call | bytes 3400000 | tf_op jit(solution)/shard_map/pallas_call | solution.py:343
  43.7 8.0 %all-to-all-start.2 = ((bf16[16,32,512]{2,1,0:T(8,128)(2,1)}), bf16[16,32,512]{2,1,0:T(8,128)(2,1)S(1)}, u32[]{:S(2)}, u32[]{:S(2)}) async-start(bf16[16,32,512]{2,1,0:T(8,128)(2,1)} %shard_map.67.after), calls=%async_computation.2 | async-start | bytes 1048576 | tf_op jit(solution)/shard_map/all_to_all | solution.py:315
  51.7 0.0 collective-permute-done.2.w_other
  51.7 0.0 collective-permute-done.5.from_left
  51.7 0.0 collective-permute-done.6.from_right
  51.7 6.3 %shard_map.70 = (bf16[1024,512]{1,0:T(8,128)(2,1)}, bf16[512,512]{1,0:T(8,128)(2,1)}, bf16[512,512]{1,0:T(8,128)(2,1)}) custom-call(bf16[256,1024]{1,0:T(8,128)(2,1)} %get-tuple-element.16.w_mine, bf16[256,1024]{1,0:T(8,128)(2,1)} %collective-permute-done.2.w_other, bf16[256,4,512]{2,1,0:T(4,128)(2,1)} %source.1, ...), custom_call_target="tpu_custom_call" | custom-call | bytes 17000000 | tf_op jit(solution)/shard_map/pallas_call | solution.py:356
  58.0 2.6 %collective-permute-start.7 = (bf16[512,512]{1,0:T(8,128)(2,1)}, bf16[512,512]{1,0:T(8,128)(2,1)S(1)}, u32[]{:S(2)}, u32[]{:S(2)}) collective-permute-start(bf16[512,512]{1,0:T(8,128)(2,1)} %get-tuple-element.23), channel_id=1, source_target_pairs={{0,1},{1,0},{2,3},{3,2},{4,5},{5,4},{6,7},{7,6},{8,9},{9,8},{10,11... | collective-permute-start | bytes 1572872 | tf_op jit(solution)/shard_map/ppermute | solution.py:375
  60.6 0.1 collective-permute-start.8
  60.7 0.0 all-to-all-done.2
  60.7 1.1 %collective-permute-start.1 = (bf16[512,512]{1,0:T(8,128)(2,1)S(1)}, bf16[512,512]{1,0:T(8,128)(2,1)S(1)}, u32[]{:S(2)}, u32[]{:S(2)}) collective-permute-start(bf16[512,512]{1,0:T(8,128)(2,1)S(1)} %bitcast.6), channel_id=1, source_target_pairs={{0,1},{1,0},{2,3},{3,2},{4,5},{5,4},{6,7},{7,6},{8,9},{9,8},{10,11... | collective-permute-start | bytes 1572872 | tf_op jit(solution)/shard_map/ppermute | solution.py:378
  61.9 0.0 copy-start.2
  61.9 1.2 %copy-done.2 = bf16[1024,512]{1,0:T(8,128)(2,1)S(1)} copy-done((bf16[1024,512]{1,0:T(8,128)(2,1)S(1)}, bf16[1024,512]{1,0:T(8,128)(2,1)}, u32[]{:S(2)}) %copy-start.2) | copy-done | bytes 1048600
  63.1 0.7 %shard_map.71.first = f32[1024,512]{1,0:T(8,128)S(1)} custom-call(s32[1]{0:T(128)} %bitcast.half.core, bf16[256,4,1024]{2,1,0:T(4,128)(2,1)S(1)} %copy-done, bf16[512,512]{1,0:T(8,128)(2,1)S(1)} %bitcast.7, bf16[1024,512]{1,0:T(8,128)(2,1)S(1)} %copy-done.2), custom_call_target="tpu_custom_call" | custom-call | bytes 3060000 | tf_op jit(solution)/shard_map/pallas_call | solution.py:379
  63.8 0.0 collective-permute-done.7.got_low
  63.8 0.0 collective-permute-done.8.got_high
  63.8 0.0 collective-permute-done.1.ct
  63.8 2.6 %shard_map.72 = bf16[256,4,512]{2,1,0:T(4,128)(2,1)} custom-call(s32[1]{0:T(128)S(6)} %sub.3.half, bf16[256,4,1024]{2,1,0:T(4,128)(2,1)S(1)} %copy-done, bf16[512,512]{1,0:T(8,128)(2,1)S(1)} %collective-permute-done.1.ct, f32[1024,512]{1,0:T(8,128)S(1)} %shard_map.71.first, bf16[512,512]{1,0:T(8,128)(2,1)S(1)} %collective-permute-done.7.got_low, ...), custom_call_target="tpu_custom_call" | custom-call | bytes 6800000 | tf_op jit(solution)/shard_map/pallas_call | solution.py:382
Async XLA Ops:
  0.0 9.8 %copy-start.3 = (s32[32,128]{1,0:T(8,128)S(1)}, s32[32,128]{1,0:T(8,128)}, u32[]{:S(2)}) copy-start(s32[32,128]{1,0:T(8,128)} %mask.1) | copy-start | bytes 49156
  0.0 9.8 %copy-start.1 = (bf16[256,4,512]{2,1,0:T(4,128)(2,1)S(1)}, bf16[256,4,512]{2,1,0:T(4,128)(2,1)}, u32[]{:S(2)}) copy-start(bf16[256,4,512]{2,1,0:T(4,128)(2,1)} %t.3) | copy-start | bytes 3145732
  0.0 9.8 %copy-start = (bf16[256,4,1024]{2,1,0:T(4,128)(2,1)S(1)}, bf16[256,4,1024]{2,1,0:T(4,128)(2,1)}, u32[]{:S(2)}) copy-start(bf16[256,4,1024]{2,1,0:T(4,128)(2,1)} %chol.7) | copy-start | bytes 6291460
  3.8 6.0 %collective-permute-start = (bf16[512,512]{1,0:T(8,128)(2,1)}, bf16[512,512]{1,0:T(8,128)(2,1)S(1)}, u32[]{:S(2)}, u32[]{:S(2)}) collective-permute-start(bf16[512,512]{1,0:T(8,128)(2,1)} %get-tuple-element.15), channel_id=1, source_target_pairs={{0,1},{1,0},{2,3},{3,2},{4,5},{5,4},{6,7},{7,6},{8,9},{9,8},{10,11... | collective-permute-start | bytes 1572872 | tf_op jit(solution)/shard_map/ppermute | solution.py:303
  7.1 16.9 %collective-permute-start.3 = (bf16[4,128,512]{2,1,0:T(8,128)(2,1)}, bf16[4,128,512]{2,1,0:T(8,128)(2,1)}, u32[]{:S(2)}, u32[]{:S(2)}) collective-permute-start(bf16[4,128,512]{2,1,0:T(8,128)(2,1)} %get-tuple-element.18.low), channel_id=1, source_target_pairs={{0,2},{2,4},{4,6},{6,0},{1,3},{3,5},{5,7},{7,1},{8,10},{10,12},{12... | collective-permute-start | bytes 1572872 | tf_op jit(solution)/shard_map/ppermute | solution.py:304
  7.1 16.9 %collective-permute-start.4 = (bf16[4,128,512]{2,1,0:T(8,128)(2,1)}, bf16[4,128,512]{2,1,0:T(8,128)(2,1)}, u32[]{:S(2)}, u32[]{:S(2)}) collective-permute-start(bf16[4,128,512]{2,1,0:T(8,128)(2,1)} %get-tuple-element.19.high), channel_id=1, source_target_pairs={{0,6},{2,0},{4,2},{6,4},{1,7},{3,1},{5,3},{7,5},{8,14},{10,8},{12,... | collective-permute-start | bytes 1572872 | tf_op jit(solution)/shard_map/ppermute | solution.py:305
  12.2 17.0 %all-to-all-start = ((bf16[16,32,512]{2,1,0:T(8,128)(2,1)}), bf16[16,32,512]{2,1,0:T(8,128)(2,1)S(1)}, u32[]{:S(2)}, u32[]{:S(2)}) async-start(bf16[16,32,512]{2,1,0:T(8,128)(2,1)} %bitcast.3), calls=%async_computation | async-start | bytes 1048576 | tf_op jit(solution)/shard_map/all_to_all | solution.py:315
  19.7 18.5 %copy-start.4 = (bf16[256,1024]{1,0:T(8,128)(2,1)S(1)}, bf16[256,1024]{1,0:T(8,128)(2,1)}, u32[]{:S(2)}) copy-start(bf16[256,1024]{1,0:T(8,128)(2,1)} %get-tuple-element.17.after) | copy-start | bytes 1572868
  26.4 25.3 %collective-permute-start.5 = (bf16[2,4,128,512]{3,2,1,0:T(8,128)(2,1)}, bf16[2,4,128,512]{3,2,1,0:T(8,128)(2,1)}, u32[]{:S(2)}, u32[]{:S(2)}) collective-permute-start(bf16[2,4,128,512]{3,2,1,0:T(8,128)(2,1)} %get-tuple-element.20), channel_id=1, source_target_pairs={{0,2},{2,4},{4,6},{6,0},{1,3},{3,5},{5,7},{7,1},{8,10},{10,12},{12... | collective-permute-start | bytes 3145736 | tf_op jit(solution)/shard_map/ppermute | solution.py:339
  26.5 25.2 %collective-permute-start.6 = (bf16[2,4,128,512]{3,2,1,0:T(8,128)(2,1)}, bf16[2,4,128,512]{3,2,1,0:T(8,128)(2,1)}, u32[]{:S(2)}, u32[]{:S(2)}) collective-permute-start(bf16[2,4,128,512]{3,2,1,0:T(8,128)(2,1)} %get-tuple-element.21), channel_id=1, source_target_pairs={{0,6},{2,0},{4,2},{6,4},{1,7},{3,1},{5,3},{7,5},{8,14},{10,8},{12,... | collective-permute-start | bytes 3145736 | tf_op jit(solution)/shard_map/ppermute | solution.py:340
  30.0 12.8 %all-to-all-start.1 = ((bf16[8,32,512]{2,1,0:T(8,128)(2,1)}), bf16[8,32,512]{2,1,0:T(8,128)(2,1)S(1)}, u32[]{:S(2)}, u32[]{:S(2)}) async-start(bf16[8,32,512]{2,1,0:T(8,128)(2,1)} %shard_map.66), calls=%async_computation.1 | async-start | bytes 524288 | tf_op jit(solution)/shard_map/all_to_all | solution.py:315
  38.1 13.5 %collective-permute-start.2 = (bf16[256,1024]{1,0:T(8,128)(2,1)S(1)}, bf16[256,1024]{1,0:T(8,128)(2,1)}, u32[]{:S(2)}, u32[]{:S(2)}) collective-permute-start(bf16[256,1024]{1,0:T(8,128)(2,1)S(1)} %copy-done.4), channel_id=1, source_target_pairs={{0,1},{1,0},{2,3},{3,2},{4,5},{5,4},{6,7},{7,6},{8,9},{9,8},{10,11... | collective-permute-start | bytes 1572872 | tf_op jit(solution)/shard_map/ppermute | solution.py:327
  43.7 17.1 %all-to-all-start.2 = ((bf16[16,32,512]{2,1,0:T(8,128)(2,1)}), bf16[16,32,512]{2,1,0:T(8,128)(2,1)S(1)}, u32[]{:S(2)}, u32[]{:S(2)}) async-start(bf16[16,32,512]{2,1,0:T(8,128)(2,1)} %shard_map.67.after), calls=%async_computation.2 | async-start | bytes 1048576 | tf_op jit(solution)/shard_map/all_to_all | solution.py:315
  58.0 5.8 %collective-permute-start.7 = (bf16[512,512]{1,0:T(8,128)(2,1)}, bf16[512,512]{1,0:T(8,128)(2,1)S(1)}, u32[]{:S(2)}, u32[]{:S(2)}) collective-permute-start(bf16[512,512]{1,0:T(8,128)(2,1)} %get-tuple-element.23), channel_id=1, source_target_pairs={{0,1},{1,0},{2,3},{3,2},{4,5},{5,4},{6,7},{7,6},{8,9},{9,8},{10,11... | collective-permute-start | bytes 1572872 | tf_op jit(solution)/shard_map/ppermute | solution.py:375
  60.6 3.2 %collective-permute-start.8 = (bf16[512,512]{1,0:T(8,128)(2,1)}, bf16[512,512]{1,0:T(8,128)(2,1)}, u32[]{:S(2)}, u32[]{:S(2)}) collective-permute-start(bf16[512,512]{1,0:T(8,128)(2,1)} %get-tuple-element.24), channel_id=1, source_target_pairs={{0,1},{1,0},{2,3},{3,2},{4,5},{5,4},{6,7},{7,6},{8,9},{9,8},{10,11... | collective-permute-start | bytes 1572872 | tf_op jit(solution)/shard_map/ppermute | solution.py:376
  60.7 3.1 %collective-permute-start.1 = (bf16[512,512]{1,0:T(8,128)(2,1)S(1)}, bf16[512,512]{1,0:T(8,128)(2,1)S(1)}, u32[]{:S(2)}, u32[]{:S(2)}) collective-permute-start(bf16[512,512]{1,0:T(8,128)(2,1)S(1)} %bitcast.6), channel_id=1, source_target_pairs={{0,1},{1,0},{2,3},{3,2},{4,5},{5,4},{6,7},{7,6},{8,9},{9,8},{10,11... | collective-permute-start | bytes 1572872 | tf_op jit(solution)/shard_map/ppermute | solution.py:378
  61.9 1.2 %copy-start.2 = (bf16[1024,512]{1,0:T(8,128)(2,1)S(1)}, bf16[1024,512]{1,0:T(8,128)(2,1)}, u32[]{:S(2)}) copy-start(bf16[1024,512]{1,0:T(8,128)(2,1)} %get-tuple-element.22.base) | copy-start | bytes 3145732
